TPU v7x, 32 devices: a whole 2x2x4 slice. The times are simulated.
32 devices in a mesh: lat: 4 (over y, x), lon: 8 (over z, core).
Axes of the slice: x: 2, y: 2, z: 4, core: 2. Of those that a mesh axis runs over, the one named last changes fastest.
Arguments:
- height: float32 [256, 8640], P('lat', 'lon'), may hold values from -6 to 6
- east_flow: float32 [256, 8640], P('lat', 'lon'), may hold values from -4 to 4
- north_flow: float32 [256, 8640], P('lat', 'lon'), may hold values from -4 to 4
- legendre: float32 [32, 256, 2048], P('lon', 'lat'), may hold values from -0.375 to 0.375
- love_numbers: float32 [2048], replicated, may hold values from 0.05 to 1
- wavenumbers: int32 [32], replicated, may hold values from 0 to 2047, as said below
- land_sea: int32 [256, 8640], P('lat', 'lon'), may hold values 0 or 1
Outputs:
- loading: float32 [256, 8640], P('lat', 'lon')
- surface: float32 [256, 8640], P('lat', 'lon')
- east_out: float32 [256, 8640], P('lat', 'lon')
- north_out: float32 [256, 8640], P('lat', 'lon')
Inputs may be any that keep to these rules, and one draw needn't show every extreme that they name: 32 distinct wavenumbers in no particular order; 0 and 2047 are always among them.
All inputs are finite; a program needn't handle non-finite values. No bound on the sum of `land_sea` on one device may be relied on, other than what follows from the above.
Results may differ from a plain program's by a relative error of at most 0.000078.
Values sent between devices are 32-bit elements; how exact they have to be, the bound alone decides.
No kernel may reach another device: no remote copies, remote signals or barrier semaphores. Data moves between devices by JAX's collectives and lax.ppermute only.
A program may use at most 64 MiB of HBM per device.

v0:
```python
import math

import jax
import jax.numpy as jnp
from jax import lax
from jax.sharding import PartitionSpec as P

SUBSTEPS = 4


east_step = 0.3
north_step = 0.3


def extended(block, sides, width, periodic):
    for axis, dim in sides:
        count = lax.axis_size(axis)
        forward = [(i, i + 1) for i in range(count - 1)]
        if periodic:
            forward.append((count - 1, 0))
        backward = [(target, source) for source, target in forward]
        low = lax.ppermute(
            lax.slice_in_dim(block, block.shape[dim] - width, None, axis=dim), axis, forward
        )
        high = lax.ppermute(lax.slice_in_dim(block, 0, width, axis=dim), axis, backward)
        block = jnp.concatenate([low, block, high], axis=dim)
    return block


def harmonic_rows(wavenumbers, first_column, column_count, period):
    columns = first_column + jnp.arange(column_count, dtype=jnp.int32)
    product = wavenumbers[:, None] * columns[None, :] % period
    angles = 2.0 * math.pi / period * product.astype(jnp.float32)
    stacked = jnp.stack([jnp.cos(angles), jnp.sin(angles)], axis=1)
    return stacked.reshape(2 * wavenumbers.shape[0], column_count)


def shards(height, east_flow, north_flow, legendre, love_numbers, wavenumbers, land_sea):
    highest = lax.Precision.HIGHEST
    band_rows, sector_cols = height.shape
    all_cols = sector_cols * lax.axis_size("lon")
    all_waves = wavenumbers.shape[0]
    own_waves = legendre.shape[0]
    sector_index = lax.axis_index("lon")
    harmonics = harmonic_rows(wavenumbers, sector_index * sector_cols, sector_cols, all_cols)
    forward_scale = 1.0 / math.sqrt(all_cols)
    partial_rows = forward_scale * lax.dot_general(
        harmonics, height, (((1,), (1,)), ((), ())), precision=highest
    )
    totals = lax.psum(partial_rows, "lon")
    owned = lax.dynamic_slice_in_dim(totals, sector_index * (2 * own_waves), 2 * own_waves, 0)
    owned = owned.reshape(own_waves, 2, band_rows)
    partial_value = jnp.einsum("mtl,mpt->mpl", legendre, owned, precision=highest)
    spectral = lax.psum(partial_value, "lat") * love_numbers[None, None, :]
    synthesized = jnp.einsum("mtl,mpl->mpt", legendre, spectral, precision=highest).reshape(
        2 * own_waves, band_rows
    )
    back_scale = 1.0 / math.sqrt(all_waves)
    loading = (
        lax.dot_general(
            lax.all_gather(synthesized, "lon", axis=0, tiled=True),
            harmonics,
            (((0,), (0,)), ((), ())),
            precision=highest,
        )
        * back_scale
    )
    wet_cells = land_sea.astype(jnp.float32)
    margin = 2 * SUBSTEPS
    stacked = jnp.stack([height, loading, east_flow, north_flow, wet_cells])
    taller = extended(stacked, (("lat", 1),), margin, False)
    window = extended(taller, (("lon", 2),), margin, True)
    surface = window[0]
    load_win = window[1]
    east_out = window[2]
    north_out = window[3]
    wet_win = window[4]
    for substep in range(SUBSTEPS):
        pressure = surface - load_win
        east_out = wet_win * (
            east_out - east_step * (jnp.roll(pressure, -1, 1) - jnp.roll(pressure, 1, 1))
        )
        north_out = wet_win * (
            north_out - north_step * (jnp.roll(pressure, -1, 0) - jnp.roll(pressure, 1, 0))
        )
        change = east_step * (jnp.roll(east_out, -1, 1) - jnp.roll(east_out, 1, 1)) + north_step * (
            jnp.roll(north_out, -1, 0) - jnp.roll(north_out, 1, 0)
        )
        surface = surface - wet_win * change
    surface = surface[margin : margin + band_rows, margin : margin + sector_cols]
    east_out = east_out[margin : margin + band_rows, margin : margin + sector_cols]
    north_out = north_out[margin : margin + band_rows, margin : margin + sector_cols]
    return (loading, surface, east_out, north_out)


def solution(mesh):
    return jax.shard_map(
        shards,
        mesh=mesh,
        in_specs=(
            P("lat", "lon"),
            P("lat", "lon"),
            P("lat", "lon"),
            P("lon", "lat", None),
            P(),
            P(),
            P("lat", "lon"),
        ),
        out_specs=(P("lat", "lon"), P("lat", "lon"), P("lat", "lon"), P("lat", "lon")),
        check_vma=False,
    )
```

profile of v0, /device:TPU:0, one launch (start us, length us, event | category | flops | bytes accessed | tf_op | source)
XLA Modules:
  0.0 142.4 jit_solution(13301912230089022923)
XLA Ops:
  7.3 1.5 %fusion.49 = (f32[32,1,1080]{2,0,1:T(8,128)S(1)}, f32[32,1,1080]{2,0,1:T(8,128)S(1)}) fusion(s32[1080]{0:T(1024)S(1)} %iota_add_fusion, s32[32]{0:T(128)} %param.12), kind=kLoop, calls=%fused_computation.85 | loop fusion | flops 311040 | bytes 280928 | tf_op jit(solution)/shard_map/cos | solution.py:34
  9.2 0.4 convolution_multiply_fusion.1
  9.7 30.3 %psum.14 = f32[64,64]{1,0:T(8,128)S(1)} all-reduce(f32[64,64]{1,0:T(8,128)S(1)} %convolution_multiply_fusion.1), channel_id=1, replica_groups=mesh['lat'=4,'lon'=8] {'lon'}, use_global_device_ids=true, to_apply=%region_0.1 | all-reduce | flops 4096 | bytes 32768 | tf_op jit(solution)/shard_map/psum | solution.py:50
  39.9 1.7 %fusion.91 = f32[4,2,2048]{2,1,0:T(2,128)} fusion(f32[4,2,64]{2,1,0:T(2,128)S(1)} %bitcast.76, f32[4,64,2048]{2,1,0:T(8,128)S(1)} %copy-done), kind=kOutput, calls=%fused_computation.126 | convolution fusion | flops 12582912 | bytes 2164736 | tf_op jit(solution)/shard_map/mtl,mpt->mpl/dot_general | solution.py:53
  41.7 0.7 bitcast_dynamic-update-slice_fusion.4
  42.4 39.1 %all-reduce.2.cloned.1.call-done = f32[4,2,2048]{2,1,0:T(2,128)} async-done(((f32[4,2,2048]{2,1,0:T(2,128)}), f32[4,2,2048]{2,1,0:T(2,128)}) %all-reduce.2.cloned.1.call-update) | async-done | bytes 65552 | tf_op jit(solution)/shard_map/psum | solution.py:54
  81.5 2.8 %fusion.51 = f32[4,2,64]{2,1,0:T(2,128)S(1)} fusion(f32[4,64,2048]{2,1,0:T(8,128)S(1)} %copy-done, f32[4,2,2048]{2,1,0:T(2,128)} %all-reduce.2.cloned.1.call-done, f32[2048]{0:T(1024)S(1)} %copy-done.7), kind=kOutput, calls=%fused_computation.87 | convolution fusion | flops 12599296 | bytes 2172928 | tf_op jit(solution)/shard_map/mtl,mpl->mpt/dot_general | solution.py:55
  84.3 14.1 %all_gather.3 = f32[64,64]{1,0:T(8,128)S(1)} all-gather(f32[8,64]{1,0:T(8,128)S(1)} %bitcast.75), channel_id=1, replica_groups=mesh['lat'=4,'lon'=8] {'lon'}, dimensions={0}, use_global_device_ids=true | all-gather | bytes 18432 | tf_op jit(solution)/shard_map/all_gather | solution.py:61
  98.4 1.2 bitcast_dynamic-update-slice_fusion.3
  99.7 3.4 %collective-permute-start = (f32[5,8,1080]{2,1,0:T(8,128)S(1)}, f32[5,8,1080]{2,1,0:T(8,128)S(1)}, u32[]{:S(2)}, u32[]{:S(2)}) collective-permute-start(f32[5,8,1080]{2,1,0:T(8,128)S(1)} %get-tuple-element.20), channel_id=1, source_target_pairs={{0,8},{8,16},{16,24},{1,9},{9,17},{17,25},{2,10},{10,18},{18,26},{... | collective-permute-start | bytes 518408 | tf_op jit(solution)/shard_map/ppermute | solution.py:22
  103.1 1.3 collective-permute-start.1
  104.4 3.0 %collective-permute-done = f32[5,8,1080]{2,1,0:T(8,128)S(1)} collective-permute-done((f32[5,8,1080]{2,1,0:T(8,128)S(1)}, f32[5,8,1080]{2,1,0:T(8,128)S(1)}, u32[]{:S(2)}, u32[]{:S(2)}) %collective-permute-start) | collective-permute-done | bytes 172832 | tf_op jit(solution)/shard_map/ppermute | solution.py:22
  107.4 5.8 %collective-permute-done.1 = f32[5,8,1080]{2,1,0:T(8,128)S(1)} collective-permute-done((f32[5,8,1080]{2,1,0:T(8,128)S(1)}, f32[5,8,1080]{2,1,0:T(8,128)S(1)}, u32[]{:S(2)}, u32[]{:S(2)}) %collective-permute-start.1) | collective-permute-done | bytes 172832 | tf_op jit(solution)/shard_map/ppermute | solution.py:25
  113.2 1.4 pad_maximum_fusion
  114.6 1.1 fusion.57
  115.9 3.5 %collective-permute-start.3 = (f32[5,80,8]{2,1,0:T(8,128)S(1)}, f32[5,80,8]{2,1,0:T(8,128)S(1)}, u32[]{:S(2)}, u32[]{:S(2)}) collective-permute-start(f32[5,80,8]{2,1,0:T(8,128)S(1)} %get-tuple-element.18), channel_id=1, source_target_pairs={{1,0},{2,1},{3,2},{4,3},{5,4},{6,5},{7,6},{0,7},{9,8},{10,9},{11,1... | collective-permute-start | bytes 38408 | tf_op jit(solution)/shard_map/ppermute | solution.py:25
  119.4 3.9 %collective-permute-done.2 = f32[5,80,8]{2,1,0:T(8,128)S(1)} collective-permute-done((f32[5,80,8]{2,1,0:T(8,128)S(1)}, f32[5,80,8]{2,1,0:T(8,128)S(1)}, u32[]{:S(2)}, u32[]{:S(2)}) %collective-permute-start.2) | collective-permute-done | bytes 12832 | tf_op jit(solution)/shard_map/ppermute | solution.py:22
  123.3 2.8 %concatenate.107 = f32[5,80,1096]{2,1,0:T(8,128)} concatenate(f32[5,80,8]{2,1,0:T(8,128)S(1)} %collective-permute-done.2, f32[5,80,1080]{2,1,0:T(8,128)} %pad_maximum_fusion, f32[5,80,8]{2,1,0:T(8,128)S(1)} %collective-permute-done.3), dimensions={2} | concatenate | bytes 3507200 | tf_op jit(solution)/shard_map/concatenate | solution.py:26
  126.1 1.1 fusion.36
  127.6 1.2 copy-done.1
  130.4 0.2 fusion.38
  132.6 0.9 slice.387
  133.5 0.9 slice.388
  134.3 1.3 slice_subtract_fusion
  (67 shorter events, 4.4 us)
Async XLA Ops:
  7.2 32.8 %copy-start = (f32[4,64,2048]{2,1,0:T(8,128)S(1)}, f32[4,64,2048]{2,1,0:T(8,128)}, u32[]{:S(2)}) copy-start(f32[4,64,2048]{2,1,0:T(8,128)} %param.10) | copy-start | bytes 6291460
  7.2 2.0 %copy-start.3 = (f32[64,1080]{1,0:T(8,128)S(1)}, f32[64,1080]{1,0:T(8,128)}, u32[]{:S(2)}) copy-start(f32[64,1080]{1,0:T(8,128)} %param.7) | copy-start | bytes 829444
  7.2 74.3 %all-reduce.2.cloned.1.call-start = ((), (), s32[]{:S(2)}) async-start(), calls=%async_computation | async-start | bytes 131072 | tf_op jit(solution)/shard_map/psum | solution.py:54
  9.2 72.3 %copy-start.7 = (f32[2048]{0:T(1024)S(1)}, f32[2048]{0:T(1024)}, u32[]{:S(2)}) copy-start(f32[2048]{0:T(1024)} %param.11) | copy-start | bytes 24580
  41.7 57.8 %copy-start.4 = (f32[64,1080]{1,0:T(8,128)S(1)}, f32[64,1080]{1,0:T(8,128)}, u32[]{:S(2)}) copy-start(f32[64,1080]{1,0:T(8,128)} %param.8) | copy-start | bytes 829444
  42.4 57.1 %copy-start.5 = (f32[64,1080]{1,0:T(8,128)S(1)}, f32[64,1080]{1,0:T(8,128)}, u32[]{:S(2)}) copy-start(f32[64,1080]{1,0:T(8,128)} %param.9) | copy-start | bytes 829444
  42.4 57.1 %copy-start.6 = (s32[64,1080]{1,0:T(8,128)S(1)}, s32[64,1080]{1,0:T(8,128)}, u32[]{:S(2)}) copy-start(s32[64,1080]{1,0:T(8,128)} %param.13) | copy-start | bytes 829444
  81.5 16.8 %copy-start.2 = (f32[5,64,1080]{2,1,0:T(8,128)S(1)}, f32[5,64,1080]{2,1,0:T(8,128)}, u32[]{:S(2)}) copy-start(f32[5,64,1080]{2,1,0:T(8,128)} %bitcast_dynamic-update-slice_fusion.4) | copy-start | bytes 4147204
  99.7 7.7 %collective-permute-start = (f32[5,8,1080]{2,1,0:T(8,128)S(1)}, f32[5,8,1080]{2,1,0:T(8,128)S(1)}, u32[]{:S(2)}, u32[]{:S(2)}) collective-permute-start(f32[5,8,1080]{2,1,0:T(8,128)S(1)} %get-tuple-element.20), channel_id=1, source_target_pairs={{0,8},{8,16},{16,24},{1,9},{9,17},{17,25},{2,10},{10,18},{18,26},{... | collective-permute-start | bytes 518408 | tf_op jit(solution)/shard_map/ppermute | solution.py:22
  103.1 10.2 %collective-permute-start.1 = (f32[5,8,1080]{2,1,0:T(8,128)S(1)}, f32[5,8,1080]{2,1,0:T(8,128)S(1)}, u32[]{:S(2)}, u32[]{:S(2)}) collective-permute-start(f32[5,8,1080]{2,1,0:T(8,128)S(1)} %get-tuple-element.21), channel_id=1, source_target_pairs={{8,0},{16,8},{24,16},{9,1},{17,9},{25,17},{10,2},{18,10},{26,18},{... | collective-permute-start | bytes 518408 | tf_op jit(solution)/shard_map/ppermute | solution.py:25
  115.8 7.5 %collective-permute-start.2 = (f32[5,80,8]{2,1,0:T(8,128)S(1)}, f32[5,80,8]{2,1,0:T(8,128)S(1)}, u32[]{:S(2)}, u32[]{:S(2)}) collective-permute-start(f32[5,80,8]{2,1,0:T(8,128)S(1)} %get-tuple-element.19), channel_id=1, source_target_pairs={{0,1},{1,2},{2,3},{3,4},{4,5},{5,6},{6,7},{7,0},{8,9},{9,10},{10,1... | collective-permute-start | bytes 38408 | tf_op jit(solution)/shard_map/ppermute | solution.py:22
  115.9 7.4 %collective-permute-start.3 = (f32[5,80,8]{2,1,0:T(8,128)S(1)}, f32[5,80,8]{2,1,0:T(8,128)S(1)}, u32[]{:S(2)}, u32[]{:S(2)}) collective-permute-start(f32[5,80,8]{2,1,0:T(8,128)S(1)} %get-tuple-element.18), channel_id=1, source_target_pairs={{1,0},{2,1},{3,2},{4,3},{5,4},{6,5},{7,6},{0,7},{9,8},{10,9},{11,1... | collective-permute-start | bytes 38408 | tf_op jit(solution)/shard_map/ppermute | solution.py:25
  127.3 1.5 %copy-start.1 = (f32[5,80,1096]{2,1,0:T(8,128)S(1)}, f32[5,80,1096]{2,1,0:T(8,128)}, u32[]{:S(2)}) copy-start(f32[5,80,1096]{2,1,0:T(8,128)} %concatenate.107) | copy-start | bytes 5260804
Sparse Core Ops, SparseCore 0:
  41.8 39.6 all-reduce.1
where the time goes:
time: 144 us; the launch traced here: 142 us
  waiting for transfers between devices  51.9 us (36%)
  blocking collectives  44.3 us (31%)
  between operations  14.4 us (10%)
  local copies, waits for them, and re-layouts  10.6 us (7%)
  starting transfers between devices  8.31 us (6%)
  other arithmetic  6.93 us (5%)
  matrix products  6.08 us (4%)
    psum x1, waiting for transfers between devices, shards(): spectral = lax.psum(partial_value, 'lat') * love_numbers[None, None, :]  39.1 us
    psum x1, blocking collectives, shards(): totals = lax.psum(partial_rows, 'lon')  30.3 us
    all_gather x1, blocking collectives, shards(): lax.all_gather(synthesized, 'lon', axis=0, tiled=True)  14.1 us
    ppermute x2, waiting for transfers between devices, extended(): lax.ppermute(lax.slice_in_dim(block, block.shape[dim] - width, None, axis...  6.93 us
    ppermute x2, waiting for transfers between devices, extended(): lax.ppermute(lax.slice_in_dim(block, 0, width, axis=dim), axis, backward)  5.82 us
    ppermute x2, starting transfers between devices, extended(): lax.ppermute(lax.slice_in_dim(block, 0, width, axis=dim), axis, backward)  4.82 us
    ppermute x2, starting transfers between devices, extended(): lax.ppermute(lax.slice_in_dim(block, block.shape[dim] - width, None, axis...  3.44 us
  transfers between devices with their start and end apart: 5, of which 4 were waited for; matrix products, arithmetic and copies ran while one was open for 1% of the time, Pallas kernels for 0%

commit v1 on v0

v1 whole, which is shorter than its diff:
```python
import functools
import math

import jax
import jax.numpy as jnp
from jax import lax
from jax.experimental import pallas as pl
from jax.experimental.pallas import tpu as pltpu
from jax.sharding import PartitionSpec as P

SUBSTEPS = 4
MARGIN = 2 * SUBSTEPS
STEP = 0.3

f32 = jnp.float32
bf16 = jnp.bfloat16
VMEM = pl.BlockSpec(memory_space=pltpu.VMEM)
SMEM = pl.BlockSpec(memory_space=pltpu.SMEM)


def split2(x):
    hi = x.astype(bf16)
    lo = (x - hi.astype(f32)).astype(bf16)
    return hi, lo


def dft_kernel(period, own_waves, first_ref, waves_ref, height_ref, part_ref, harm_ref, field_ref):
    rows, cols = height_ref.shape
    waves, width = harm_ref.shape[0] // 2, harm_ref.shape[1]
    wave = waves_ref[...]
    start = wave * first_ref[0]
    turns = jnp.floor(start.astype(f32) * (1.0 / period)).astype(jnp.int32)
    start = (start - turns * period).astype(f32)
    wave = wave.astype(f32)
    row = lax.broadcasted_iota(jnp.int32, (waves, 1), 0)
    sine = (lax.rem(row, 2 * own_waves) >= own_waves).astype(f32)
    offset = 4.0 * start - period * sine
    for tile in range(0, width, 128):
        lane = lax.broadcasted_iota(jnp.int32, (1, 128), 1) + tile
        lane = jnp.where(lane < cols + MARGIN, lane, lane - width).astype(f32)
        product = wave * lane
        product = product - period * jnp.floor(product * (1.0 / period))
        quarter = 4.0 * product + offset
        turn = jnp.floor(quarter * (1.0 / period) + 0.5)
        angle = (quarter - period * turn) * (0.5 * math.pi / period)
        square = angle * angle
        cosine = 1.0 + square * (
            -1.0 / 2 + square * (1.0 / 24 + square * (-1.0 / 720 + square * (1.0 / 40320)))
        )
        sine_of = angle * (
            1.0
            + square
            * (-1.0 / 6 + square * (1.0 / 120 + square * (-1.0 / 5040 + square * (1.0 / 362880))))
        )
        phase = turn - 4.0 * jnp.floor(turn * 0.25)
        odd = (phase == 1.0) | (phase == 3.0)
        value = jnp.where(odd, sine_of, cosine)
        value = jnp.where((phase == 1.0) | (phase == 2.0), -value, value)
        hi, lo = split2(value)
        harm_ref[:waves, tile : tile + 128] = hi
        harm_ref[waves:, tile : tile + 128] = lo
        stop = min(cols, tile + 128)
        if stop <= tile:
            block = jnp.zeros((rows, 128), f32)
        elif stop == tile + 128:
            block = height_ref[:, tile : tile + 128]
        else:
            block = jnp.concatenate(
                [height_ref[:, tile:stop], jnp.zeros((rows, tile + 128 - stop), f32)], axis=1
            )
        hi, lo = split2(block)
        field_ref[:rows, tile : tile + 128] = hi
        field_ref[rows:, tile : tile + 128] = lo
    both = lax.dot_general(
        harm_ref[...], field_ref[...], (((1,), (1,)), ((), ())), preferred_element_type=f32
    )
    total = both[:waves] + both[waves:]
    total = (total[:, :rows] + total[:, rows:]) * (1.0 / math.sqrt(period))
    part_ref[...] = total.reshape(part_ref.shape)


def analysis_kernel(part_ref, legendre_ref, spectral_ref):
    slots, rows, degrees = legendre_ref.shape
    fourier = jnp.sum(part_ref[...], axis=0)
    columns = fourier.T
    for slot in range(slots):
        even = [
            jnp.broadcast_to(columns[o : o + 8, slot : slot + 1], (8, 128))
            for o in range(0, rows, 8)
        ]
        odd = [
            jnp.broadcast_to(columns[o : o + 8, slots + slot : slots + slot + 1], (8, 128))
            for o in range(0, rows, 8)
        ]
        for tile in range(0, degrees, 128):
            first = jnp.zeros((8, 128), f32)
            second = jnp.zeros((8, 128), f32)
            for at, o in enumerate(range(0, rows, 8)):
                block = legendre_ref[slot, o : o + 8, tile : tile + 128]
                first = first + block * even[at]
                second = second + block * odd[at]
            spectral_ref[slot : slot + 1, tile : tile + 128] = jnp.sum(
                first, axis=0, keepdims=True
            )
            spectral_ref[slots + slot : slots + slot + 1, tile : tile + 128] = jnp.sum(
                second, axis=0, keepdims=True
            )


def synthesis_kernel(
    parts_refs, love_ref, legendre_ref, low_ref, high_ref, out_ref, spectral_ref
):
    slots, rows, degrees = legendre_ref.shape
    total = parts_refs[0][...]
    for ref in parts_refs[1:]:
        total = total + ref[...]
    spectral_ref[...] = total * love_ref[...]
    taller = rows + 2 * MARGIN
    lanes = lax.broadcasted_iota(jnp.int32, (8, 128), 1)
    octets = [(low_ref, 0)] + [(legendre_ref, o) for o in range(0, rows, 8)] + [(high_ref, 0)]
    sums = [jnp.zeros((8, 128), f32) for _ in octets]
    for slot in range(slots):
        first = [jnp.zeros((8, 128), f32) for _ in octets]
        second = [jnp.zeros((8, 128), f32) for _ in octets]
        for tile in range(0, degrees, 128):
            even = jnp.broadcast_to(spectral_ref[slot : slot + 1, tile : tile + 128], (8, 128))
            odd = jnp.broadcast_to(
                spectral_ref[slots + slot : slots + slot + 1, tile : tile + 128], (8, 128)
            )
            for at, (ref, o) in enumerate(octets):
                block = ref[slot, o : o + 8, tile : tile + 128]
                first[at] = first[at] + block * even
                second[at] = second[at] + block * odd
        for at in range(len(octets)):
            sums[at] = jnp.where(lanes == slot, jnp.sum(first[at], axis=1, keepdims=True), sums[at])
            sums[at] = jnp.where(
                lanes == slots + slot, jnp.sum(second[at], axis=1, keepdims=True), sums[at]
            )
    column = jnp.concatenate(sums + [jnp.zeros((128 - taller, 128), f32)], axis=0)
    out_ref[...] = column.T[: 2 * slots]


def substep_kernel(
    synth_ref,
    harm_ref,
    height_ref,
    east_ref,
    north_ref,
    land_ref,
    low_ref,
    high_ref,
    left_ref,
    right_ref,
    loading_out,
    surface_out,
    east_out,
    north_out,
    load,
    pressure,
    surface,
    east,
    north,
    wet,
):
    rows, cols = height_ref.shape
    taller = rows + 2 * MARGIN
    width = harm_ref.shape[1]
    waves = harm_ref.shape[0] // 2
    synth = synth_ref[...].reshape(waves, 128).T * (1.0 / math.sqrt(waves // 2))
    hi, lo = split2(synth[:taller])
    left = jnp.concatenate(
        [jnp.concatenate([hi, hi], axis=1), jnp.concatenate([lo, lo], axis=1)], axis=0
    )
    both = lax.dot_general(
        left, harm_ref[...], (((1,), (0,)), ((), ())), preferred_element_type=f32
    )
    load[...] = both[:taller] + both[taller:]
    last = (cols // 128) * 128
    own = cols - last
    lanes = lax.broadcasted_iota(jnp.int32, (taller, width - last), 1)
    for at, (target, top, source) in enumerate(
        (
            (surface, 0, height_ref),
            (east, 0, east_ref),
            (north, 8, north_ref),
            (wet, 0, land_ref),
        )
    ):
        lows, middle, highs = (
            pl.ds(top, MARGIN),
            pl.ds(top + MARGIN, rows),
            pl.ds(top + MARGIN + rows, MARGIN),
        )
        target[lows, :last] = low_ref[at, :, :last]
        target[middle, :last] = source[:, :last].astype(f32)
        target[highs, :last] = high_ref[at, :, :last]
        tail = jnp.concatenate(
            [low_ref[at, :, last:cols], source[:, last:].astype(f32), high_ref[at, :, last:cols]],
            axis=0,
        )
        tail = jnp.concatenate([tail, jnp.zeros((taller, width - cols), f32)], axis=1)
        after = pltpu.roll(right_ref[...], (own - 2 * MARGIN * at) % 128, 1)
        before = pltpu.roll(left_ref[...], (-MARGIN - 2 * MARGIN * at - MARGIN) % 128, 1)
        after = jnp.concatenate([after] * ((width - last) // 128), axis=1)
        before = jnp.concatenate([before] * ((width - last) // 128), axis=1)
        tail = jnp.where((lanes >= own) & (lanes < own + MARGIN), after, tail)
        tail = jnp.where(lanes >= width - last - MARGIN, before, tail)
        target[pl.ds(top, taller), last:] = tail
    edge = jnp.zeros((8, width), f32)
    pressure[:8] = edge
    pressure[taller + 8 :] = edge
    north[:8] = edge
    north[taller + 8 :] = edge
    for substep in range(SUBSTEPS):
        for o in range(0, taller, 8):
            pressure[8 + o : 16 + o] = surface[o : o + 8] - load[o : o + 8]
        for o in range(0, taller, 8):
            here = pressure[8 + o : 16 + o]
            damp = wet[o : o + 8]
            east[o : o + 8] = damp * (
                east[o : o + 8]
                - STEP * (pltpu.roll(here, width - 1, 1) - pltpu.roll(here, 1, 1))
            )
            north[8 + o : 16 + o] = damp * (
                north[8 + o : 16 + o] - STEP * (pressure[9 + o : 17 + o] - pressure[7 + o : 15 + o])
            )
        for o in range(0, taller, 8):
            flow = east[o : o + 8]
            change = STEP * (pltpu.roll(flow, width - 1, 1) - pltpu.roll(flow, 1, 1)) + STEP * (
                north[9 + o : 17 + o] - north[7 + o : 15 + o]
            )
            surface[o : o + 8] = surface[o : o + 8] - wet[o : o + 8] * change
    loading_out[...] = load[MARGIN : MARGIN + rows, :cols]
    surface_out[...] = surface[MARGIN : MARGIN + rows, :cols]
    east_out[...] = east[MARGIN : MARGIN + rows, :cols]
    north_out[...] = north[8 + MARGIN : 8 + MARGIN + rows, :cols]


def edges_kernel(
    legendre_ref, height_ref, east_ref, north_ref, land_ref, up_ref, down_ref, semaphore
):
    slots, rows, degrees = legendre_ref.shape
    cols = height_ref.shape[1]
    copies = [
        pltpu.make_async_copy(
            legendre_ref.at[:, pl.ds(first, MARGIN), :],
            ref.at[pl.ds(0, slots), :, pl.ds(0, degrees)],
            semaphore.at[at],
        )
        for at, (ref, first) in enumerate(((up_ref, rows - MARGIN), (down_ref, 0)))
    ]
    for copy in copies:
        copy.start()
    for at, source in enumerate((height_ref, east_ref, north_ref, land_ref)):
        up_ref[at, :, degrees : degrees + cols] = source[rows - MARGIN :].astype(f32)
        down_ref[at, :, degrees : degrees + cols] = source[:MARGIN].astype(f32)
    for copy in copies:
        copy.wait()


def sides_kernel(
    height_ref, east_ref, north_ref, land_ref, low_ref, high_ref, tile_ref
):
    rows, cols = height_ref.shape
    taller = rows + 2 * MARGIN
    pieces = []
    for at, source in enumerate((height_ref, east_ref, north_ref, land_ref)):
        for first in (0, cols - MARGIN):
            window = slice(first, first + MARGIN)
            pieces.append(
                jnp.concatenate(
                    [low_ref[at, :, window], source[:, window].astype(f32), high_ref[at, :, window]],
                    axis=0,
                )
            )
    pieces.append(jnp.zeros((taller, 128 - 8 * MARGIN), f32))
    tile_ref[...] = jnp.concatenate(pieces, axis=1)


def struct(shape, dtype=f32):
    return jax.ShapeDtypeStruct(shape, dtype)


def lat_sum_parts(value):
    count = lax.axis_size("lat")
    if count & (count - 1) or count > 4:
        return [lax.psum(value, "lat")]
    return [value] + [
        lax.ppermute(value, "lat", [(i, i ^ step) for i in range(count)])
        for step in range(1, count)
    ]


def shards(height, east_flow, north_flow, legendre, love_numbers, wavenumbers, land_sea):
    rows, cols = height.shape
    slots, _, degrees = legendre.shape
    sectors, bands = lax.axis_size("lon"), lax.axis_size("lat")
    waves = wavenumbers.shape[0]
    period = cols * sectors
    width = -(-(cols + 2 * MARGIN) // 128) * 128
    taller = rows + 2 * MARGIN
    upward = [(i, i + 1) for i in range(bands - 1)]
    downward = [(target, source) for source, target in upward]
    eastward = [(i, (i + 1) % sectors) for i in range(sectors)]
    westward = [(target, source) for source, target in eastward]

    up, down = pl.pallas_call(
        edges_kernel,
        out_shape=[struct((max(4, slots), MARGIN, degrees + width))] * 2,
        in_specs=[pl.BlockSpec(memory_space=pl.ANY)] + [VMEM] * 4,
        out_specs=[VMEM] * 2,
        scratch_shapes=[pltpu.SemaphoreType.DMA((2,))],
        name="edges",
    )(legendre, height, east_flow, north_flow, land_sea)
    low = lax.ppermute(up, "lat", upward)
    high = lax.ppermute(down, "lat", downward)

    first = (lax.axis_index("lon") * cols).astype(jnp.int32).reshape(1)
    column = jnp.broadcast_to(wavenumbers.reshape(sectors, 1, slots), (sectors, 2, slots))
    part, harmonics = pl.pallas_call(
        functools.partial(dft_kernel, period, slots),
        out_shape=[struct((sectors, 2 * slots, rows)), struct((4 * waves, width), bf16)],
        in_specs=[SMEM, VMEM, VMEM],
        out_specs=[VMEM, VMEM],
        scratch_shapes=[pltpu.VMEM((2 * rows, width), bf16)],
        name="dft",
    )(first, column.reshape(2 * waves, 1), height)
    parts = lax.all_to_all(part, "lon", 0, 0, tiled=True)

    spectral = pl.pallas_call(
        analysis_kernel,
        out_shape=struct((2 * slots, degrees)),
        in_specs=[VMEM, VMEM],
        out_specs=VMEM,
        name="analysis",
    )(parts, legendre)
    pieces = lat_sum_parts(spectral)

    def synthesis(*refs):
        synthesis_kernel(refs[: len(pieces)], *refs[len(pieces) :])

    low_rows, high_rows = low[:, :, degrees : degrees + cols], high[:, :, degrees : degrees + cols]
    synth = pl.pallas_call(
        synthesis,
        out_shape=struct((2 * slots, 128)),
        in_specs=[VMEM] * (len(pieces) + 4),
        out_specs=VMEM,
        scratch_shapes=[pltpu.VMEM((2 * slots, degrees), f32)],
        name="synthesis",
    )(*pieces, love_numbers.reshape(1, degrees), legendre, low, high)
    everyone = lax.all_to_all(
        jnp.broadcast_to(synth[None], (sectors, 2 * slots, 128)), "lon", 0, 0, tiled=True
    )

    sides = pl.pallas_call(
        sides_kernel,
        out_shape=struct((taller, 128)),
        in_specs=[VMEM] * 6,
        out_specs=VMEM,
        name="sides",
    )(height, east_flow, north_flow, land_sea, low_rows, high_rows)
    left = lax.ppermute(sides, "lon", eastward)
    right = lax.ppermute(sides, "lon", westward)

    return pl.pallas_call(
        substep_kernel,
        out_shape=[struct((rows, cols))] * 4,
        in_specs=[VMEM] * 10,
        out_specs=[VMEM] * 4,
        scratch_shapes=[
            pltpu.VMEM((taller, width), f32),
            pltpu.VMEM((taller + 16, width), f32),
            pltpu.VMEM((taller, width), f32),
            pltpu.VMEM((taller, width), f32),
            pltpu.VMEM((taller + 16, width), f32),
            pltpu.VMEM((taller, width), f32),
        ],
        name="substeps",
    )(
        everyone,
        harmonics,
        height,
        east_flow,
        north_flow,
        land_sea,
        low_rows,
        high_rows,
        left,
        right,
    )


def solution(mesh):
    return jax.shard_map(
        shards,
        mesh=mesh,
        in_specs=(
            P("lat", "lon"),
            P("lat", "lon"),
            P("lat", "lon"),
            P("lon", "lat", None),
            P(),
            P(),
            P("lat", "lon"),
        ),
        out_specs=(P("lat", "lon"), P("lat", "lon"), P("lat", "lon"), P("lat", "lon")),
        check_vma=False,
    )
```

time: 144 us -> 63.7 us (0.44)
  waiting for transfers between devices: 51.9 us -> 6.51 us
  blocking collectives: 44.3 us -> 10.3 us
  Pallas kernels: 0 us -> 18 us
  between operations: 14.4 us -> 0.74 us
  starting transfers between devices: 8.31 us -> 18.1 us
  other arithmetic: 6.93 us -> 0.68 us
  matrix products: 6.08 us -> 0 us
  local copies, waits for them, and re-layouts: 10.6 us -> 8.79 us
    psum x1 -> x0, waiting for transfers between devices: 39.1 us -> none  [shards(): spectral = lax.psum(partial_value, 'lat') * love_numbers[None, None, :]]
    psum x1 -> x0, blocking collectives: 30.3 us -> none  [shards(): totals = lax.psum(partial_rows, 'lon')]
    pallas_call x0 -> x6, Pallas kernels: none -> 18 us  [the longest x1 4.61 us: shards(): pl.pallas_call(substep_kernel, out_shape=[struct((rows, cols))] * 4, in_s...]
    all_gather x1 -> x0, blocking collectives: 14.1 us -> none  [shards(): lax.all_gather(synthesized, 'lon', axis=0, tiled=True)]
    all_to_all x0 -> x1, blocking collectives: none -> 10.3 us  [shards(): parts = lax.all_to_all(part, 'lon', 0, 0, tiled=True)]
    ppermute x4 -> x7, starting transfers between devices: 8.27 us -> 14.7 us  [the longest x3 5.01 us: lat_sum_parts(): lax.ppermute(value, 'lat', [(i, i ^ step) for i in range(count)])]
    ppermute x4 -> x7, waiting for transfers between devices: 12.7 us -> 6.51 us  [the longest x3 4.52 us: lat_sum_parts(): lax.ppermute(value, 'lat', [(i, i ^ step) for i in range(count)])]
    dot_general x4 -> x0, matrix products: 6.08 us -> none  [the longest x1 2.77 us: shards(): jnp.einsum('mtl,mpl->mpt', legendre, spectral, precision=highest)]
  transfers between devices with their start and end apart: 5 -> 8, of which waited for: 4 -> 5; matrix products, arithmetic and copies ran while one was open for 1% -> 11% of each run, Pallas kernels for 0% -> 12%
where the time goes in v1:
time: 63.7 us; the launch traced here: 63.2 us
  starting transfers between devices  18.1 us (28%)
  Pallas kernels  18 us (28%)
  blocking collectives  10.3 us (16%)
  local copies, waits for them, and re-layouts  8.79 us (14%)
  waiting for transfers between devices  6.51 us (10%)
  between operations  0.74 us (1%)
  other arithmetic  0.68 us (1%)
    all_to_all x1, blocking collectives, shards(): parts = lax.all_to_all(part, 'lon', 0, 0, tiled=True)  10.3 us
    ppermute x3, starting transfers between devices, lat_sum_parts(): lax.ppermute(value, 'lat', [(i, i ^ step) for i in range(count)])  5.01 us
    ppermute x1, starting transfers between devices, shards(): low = lax.ppermute(up, 'lat', upward)  4.87 us
    pallas_call x1, Pallas kernels, shards(): pl.pallas_call(substep_kernel, out_shape=[struct((rows, cols))] * 4, in_s...  4.61 us
    ppermute x3, waiting for transfers between devices, lat_sum_parts(): lax.ppermute(value, 'lat', [(i, i ^ step) for i in range(count)])  4.52 us
    all_to_all x1, starting transfers between devices, shards(): lax.all_to_all(jnp.broadcast_to(synth[None], (sectors, 2 * slots, 128)),...  3.34 us
    pallas_call x1, Pallas kernels, shards(): pl.pallas_call(edges_kernel, out_shape=[struct((max(4, slots), MARGIN, de...  3.18 us
    ppermute x1, starting transfers between devices, shards(): right = lax.ppermute(sides, 'lon', westward)  3.14 us
  transfers between devices with their start and end apart: 8, of which 5 were waited for; matrix products, arithmetic and copies ran while one was open for 11% of the time, Pallas kernels for 12%

profile of v1, /device:TPU:0, one launch (start us, length us, event | category | flops | bytes accessed | tf_op | source)
XLA Modules:
  0.0 63.2 jit_solution(15995513435465868394)
XLA Ops:
  0.6 3.2 %edges.1 = (f32[4,8,3200]{2,1,0:T(8,128)}, f32[4,8,3200]{2,1,0:T(8,128)}) custom-call(f32[4,64,2048]{2,1,0:T(8,128)} %refs_5_.1, f32[64,1080]{1,0:T(8,128)} %height_ref.7, f32[64,1080]{1,0:T(8,128)} %east_ref.5, f32[64,1080]{1,0:T(8,128)} %north_ref.5, s32[64,1080]{1,0:T(8,128)} %land_ref.5), custom_call_target="tpu_custom_call" | custom-call | tf_op jit(solution)/shard_map/edges/pallas_call | solution.py:307
  3.8 4.9 %collective-permute-start.3 = (f32[4,8,3200]{2,1,0:T(8,128)}, f32[4,8,3200]{2,1,0:T(8,128)S(1)}, u32[]{:S(2)}, u32[]{:S(2)}) collective-permute-start(f32[4,8,3200]{2,1,0:T(8,128)} %get-tuple-element.9), channel_id=1, source_target_pairs={{0,8},{8,16},{16,24},{1,9},{9,17},{17,25},{2,10},{10,18},{18,26},{... | collective-permute-start | bytes 1228808 | tf_op jit(solution)/shard_map/ppermute | solution.py:315
  8.7 1.3 %collective-permute-start.4 = (f32[4,8,3200]{2,1,0:T(8,128)}, f32[4,8,3200]{2,1,0:T(8,128)S(1)}, u32[]{:S(2)}, u32[]{:S(2)}) collective-permute-start(f32[4,8,3200]{2,1,0:T(8,128)} %get-tuple-element.10), channel_id=1, source_target_pairs={{8,0},{16,8},{24,16},{9,1},{17,9},{25,17},{10,2},{18,10},{26,18},{... | collective-permute-start | bytes 1228808 | tf_op jit(solution)/shard_map/ppermute | solution.py:316
  10.1 0.7 %reshape.23.waves_ref = s32[64,1]{1,0:T(8,128)} reshape(s32[8,2,4]{2,1,0:T(2,128)S(1)} %broadcast_in_dim.14) | data formatting | bytes 512 | tf_op jit(solution)/shard_map/reshape | solution.py:327
  10.8 2.4 %dft.1 = (f32[8,8,64]{2,1,0:T(8,128)}, bf16[128,1152]{1,0:T(8,128)(2,1)}) custom-call(s32[1]{0:T(128)} %bitcast.first_ref, s32[64,1]{1,0:T(8,128)} %reshape.23.waves_ref, f32[64,1080]{1,0:T(8,128)} %height_ref.7), custom_call_target="tpu_custom_call" | custom-call | tf_op jit(solution)/shard_map/dft/pallas_call | solution.py:320
  13.2 0.8 %reshape.24 = f32[8,1,512]{2,1,0:T(1,128)S(1)} reshape(f32[8,8,64]{2,1,0:T(8,128)} %get-tuple-element.8) | data formatting | bytes 32768
  14.1 10.3 %all_to_all.10 = f32[8,1,512]{2,1,0:T(1,128)S(1)} all-to-all(f32[8,1,512]{2,1,0:T(1,128)S(1)} %reshape.24), channel_id=1, replica_groups=mesh['lat'=4,'lon'=8] {'lon'}, dimensions={0} | all-to-all | bytes 32768 | tf_op jit(solution)/shard_map/all_to_all | solution.py:328
  24.9 0.7 %reduce = f32[8,512]{1,0:T(8,128)S(1)} reduce(f32[8,1,512]{2,1,0:T(1,128)S(1)} %all_to_all.10, f32[]{:T(128)} %broadcast.1), dimensions={1}, to_apply=%all_to_all.6.reduce_sub_computation | reduce | bytes 32772 | tf_op jit(solution)/shard_map/all_to_all | solution.py:328
  25.6 0.7 %reshape.25.part_ref = f32[8,8,64]{2,1,0:T(8,128)} reshape(f32[8,512]{1,0:T(8,128)S(1)} %reduce) | data formatting | bytes 32768
  26.3 2.8 %analysis.1.refs_0_ = f32[8,2048]{1,0:T(8,128)} custom-call(f32[8,8,64]{2,1,0:T(8,128)} %reshape.25.part_ref, f32[4,64,2048]{2,1,0:T(8,128)} %refs_5_.1), custom_call_target="tpu_custom_call" | custom-call | tf_op jit(solution)/shard_map/analysis/pallas_call | solution.py:330
  29.1 2.6 %collective-permute-start = (f32[8,2048]{1,0:T(8,128)}, f32[8,2048]{1,0:T(8,128)S(1)}, u32[]{:S(2)}, u32[]{:S(2)}) collective-permute-start(f32[8,2048]{1,0:T(8,128)} %analysis.1.refs_0_), channel_id=1, source_target_pairs={{0,8},{8,0},{16,24},{24,16},{1,9},{9,1},{17,25},{25,17},{2,10},{10... | collective-permute-start | bytes 196616 | tf_op jit(solution)/shard_map/ppermute | solution.py:289
  31.7 1.5 %collective-permute-start.1 = (f32[8,2048]{1,0:T(8,128)}, f32[8,2048]{1,0:T(8,128)S(1)}, u32[]{:S(2)}, u32[]{:S(2)}) collective-permute-start(f32[8,2048]{1,0:T(8,128)} %analysis.1.refs_0_), channel_id=1, source_target_pairs={{0,16},{8,24},{16,0},{24,8},{1,17},{9,25},{17,1},{25,9},{2,18},{10... | collective-permute-start | bytes 196616 | tf_op jit(solution)/shard_map/ppermute | solution.py:289
  33.3 0.9 %collective-permute-start.2 = (f32[8,2048]{1,0:T(8,128)}, f32[8,2048]{1,0:T(8,128)S(1)}, u32[]{:S(2)}, u32[]{:S(2)}) collective-permute-start(f32[8,2048]{1,0:T(8,128)} %analysis.1.refs_0_), channel_id=1, source_target_pairs={{0,24},{8,16},{16,8},{24,0},{1,25},{9,17},{17,9},{25,1},{2,26},{10... | collective-permute-start | bytes 196616 | tf_op jit(solution)/shard_map/ppermute | solution.py:289
  34.2 2.0 %collective-permute-done.1.refs_2_ = f32[8,2048]{1,0:T(8,128)S(1)} collective-permute-done((f32[8,2048]{1,0:T(8,128)}, f32[8,2048]{1,0:T(8,128)S(1)}, u32[]{:S(2)}, u32[]{:S(2)}) %collective-permute-start.1) | collective-permute-done | bytes 65568 | tf_op jit(solution)/shard_map/ppermute | solution.py:289
  36.2 2.4 %collective-permute-done.2.refs_3_ = f32[8,2048]{1,0:T(8,128)S(1)} collective-permute-done((f32[8,2048]{1,0:T(8,128)}, f32[8,2048]{1,0:T(8,128)S(1)}, u32[]{:S(2)}, u32[]{:S(2)}) %collective-permute-start.2) | collective-permute-done | bytes 65568 | tf_op jit(solution)/shard_map/ppermute | solution.py:289
  39.5 3.0 %synthesis.1 = f32[8,128]{1,0:T(8,128)} custom-call(f32[8,2048]{1,0:T(8,128)} %analysis.1.refs_0_, f32[8,2048]{1,0:T(8,128)} %copy-done.3, f32[8,2048]{1,0:T(8,128)} %copy-done.4, f32[8,2048]{1,0:T(8,128)} %copy-done.5, f32[1,2048]{1,0:T(1,128)} %bitcast.2, f32[4,64,2048]{2,1,0:T(8,128)} %refs_5_.1, f32[4,8,3200]{2,1,0:T(8,128)} %copy-done, ...), custom_call_target="tpu_custom_call" | custom-call | tf_op jit(solution)/shard_map/synthesis/pallas_call | solution.py:343
  42.5 1.3 %broadcast_in_dim.15 = f32[8,8,128]{2,1,0:T(8,128)} broadcast(f32[8,128]{1,0:T(8,128)} %synthesis.1), dimensions={1,2} | broadcast | bytes 36864 | tf_op jit(solution)/shard_map/broadcast_in_dim | solution.py:352
  43.8 3.3 %all-to-all-start.1 = ((f32[8,8,128]{2,1,0:T(8,128)}), f32[8,8,128]{2,1,0:T(8,128)S(1)}, u32[]{:S(2)}, u32[]{:S(2)}) async-start(f32[8,8,128]{2,1,0:T(8,128)} %broadcast_in_dim.15), calls=%async_computation.1 | async-start | bytes 65536 | tf_op jit(solution)/shard_map/all_to_all | solution.py:351
  47.1 1.6 %slice.8.low_ref = f32[4,8,1080]{2,1,0:T(8,128)} slice(f32[4,8,3200]{2,1,0:T(8,128)} %copy-done), slice={[0:4], [0:8], [2048:3128]} | slice | bytes 276480 | tf_op jit(solution)/shard_map/slice | solution.py:342
  48.7 1.6 %slice.9.high_ref = f32[4,8,1080]{2,1,0:T(8,128)} slice(f32[4,8,3200]{2,1,0:T(8,128)} %copy-done.1), slice={[0:4], [0:8], [2048:3128]} | slice | bytes 276480 | tf_op jit(solution)/shard_map/slice | solution.py:342
  50.3 2.1 %sides.1 = f32[80,128]{1,0:T(8,128)} custom-call(f32[64,1080]{1,0:T(8,128)} %height_ref.7, f32[64,1080]{1,0:T(8,128)} %east_ref.5, f32[64,1080]{1,0:T(8,128)} %north_ref.5, s32[64,1080]{1,0:T(8,128)} %land_ref.5, f32[4,8,1080]{2,1,0:T(8,128)} %slice.8.low_ref, f32[4,8,1080]{2,1,0:T(8,128)} %slice.9.high_ref), custom_call_target="tpu_custom_call" | custom-call | tf_op jit(solution)/shard_map/sides/pallas_call | solution.py:355
  52.8 3.1 %collective-permute-start.6 = (f32[80,128]{1,0:T(8,128)}, f32[80,128]{1,0:T(8,128)S(1)}, u32[]{:S(2)}, u32[]{:S(2)}) collective-permute-start(f32[80,128]{1,0:T(8,128)} %sides.1), channel_id=1, source_target_pairs={{1,0},{2,1},{3,2},{4,3},{5,4},{6,5},{7,6},{0,7},{9,8},{10,9},{11,1... | collective-permute-start | bytes 122888 | tf_op jit(solution)/shard_map/ppermute | solution.py:363
  55.9 1.9 %collective-permute-done.5.left_ref = f32[80,128]{1,0:T(8,128)S(1)} collective-permute-done((f32[80,128]{1,0:T(8,128)}, f32[80,128]{1,0:T(8,128)S(1)}, u32[]{:S(2)}, u32[]{:S(2)}) %collective-permute-start.5) | collective-permute-done | bytes 40992 | tf_op jit(solution)/shard_map/ppermute | solution.py:362
  58.5 4.6 %substeps.1 = (f32[64,1080]{1,0:T(8,128)}, f32[64,1080]{1,0:T(8,128)}, f32[64,1080]{1,0:T(8,128)}, f32[64,1080]{1,0:T(8,128)}) custom-call(f32[8,8,128]{2,1,0:T(8,128)} %copy-done.2, bf16[128,1152]{1,0:T(8,128)(2,1)} %get-tuple-element.11.harm_ref, f32[64,1080]{1,0:T(8,128)} %height_ref.7, f32[64,1080]{1,0:T(8,128)} %east_ref.5, f32[64,1080]{1,0:T(8,128)} %north_ref.5, ...), custom_call_target="tpu_custom_call" | custom-call | tf_op jit(solution)/shard_map/substeps/pallas_call | solution.py:365
  (27 shorter events, 2.7 us)
Async XLA Ops:
  0.6 9.4 %copy-start.8 = (s32[32]{0:T(128)S(1)}, s32[32]{0:T(128)}, u32[]{:S(2)}) copy-start(s32[32]{0:T(128)} %param.12) | copy-start | bytes 388
  3.8 34.8 %collective-permute-start.3 = (f32[4,8,3200]{2,1,0:T(8,128)}, f32[4,8,3200]{2,1,0:T(8,128)S(1)}, u32[]{:S(2)}, u32[]{:S(2)}) collective-permute-start(f32[4,8,3200]{2,1,0:T(8,128)} %get-tuple-element.9), channel_id=1, source_target_pairs={{0,8},{8,16},{16,24},{1,9},{9,17},{17,25},{2,10},{10,18},{18,26},{... | collective-permute-start | bytes 1228808 | tf_op jit(solution)/shard_map/ppermute | solution.py:315
  8.7 29.9 %collective-permute-start.4 = (f32[4,8,3200]{2,1,0:T(8,128)}, f32[4,8,3200]{2,1,0:T(8,128)S(1)}, u32[]{:S(2)}, u32[]{:S(2)}) collective-permute-start(f32[4,8,3200]{2,1,0:T(8,128)} %get-tuple-element.10), channel_id=1, source_target_pairs={{8,0},{16,8},{24,16},{9,1},{17,9},{25,17},{10,2},{18,10},{26,18},{... | collective-permute-start | bytes 1228808 | tf_op jit(solution)/shard_map/ppermute | solution.py:316
  29.1 5.1 %collective-permute-start = (f32[8,2048]{1,0:T(8,128)}, f32[8,2048]{1,0:T(8,128)S(1)}, u32[]{:S(2)}, u32[]{:S(2)}) collective-permute-start(f32[8,2048]{1,0:T(8,128)} %analysis.1.refs_0_), channel_id=1, source_target_pairs={{0,8},{8,0},{16,24},{24,16},{1,9},{9,1},{17,25},{25,17},{2,10},{10... | collective-permute-start | bytes 196616 | tf_op jit(solution)/shard_map/ppermute | solution.py:289
  31.7 4.5 %collective-permute-start.1 = (f32[8,2048]{1,0:T(8,128)}, f32[8,2048]{1,0:T(8,128)S(1)}, u32[]{:S(2)}, u32[]{:S(2)}) collective-permute-start(f32[8,2048]{1,0:T(8,128)} %analysis.1.refs_0_), channel_id=1, source_target_pairs={{0,16},{8,24},{16,0},{24,8},{1,17},{9,25},{17,1},{25,9},{2,18},{10... | collective-permute-start | bytes 196616 | tf_op jit(solution)/shard_map/ppermute | solution.py:289
  33.3 5.4 %collective-permute-start.2 = (f32[8,2048]{1,0:T(8,128)}, f32[8,2048]{1,0:T(8,128)S(1)}, u32[]{:S(2)}, u32[]{:S(2)}) collective-permute-start(f32[8,2048]{1,0:T(8,128)} %analysis.1.refs_0_), channel_id=1, source_target_pairs={{0,24},{8,16},{16,8},{24,0},{1,25},{9,17},{17,9},{25,1},{2,26},{10... | collective-permute-start | bytes 196616 | tf_op jit(solution)/shard_map/ppermute | solution.py:289
  34.2 4.5 %copy-start.3 = (f32[8,2048]{1,0:T(8,128)}, f32[8,2048]{1,0:T(8,128)S(1)}, u32[]{:S(2)}) copy-start(f32[8,2048]{1,0:T(8,128)S(1)} %collective-permute-done.refs_1_) | copy-start | bytes 196612
  36.2 2.4 %copy-start.4 = (f32[8,2048]{1,0:T(8,128)}, f32[8,2048]{1,0:T(8,128)S(1)}, u32[]{:S(2)}) copy-start(f32[8,2048]{1,0:T(8,128)S(1)} %collective-permute-done.1.refs_2_) | copy-start | bytes 196612
  38.6 0.6 copy-start.5
  38.6 0.8 %copy-start = (f32[4,8,3200]{2,1,0:T(8,128)}, f32[4,8,3200]{2,1,0:T(8,128)S(1)}, u32[]{:S(2)}) copy-start(f32[4,8,3200]{2,1,0:T(8,128)S(1)} %collective-permute-done.3.refs_6_) | copy-start | bytes 1228804
  38.6 0.9 %copy-start.1 = (f32[4,8,3200]{2,1,0:T(8,128)}, f32[4,8,3200]{2,1,0:T(8,128)S(1)}, u32[]{:S(2)}) copy-start(f32[4,8,3200]{2,1,0:T(8,128)S(1)} %collective-permute-done.4.refs_7_) | copy-start | bytes 1228804
  43.8 14.1 %all-to-all-start.1 = ((f32[8,8,128]{2,1,0:T(8,128)}), f32[8,8,128]{2,1,0:T(8,128)S(1)}, u32[]{:S(2)}, u32[]{:S(2)}) async-start(f32[8,8,128]{2,1,0:T(8,128)} %broadcast_in_dim.15), calls=%async_computation.1 | async-start | bytes 65536 | tf_op jit(solution)/shard_map/all_to_all | solution.py:351
  52.4 5.4 %collective-permute-start.5 = (f32[80,128]{1,0:T(8,128)}, f32[80,128]{1,0:T(8,128)S(1)}, u32[]{:S(2)}, u32[]{:S(2)}) collective-permute-start(f32[80,128]{1,0:T(8,128)} %sides.1), channel_id=1, source_target_pairs={{0,1},{1,2},{2,3},{3,4},{4,5},{5,6},{6,7},{7,0},{8,9},{9,10},{10,1... | collective-permute-start | bytes 122888 | tf_op jit(solution)/shard_map/ppermute | solution.py:362
  52.8 5.1 %collective-permute-start.6 = (f32[80,128]{1,0:T(8,128)}, f32[80,128]{1,0:T(8,128)S(1)}, u32[]{:S(2)}, u32[]{:S(2)}) collective-permute-start(f32[80,128]{1,0:T(8,128)} %sides.1), channel_id=1, source_target_pairs={{1,0},{2,1},{3,2},{4,3},{5,4},{6,5},{7,6},{0,7},{9,8},{10,9},{11,1... | collective-permute-start | bytes 122888 | tf_op jit(solution)/shard_map/ppermute | solution.py:363
  57.8 0.6 copy-start.6
  57.9 0.6 copy-start.7
  57.9 0.6 copy-start.2

commit v2 on v1

--- a/solution.py
+++ b/solution.py
@@ -15,7 +15,11 @@
 f32 = jnp.float32
 bf16 = jnp.bfloat16
 VMEM = pl.BlockSpec(memory_space=pltpu.VMEM)
+HBM = pl.BlockSpec(memory_space=pltpu.HBM)
 SMEM = pl.BlockSpec(memory_space=pltpu.SMEM)
+
+
+LIMIT = pltpu.CompilerParams(vmem_limit_bytes=24 * 2**20)
 
 
 def split2(x):
@@ -24,16 +28,27 @@
     return hi, lo
 
 
-def dft_kernel(period, own_waves, first_ref, waves_ref, height_ref, part_ref, harm_ref, field_ref):
-    rows, cols = height_ref.shape
+def harmonic_rows(period, cols, slots, me_ref, waves_ref, harm_ref):
     waves, width = harm_ref.shape[0] // 2, harm_ref.shape[1]
-    wave = waves_ref[...]
-    start = wave * first_ref[0]
+    sectors = waves // (2 * slots)
+    me = me_ref[0]
+    row = lax.broadcasted_iota(jnp.int32, (2 * slots, 1), 0)
+    groups = []
+    for core in range(2):
+        for chip in range(sectors // 2):
+            owner = lax.bitwise_xor(me, 2 * chip + core)
+            group = jnp.zeros((2 * slots, 1), jnp.int32)
+            for slot in range(slots):
+                value = waves_ref[owner * slots + slot]
+                group = jnp.where((row == slot) | (row == slots + slot), value, group)
+            groups.append(group)
+    wave = jnp.concatenate(groups, axis=0)
+    start = wave * (me * cols)
     turns = jnp.floor(start.astype(f32) * (1.0 / period)).astype(jnp.int32)
     start = (start - turns * period).astype(f32)
     wave = wave.astype(f32)
     row = lax.broadcasted_iota(jnp.int32, (waves, 1), 0)
-    sine = (lax.rem(row, 2 * own_waves) >= own_waves).astype(f32)
+    sine = (lax.rem(row, 2 * slots) >= slots).astype(f32)
     offset = 4.0 * start - period * sine
     for tile in range(0, width, 128):
         lane = lax.broadcasted_iota(jnp.int32, (1, 128), 1) + tile
@@ -59,6 +74,28 @@
         hi, lo = split2(value)
         harm_ref[:waves, tile : tile + 128] = hi
         harm_ref[waves:, tile : tile + 128] = lo
+
+
+def dft_kernel(
+    period,
+    slots,
+    me_ref,
+    waves_ref,
+    height_hbm,
+    keep_ref,
+    send_ref,
+    harm_ref,
+    height_ref,
+    field_ref,
+    semaphore,
+):
+    copy = pltpu.make_async_copy(height_hbm, height_ref, semaphore)
+    copy.start()
+    rows, cols = height_ref.shape
+    waves, width = harm_ref.shape[0] // 2, harm_ref.shape[1]
+    harmonic_rows(period, cols, slots, me_ref, waves_ref, harm_ref)
+    copy.wait()
+    for tile in range(0, width, 128):
         stop = min(cols, tile + 128)
         if stop <= tile:
             block = jnp.zeros((rows, 128), f32)
@@ -76,12 +113,16 @@
     )
     total = both[:waves] + both[waves:]
     total = (total[:, :rows] + total[:, rows:]) * (1.0 / math.sqrt(period))
-    part_ref[...] = total.reshape(part_ref.shape)
-
-
-def analysis_kernel(part_ref, legendre_ref, spectral_ref):
+    total = jnp.concatenate([total, jnp.zeros((waves, 128 - rows), f32)], axis=1)
+    keep_ref[...] = total[: waves // 2].reshape(keep_ref.shape)
+    send_ref[...] = total[waves // 2 :].reshape(send_ref.shape)
+
+
+def analysis_kernel(part_refs, legendre_ref, spectral_ref):
     slots, rows, degrees = legendre_ref.shape
-    fourier = jnp.sum(part_ref[...], axis=0)
+    fourier = part_refs[0][...]
+    for ref in part_refs[1:]:
+        fourier = fourier + ref[...]
     columns = fourier.T
     for slot in range(slots):
         even = [
@@ -141,14 +182,13 @@
 
 
 def substep_kernel(
-    synth_ref,
+    cols,
+    synth_refs,
     harm_ref,
-    height_ref,
+    surface_ref,
     east_ref,
     north_ref,
-    land_ref,
-    low_ref,
-    high_ref,
+    wet,
     left_ref,
     right_ref,
     loading_out,
@@ -160,13 +200,14 @@
     surface,
     east,
     north,
-    wet,
 ):
-    rows, cols = height_ref.shape
-    taller = rows + 2 * MARGIN
-    width = harm_ref.shape[1]
+    taller, width = surface_ref.shape
+    rows = taller - 2 * MARGIN
     waves = harm_ref.shape[0] // 2
-    synth = synth_ref[...].reshape(waves, 128).T * (1.0 / math.sqrt(waves // 2))
+    synth = jnp.concatenate(
+        [ref[core] for core in range(2) for ref in synth_refs], axis=0
+    )
+    synth = synth.T * (1.0 / math.sqrt(waves // 2))
     hi, lo = split2(synth[:taller])
     left = jnp.concatenate(
         [jnp.concatenate([hi, hi], axis=1), jnp.concatenate([lo, lo], axis=1)], axis=0
@@ -179,33 +220,18 @@
     own = cols - last
     lanes = lax.broadcasted_iota(jnp.int32, (taller, width - last), 1)
     for at, (target, top, source) in enumerate(
-        (
-            (surface, 0, height_ref),
-            (east, 0, east_ref),
-            (north, 8, north_ref),
-            (wet, 0, land_ref),
-        )
+        ((surface, 0, surface_ref), (east, 0, east_ref), (north, 8, north_ref), (wet, 0, wet))
     ):
-        lows, middle, highs = (
-            pl.ds(top, MARGIN),
-            pl.ds(top + MARGIN, rows),
-            pl.ds(top + MARGIN + rows, MARGIN),
-        )
-        target[lows, :last] = low_ref[at, :, :last]
-        target[middle, :last] = source[:, :last].astype(f32)
-        target[highs, :last] = high_ref[at, :, :last]
-        tail = jnp.concatenate(
-            [low_ref[at, :, last:cols], source[:, last:].astype(f32), high_ref[at, :, last:cols]],
-            axis=0,
-        )
-        tail = jnp.concatenate([tail, jnp.zeros((taller, width - cols), f32)], axis=1)
+        inside = pl.ds(top, taller)
+        if source is not target:
+            target[inside, :last] = source[:, :last]
         after = pltpu.roll(right_ref[...], (own - 2 * MARGIN * at) % 128, 1)
         before = pltpu.roll(left_ref[...], (-MARGIN - 2 * MARGIN * at - MARGIN) % 128, 1)
         after = jnp.concatenate([after] * ((width - last) // 128), axis=1)
         before = jnp.concatenate([before] * ((width - last) // 128), axis=1)
-        tail = jnp.where((lanes >= own) & (lanes < own + MARGIN), after, tail)
+        tail = jnp.where((lanes >= own) & (lanes < own + MARGIN), after, source[:, last:])
         tail = jnp.where(lanes >= width - last - MARGIN, before, tail)
-        target[pl.ds(top, taller), last:] = tail
+        target[inside, last:] = tail
     edge = jnp.zeros((8, width), f32)
     pressure[:8] = edge
     pressure[taller + 8 :] = edge
@@ -237,44 +263,101 @@
 
 
 def edges_kernel(
-    legendre_ref, height_ref, east_ref, north_ref, land_ref, up_ref, down_ref, semaphore
+    legendre_hbm,
+    height_hbm,
+    east_hbm,
+    north_hbm,
+    land_hbm,
+    up_ref,
+    down_ref,
+    flows,
+    lands,
+    semaphores,
 ):
-    slots, rows, degrees = legendre_ref.shape
-    cols = height_ref.shape[1]
+    slots, rows, degrees = legendre_hbm.shape
+    cols = height_hbm.shape[1]
+    copies = []
+    for side, (ref, first) in enumerate(((up_ref, rows - MARGIN), (down_ref, 0))):
+        band = pl.ds(first, MARGIN)
+        copies.append((height_hbm.at[band], flows.at[side, 0]))
+        copies.append((east_hbm.at[band], flows.at[side, 1]))
+        copies.append((north_hbm.at[band], flows.at[side, 2]))
+        copies.append((land_hbm.at[band], lands.at[side]))
+        copies.append((legendre_hbm.at[:, band], ref.at[pl.ds(0, slots), :, pl.ds(0, degrees)]))
     copies = [
-        pltpu.make_async_copy(
-            legendre_ref.at[:, pl.ds(first, MARGIN), :],
-            ref.at[pl.ds(0, slots), :, pl.ds(0, degrees)],
-            semaphore.at[at],
-        )
-        for at, (ref, first) in enumerate(((up_ref, rows - MARGIN), (down_ref, 0)))
+        pltpu.make_async_copy(source, target, semaphores.at[at])
+        for at, (source, target) in enumerate(copies)
     ]
     for copy in copies:
         copy.start()
-    for at, source in enumerate((height_ref, east_ref, north_ref, land_ref)):
-        up_ref[at, :, degrees : degrees + cols] = source[rows - MARGIN :].astype(f32)
-        down_ref[at, :, degrees : degrees + cols] = source[:MARGIN].astype(f32)
     for copy in copies:
         copy.wait()
-
-
-def sides_kernel(
-    height_ref, east_ref, north_ref, land_ref, low_ref, high_ref, tile_ref
+    for side, ref in enumerate((up_ref, down_ref)):
+        for at in range(3):
+            ref[at, :, degrees : degrees + cols] = flows[side, at]
+        ref[3, :, degrees : degrees + cols] = lands[side].astype(f32)
+
+
+def windows_kernel(
+    base,
+    height_hbm,
+    east_hbm,
+    north_hbm,
+    land_hbm,
+    low_ref,
+    high_ref,
+    surface_ref,
+    east_ref,
+    north_ref,
+    wet_ref,
+    tile_ref,
+    fields,
+    land,
+    semaphores,
 ):
-    rows, cols = height_ref.shape
+    rows, cols = height_hbm.shape
+    width = surface_ref.shape[1]
     taller = rows + 2 * MARGIN
+    last = (cols // 128) * 128
+    copies = [
+        pltpu.make_async_copy(source, target, semaphores.at[at])
+        for at, (source, target) in enumerate(
+            (
+                (height_hbm, fields.at[0]),
+                (east_hbm, fields.at[1]),
+                (north_hbm, fields.at[2]),
+                (land_hbm, land),
+            )
+        )
+    ]
+    for copy in copies:
+        copy.start()
     pieces = []
-    for at, source in enumerate((height_ref, east_ref, north_ref, land_ref)):
-        for first in (0, cols - MARGIN):
-            window = slice(first, first + MARGIN)
-            pieces.append(
-                jnp.concatenate(
-                    [low_ref[at, :, window], source[:, window].astype(f32), high_ref[at, :, window]],
-                    axis=0,
-                )
-            )
+    for at, target in enumerate((surface_ref, east_ref, north_ref, wet_ref)):
+        copies[at].wait()
+        source = fields.at[at] if at < 3 else land
+        target[:MARGIN, :last] = low_ref[at, :, base : base + last]
+        target[MARGIN : MARGIN + rows, :last] = source[:, :last].astype(f32)
+        target[MARGIN + rows :, :last] = high_ref[at, :, base : base + last]
+        tail = jnp.concatenate(
+            [
+                low_ref[at, :, base + last : base + cols],
+                source[:, last:].astype(f32),
+                high_ref[at, :, base + last : base + cols],
+            ],
+            axis=0,
+        )
+        target[:, last:] = jnp.concatenate(
+            [tail, jnp.zeros((taller, width - cols), f32)], axis=1
+        )
+        pieces.append(target[:, :MARGIN])
+        pieces.append(target[:, cols - MARGIN : cols])
     pieces.append(jnp.zeros((taller, 128 - 8 * MARGIN), f32))
     tile_ref[...] = jnp.concatenate(pieces, axis=1)
+
+
+def in_hbm(x):
+    return pltpu.with_memory_space_constraint(x, pltpu.HBM)
 
 
 def struct(shape, dtype=f32):
@@ -304,42 +387,61 @@
     eastward = [(i, (i + 1) % sectors) for i in range(sectors)]
     westward = [(target, source) for source, target in eastward]
 
+    chips = sectors // 2
+    pair = [(i, i ^ 1) for i in range(sectors)]
+    chain = [[(i, i ^ (2 * chip)) for i in range(sectors)] for chip in range(1, chips)]
+    me = lax.axis_index("lon").astype(jnp.int32).reshape(1)
+    keep, send, harmonics = pl.pallas_call(
+        functools.partial(dft_kernel, period, slots),
+        out_shape=[struct((chips, 2 * slots, 128))] * 2 + [struct((4 * waves, width), bf16)],
+        in_specs=[SMEM, SMEM, HBM],
+        out_specs=[VMEM] * 3,
+        scratch_shapes=[
+            pltpu.VMEM((rows, cols), f32),
+            pltpu.VMEM((2 * rows, width), bf16),
+            pltpu.SemaphoreType.DMA,
+        ],
+        name="dft",
+        compiler_params=LIMIT,
+    )(me, wavenumbers, in_hbm(height))
+    part = keep + lax.ppermute(send, "lon", pair)
+    part, legendre_later = lax.optimization_barrier((part, legendre))
     up, down = pl.pallas_call(
         edges_kernel,
         out_shape=[struct((max(4, slots), MARGIN, degrees + width))] * 2,
-        in_specs=[pl.BlockSpec(memory_space=pl.ANY)] + [VMEM] * 4,
+        in_specs=[HBM] * 5,
         out_specs=[VMEM] * 2,
-        scratch_shapes=[pltpu.SemaphoreType.DMA((2,))],
+        scratch_shapes=[
+            pltpu.VMEM((2, 3, MARGIN, cols), f32),
+            pltpu.VMEM((2, MARGIN, cols), jnp.int32),
+            pltpu.SemaphoreType.DMA((10,)),
+        ],
         name="edges",
-    )(legendre, height, east_flow, north_flow, land_sea)
+        compiler_params=LIMIT,
+    )(*map(in_hbm, (legendre_later, height, east_flow, north_flow, land_sea)))
     low = lax.ppermute(up, "lat", upward)
     high = lax.ppermute(down, "lat", downward)
 
-    first = (lax.axis_index("lon") * cols).astype(jnp.int32).reshape(1)
-    column = jnp.broadcast_to(wavenumbers.reshape(sectors, 1, slots), (sectors, 2, slots))
-    part, harmonics = pl.pallas_call(
-        functools.partial(dft_kernel, period, slots),
-        out_shape=[struct((sectors, 2 * slots, rows)), struct((4 * waves, width), bf16)],
-        in_specs=[SMEM, VMEM, VMEM],
-        out_specs=[VMEM, VMEM],
-        scratch_shapes=[pltpu.VMEM((2 * rows, width), bf16)],
-        name="dft",
-    )(first, column.reshape(2 * waves, 1), height)
-    parts = lax.all_to_all(part, "lon", 0, 0, tiled=True)
+    parts = [part[0]] + [
+        lax.ppermute(part[chip], "lon", links) for chip, links in enumerate(chain, 1)
+    ]
+
+    def analysis(*refs):
+        analysis_kernel(refs[:chips], *refs[chips:])
 
     spectral = pl.pallas_call(
-        analysis_kernel,
+        analysis,
         out_shape=struct((2 * slots, degrees)),
-        in_specs=[VMEM, VMEM],
+        in_specs=[VMEM] * (chips + 1),
         out_specs=VMEM,
         name="analysis",
-    )(parts, legendre)
+        compiler_params=LIMIT,
+    )(*parts, legendre)
     pieces = lat_sum_parts(spectral)
 
     def synthesis(*refs):
         synthesis_kernel(refs[: len(pieces)], *refs[len(pieces) :])
 
-    low_rows, high_rows = low[:, :, degrees : degrees + cols], high[:, :, degrees : degrees + cols]
     synth = pl.pallas_call(
         synthesis,
         out_shape=struct((2 * slots, 128)),
@@ -347,25 +449,34 @@
         out_specs=VMEM,
         scratch_shapes=[pltpu.VMEM((2 * slots, degrees), f32)],
         name="synthesis",
+        compiler_params=LIMIT,
     )(*pieces, love_numbers.reshape(1, degrees), legendre, low, high)
-    everyone = lax.all_to_all(
-        jnp.broadcast_to(synth[None], (sectors, 2 * slots, 128)), "lon", 0, 0, tiled=True
-    )
-
-    sides = pl.pallas_call(
-        sides_kernel,
-        out_shape=struct((taller, 128)),
-        in_specs=[VMEM] * 6,
-        out_specs=VMEM,
-        name="sides",
-    )(height, east_flow, north_flow, land_sea, low_rows, high_rows)
+    both = jnp.stack([synth, lax.ppermute(synth, "lon", pair)])
+    everyone = [both] + [lax.ppermute(both, "lon", links) for links in chain]
+
+    surface, east, north, wet, sides = pl.pallas_call(
+        functools.partial(windows_kernel, degrees),
+        out_shape=[struct((taller, width))] * 4 + [struct((taller, 128))],
+        in_specs=[HBM] * 4 + [VMEM] * 2,
+        out_specs=[VMEM] * 5,
+        scratch_shapes=[
+            pltpu.VMEM((3, rows, cols), f32),
+            pltpu.VMEM((rows, cols), jnp.int32),
+            pltpu.SemaphoreType.DMA((4,)),
+        ],
+        name="windows",
+        compiler_params=LIMIT,
+    )(*map(in_hbm, (height, east_flow, north_flow, land_sea)), low, high)
     left = lax.ppermute(sides, "lon", eastward)
     right = lax.ppermute(sides, "lon", westward)
 
+    def substeps(*refs):
+        substep_kernel(cols, refs[:chips], *refs[chips:])
+
     return pl.pallas_call(
-        substep_kernel,
+        substeps,
         out_shape=[struct((rows, cols))] * 4,
-        in_specs=[VMEM] * 10,
+        in_specs=[VMEM] * (chips + 7),
         out_specs=[VMEM] * 4,
         scratch_shapes=[
             pltpu.VMEM((taller, width), f32),
@@ -373,21 +484,10 @@
             pltpu.VMEM((taller, width), f32),
             pltpu.VMEM((taller, width), f32),
             pltpu.VMEM((taller + 16, width), f32),
-            pltpu.VMEM((taller, width), f32),
         ],
         name="substeps",
-    )(
-        everyone,
-        harmonics,
-        height,
-        east_flow,
-        north_flow,
-        land_sea,
-        low_rows,
-        high_rows,
-        left,
-        right,
-    )
+        compiler_params=LIMIT,
+    )(*everyone, harmonics, surface, east, north, wet, left, right)
 
 
 def solution(mesh):

time: 63.7 us -> 49 us (0.77)
  blocking collectives: 10.3 us -> 0 us
  Pallas kernels: 18 us -> 8.79 us
  local copies, waits for them, and re-layouts: 8.79 us -> 0.81 us
  waiting for transfers between devices: 6.51 us -> 13.6 us
  starting transfers between devices: 18.1 us -> 24.3 us
  other arithmetic: 0.68 us -> 0.01 us
    all_to_all x1 -> x0, blocking collectives: 10.3 us -> none  [shards(): parts = lax.all_to_all(part, 'lon', 0, 0, tiled=True)]
    ppermute x0 -> x8, starting transfers between devices: none -> 9.43 us  [the longest x3 4.45 us: shards(): lax.ppermute(part[chip], 'lon', links)]
    ppermute x0 -> x8, waiting for transfers between devices: none -> 6.18 us  [the longest x3 3.72 us: shards(): lax.ppermute(part[chip], 'lon', links)]
    pallas_call x3, Pallas kernels: 9.48 us -> 5.11 us  [the longest x1 3.14 us: shards(): pl.pallas_call(substeps, out_shape=[struct((rows, cols))] * 4, in_specs=[...]
    all_to_all x1 -> x0, starting transfers between devices: 3.34 us -> none  [shards(): lax.all_to_all(jnp.broadcast_to(synth[None], (sectors, 2 * slots, 128)),...]
    slice x2 -> x0, local copies, waits for them, and re-layouts: 3.17 us -> none  [the longest x1 1.59 us: shards(): high[:, :, degrees:degrees + cols]]
    ppermute x3, waiting for transfers between devices: 4.52 us -> 7.41 us  [lat_sum_parts(): lax.ppermute(value, 'lat', [(i, i ^ step) for i in range(count)])]
    pallas_call x1, Pallas kernels: 2.97 us -> 0.51 us  [shards(): pl.pallas_call(synthesis, out_shape=struct((2 * slots, 128)), in_specs=[V...]
  transfers between devices with their start and end apart: 8 -> 15, of which waited for: 5 -> 9; matrix products, arithmetic and copies ran while one was open for 11% -> 0% of each run, Pallas kernels for 12% -> 4%
where the time goes in v2:
time: 49 us; the launch traced here: 48.3 us
  starting transfers between devices  24.3 us (50%)
  waiting for transfers between devices  13.6 us (28%)
  Pallas kernels  8.79 us (18%)
  local copies, waits for them, and re-layouts  0.81 us (2%)
  between operations  0.74 us (2%)
    ppermute x3, waiting for transfers between devices, lat_sum_parts(): lax.ppermute(value, 'lat', [(i, i ^ step) for i in range(count)])  7.41 us
    ppermute x3, starting transfers between devices, lat_sum_parts(): lax.ppermute(value, 'lat', [(i, i ^ step) for i in range(count)])  5.08 us
    ppermute x1, starting transfers between devices, shards(): low = lax.ppermute(up, 'lat', upward)  4.76 us
    ppermute x3, starting transfers between devices, shards(): lax.ppermute(part[chip], 'lon', links)  4.45 us
    ppermute x3, starting transfers between devices, shards(): everyone = [both] + [lax.ppermute(both, 'lon', links) for links in chain]  4.45 us
    ppermute x1, starting transfers between devices, shards(): right = lax.ppermute(sides, 'lon', westward)  3.75 us
    ppermute x3, waiting for transfers between devices, shards(): lax.ppermute(part[chip], 'lon', links)  3.72 us
    pallas_call x1, Pallas kernels, shards(): pl.pallas_call(substeps, out_shape=[struct((rows, cols))] * 4, in_specs=[...  3.14 us
  transfers between devices with their start and end apart: 15, of which 9 were waited for; matrix products, arithmetic and copies ran while one was open for 0% of the time, Pallas kernels for 4%

profile of v2, /device:TPU:0, one launch (start us, length us, event | category | flops | bytes accessed | tf_op | source)
XLA Modules:
  0.0 48.3 jit_solution(17842120633892001450)
XLA Ops:
  0.7 0.8 %copy-done.2 = s32[32]{0:T(128)S(1)} copy-done((s32[32]{0:T(128)S(1)}, s32[32]{0:T(128)}, u32[]{:S(2)}) %copy-start.2) | copy-done | bytes 152
  1.4 1.9 %dft.1 = (f32[4,8,128]{2,1,0:T(8,128)S(1)}, f32[4,8,128]{2,1,0:T(8,128)S(1)}, bf16[128,1152]{1,0:T(8,128)(2,1)S(1)}) custom-call(s32[1]{0:T(128)} %bitcast.me_ref, s32[32]{0:T(128)S(1)} %copy-done.2, f32[64,1080]{1,0:T(8,128)} %height_hbm.5), custom_call_target="tpu_custom_call" | custom-call | tf_op jit(solution)/shard_map/dft/pallas_call | solution.py:394
  3.3 0.5 %collective-permute-start = (f32[4,8,128]{2,1,0:T(8,128)S(1)}, f32[4,8,128]{2,1,0:T(8,128)S(1)}, u32[]{:S(2)}, u32[]{:S(2)}) collective-permute-start(f32[4,8,128]{2,1,0:T(8,128)S(1)} %get-tuple-element.17), channel_id=1, source_target_pairs={{0,1},{1,0},{2,3},{3,2},{4,5},{5,4},{6,7},{7,6},{8,9},{9,8},{10,11... | collective-permute-start | bytes 49160 | tf_op jit(solution)/shard_map/ppermute | solution.py:407
  3.8 0.8 %collective-permute-done = f32[4,8,128]{2,1,0:T(8,128)S(1)} collective-permute-done((f32[4,8,128]{2,1,0:T(8,128)S(1)}, f32[4,8,128]{2,1,0:T(8,128)S(1)}, u32[]{:S(2)}, u32[]{:S(2)}) %collective-permute-start) | collective-permute-done | bytes 16416 | tf_op jit(solution)/shard_map/ppermute | solution.py:407
  4.7 1.3 %edges.1 = (f32[4,8,3200]{2,1,0:T(8,128)S(1)}, f32[4,8,3200]{2,1,0:T(8,128)S(1)}) custom-call(f32[4,64,2048]{2,1,0:T(8,128)} %refs_5_.1, f32[64,1080]{1,0:T(8,128)} %height_hbm.5, f32[64,1080]{1,0:T(8,128)} %east_hbm.3, f32[64,1080]{1,0:T(8,128)} %north_hbm.3, s32[64,1080]{1,0:T(8,128)} %land_hbm.3), custom_call_target="tpu_custom_call" | custom-call | tf_op jit(solution)/shard_map/edges/pallas_call | solution.py:409
  6.0 4.8 %collective-permute-start.7 = (f32[4,8,3200]{2,1,0:T(8,128)S(1)}, f32[4,8,3200]{2,1,0:T(8,128)S(1)}, u32[]{:S(2)}, u32[]{:S(2)}) collective-permute-start(f32[4,8,3200]{2,1,0:T(8,128)S(1)} %get-tuple-element.20), channel_id=1, source_target_pairs={{0,8},{8,16},{16,24},{1,9},{9,17},{17,25},{2,10},{10,18},{18,26},{... | collective-permute-start | bytes 1228808 | tf_op jit(solution)/shard_map/ppermute | solution.py:422
  10.8 1.3 %collective-permute-start.8 = (f32[4,8,3200]{2,1,0:T(8,128)S(1)}, f32[4,8,3200]{2,1,0:T(8,128)S(1)}, u32[]{:S(2)}, u32[]{:S(2)}) collective-permute-start(f32[4,8,3200]{2,1,0:T(8,128)S(1)} %get-tuple-element.21), channel_id=1, source_target_pairs={{8,0},{16,8},{24,16},{9,1},{17,9},{25,17},{10,2},{18,10},{26,18},{... | collective-permute-start | bytes 1228808 | tf_op jit(solution)/shard_map/ppermute | solution.py:423
  12.1 3.7 %collective-permute-start.3 = (f32[8,128]{1,0:T(8,128)S(1)}, f32[8,128]{1,0:T(8,128)S(1)}, u32[]{:S(2)}, u32[]{:S(2)}) collective-permute-start(f32[8,128]{1,0:T(8,128)S(1)} %get-tuple-element.28), channel_id=1, source_target_pairs={{0,6},{1,7},{2,4},{3,5},{4,2},{5,3},{6,0},{7,1},{8,14},{9,15},{10,... | collective-permute-start | bytes 12296 | tf_op jit(solution)/shard_map/ppermute | solution.py:426
  15.8 0.8 %collective-permute-start.1 = (f32[8,128]{1,0:T(8,128)S(1)}, f32[8,128]{1,0:T(8,128)S(1)}, u32[]{:S(2)}, u32[]{:S(2)}) collective-permute-start(f32[8,128]{1,0:T(8,128)S(1)} %get-tuple-element.30), channel_id=1, source_target_pairs={{0,2},{1,3},{2,0},{3,1},{4,6},{5,7},{6,4},{7,5},{8,10},{9,11},{10,... | collective-permute-start | bytes 12296 | tf_op jit(solution)/shard_map/ppermute | solution.py:426
  16.5 1.0 %collective-permute-done.3.refs_3_ = f32[8,128]{1,0:T(8,128)S(1)} collective-permute-done((f32[8,128]{1,0:T(8,128)S(1)}, f32[8,128]{1,0:T(8,128)S(1)}, u32[]{:S(2)}, u32[]{:S(2)}) %collective-permute-start.3) | collective-permute-done | bytes 4128 | tf_op jit(solution)/shard_map/ppermute | solution.py:426
  17.6 2.7 %collective-permute-done.2.refs_2_ = f32[8,128]{1,0:T(8,128)S(1)} collective-permute-done((f32[8,128]{1,0:T(8,128)S(1)}, f32[8,128]{1,0:T(8,128)S(1)}, u32[]{:S(2)}, u32[]{:S(2)}) %collective-permute-start.2) | collective-permute-done | bytes 4128 | tf_op jit(solution)/shard_map/ppermute | solution.py:426
  20.3 0.6 %analysis.1.refs_0_ = f32[8,2048]{1,0:T(8,128)S(1)} custom-call(f32[8,128]{1,0:T(8,128)S(1)} %get-tuple-element.31.refs_0_, f32[8,128]{1,0:T(8,128)S(1)} %collective-permute-done.1.refs_1_, f32[8,128]{1,0:T(8,128)S(1)} %collective-permute-done.2.refs_2_, f32[8,128]{1,0:T(8,128)S(1)} %collective-permute-done.3.refs_3_, f32[4,64,2048]{2,1,0:T(8,128)S(1)} %copy-done), custom_call_target="tpu_custom_call" | custom-call | tf_op jit(solution)/shard_map/analysis/pallas_call | solution.py:432
  20.8 3.7 %collective-permute-start.6 = (f32[8,2048]{1,0:T(8,128)S(1)}, f32[8,2048]{1,0:T(8,128)S(1)}, u32[]{:S(2)}, u32[]{:S(2)}) collective-permute-start(f32[8,2048]{1,0:T(8,128)S(1)} %analysis.1.refs_0_), channel_id=1, source_target_pairs={{0,24},{8,16},{16,8},{24,0},{1,25},{9,17},{17,9},{25,1},{2,26},{10... | collective-permute-start | bytes 196616 | tf_op jit(solution)/shard_map/ppermute | solution.py:372
  25.0 0.9 %collective-permute-start.4 = (f32[8,2048]{1,0:T(8,128)S(1)}, f32[8,2048]{1,0:T(8,128)S(1)}, u32[]{:S(2)}, u32[]{:S(2)}) collective-permute-start(f32[8,2048]{1,0:T(8,128)S(1)} %analysis.1.refs_0_), channel_id=1, source_target_pairs={{0,8},{8,0},{16,24},{24,16},{1,9},{9,1},{17,25},{25,17},{2,10},{10... | collective-permute-start | bytes 196616 | tf_op jit(solution)/shard_map/ppermute | solution.py:372
  25.9 1.4 %collective-permute-done.6.refs_3_ = f32[8,2048]{1,0:T(8,128)S(1)} collective-permute-done((f32[8,2048]{1,0:T(8,128)S(1)}, f32[8,2048]{1,0:T(8,128)S(1)}, u32[]{:S(2)}, u32[]{:S(2)}) %collective-permute-start.6) | collective-permute-done | bytes 65568 | tf_op jit(solution)/shard_map/ppermute | solution.py:372
  27.3 1.4 %collective-permute-done.5.refs_2_ = f32[8,2048]{1,0:T(8,128)S(1)} collective-permute-done((f32[8,2048]{1,0:T(8,128)S(1)}, f32[8,2048]{1,0:T(8,128)S(1)}, u32[]{:S(2)}, u32[]{:S(2)}) %collective-permute-start.5) | collective-permute-done | bytes 65568 | tf_op jit(solution)/shard_map/ppermute | solution.py:372
  28.8 4.6 %collective-permute-done.4.refs_1_ = f32[8,2048]{1,0:T(8,128)S(1)} collective-permute-done((f32[8,2048]{1,0:T(8,128)S(1)}, f32[8,2048]{1,0:T(8,128)S(1)}, u32[]{:S(2)}, u32[]{:S(2)}) %collective-permute-start.4) | collective-permute-done | bytes 65568 | tf_op jit(solution)/shard_map/ppermute | solution.py:372
  33.3 0.5 %synthesis.1 = f32[8,128]{1,0:T(8,128)S(1)} custom-call(f32[8,2048]{1,0:T(8,128)S(1)} %analysis.1.refs_0_, f32[8,2048]{1,0:T(8,128)S(1)} %collective-permute-done.4.refs_1_, f32[8,2048]{1,0:T(8,128)S(1)} %collective-permute-done.5.refs_2_, f32[8,2048]{1,0:T(8,128)S(1)} %collective-permute-done.6.refs_3_, f32[1,2048]{1,0:T(1,128)S(1)} %bitcast.13, ...), custom_call_target="tpu_custom_call" | custom-call | tf_op jit(solution)/shard_map/synthesis/pallas_call | solution.py:445
  33.9 1.4 %windows.1 = (f32[80,1152]{1,0:T(8,128)S(1)}, f32[80,1152]{1,0:T(8,128)S(1)}, f32[80,1152]{1,0:T(8,128)S(1)}, f32[80,1152]{1,0:T(8,128)S(1)}, f32[80,128]{1,0:T(8,128)S(1)}) custom-call(f32[64,1080]{1,0:T(8,128)} %height_hbm.5, f32[64,1080]{1,0:T(8,128)} %east_hbm.3, f32[64,1080]{1,0:T(8,128)} %north_hbm.3, s32[64,1080]{1,0:T(8,128)} %land_hbm.3, ...), custom_call_target="tpu_custom_call" | custom-call | tf_op jit(solution)/shard_map/windows/pallas_call | solution.py:457
  35.3 3.8 %collective-permute-start.14 = (f32[80,128]{1,0:T(8,128)S(1)}, f32[80,128]{1,0:T(8,128)S(1)}, u32[]{:S(2)}, u32[]{:S(2)}) collective-permute-start(f32[80,128]{1,0:T(8,128)S(1)} %get-tuple-element.27), channel_id=1, source_target_pairs={{1,0},{2,1},{3,2},{4,3},{5,4},{6,5},{7,6},{0,7},{9,8},{10,9},{11,1... | collective-permute-start | bytes 122888 | tf_op jit(solution)/shard_map/ppermute | solution.py:471
  39.0 0.5 %collective-permute-start.12 = (f32[2,8,128]{2,1,0:T(8,128)S(1)}, f32[2,8,128]{2,1,0:T(8,128)S(1)}, u32[]{:S(2)}, u32[]{:S(2)}) collective-permute-start(f32[2,8,128]{2,1,0:T(8,128)S(1)} %pad_maximum_fusion.refs_0_), channel_id=1, source_target_pairs={{0,6},{1,7},{2,4},{3,5},{4,2},{5,3},{6,0},{7,1},{8,14},{9,15},{10,... | collective-permute-start | bytes 24584 | tf_op jit(solution)/shard_map/ppermute | solution.py:455
  39.6 3.9 %collective-permute-start.10 = (f32[2,8,128]{2,1,0:T(8,128)S(1)}, f32[2,8,128]{2,1,0:T(8,128)S(1)}, u32[]{:S(2)}, u32[]{:S(2)}) collective-permute-start(f32[2,8,128]{2,1,0:T(8,128)S(1)} %pad_maximum_fusion.refs_0_), channel_id=1, source_target_pairs={{0,2},{1,3},{2,0},{3,1},{4,6},{5,7},{6,4},{7,5},{8,10},{9,11},{10,... | collective-permute-start | bytes 24584 | tf_op jit(solution)/shard_map/ppermute | solution.py:455
  43.5 1.1 %collective-permute-done.12.refs_3_ = f32[2,8,128]{2,1,0:T(8,128)S(1)} collective-permute-done((f32[2,8,128]{2,1,0:T(8,128)S(1)}, f32[2,8,128]{2,1,0:T(8,128)S(1)}, u32[]{:S(2)}, u32[]{:S(2)}) %collective-permute-start.12) | collective-permute-done | bytes 8224 | tf_op jit(solution)/shard_map/ppermute | solution.py:455
  45.1 3.1 %substeps.1 = (f32[64,1080]{1,0:T(8,128)}, f32[64,1080]{1,0:T(8,128)}, f32[64,1080]{1,0:T(8,128)}, f32[64,1080]{1,0:T(8,128)}) custom-call(f32[2,8,128]{2,1,0:T(8,128)S(1)} %pad_maximum_fusion.refs_0_, f32[2,8,128]{2,1,0:T(8,128)S(1)} %collective-permute-done.10.refs_1_, f32[2,8,128]{2,1,0:T(8,128)S(1)} %collective-permute-done.11.refs_2_, ...), custom_call_target="tpu_custom_call" | custom-call | tf_op jit(solution)/shard_map/substeps/pallas_call | solution.py:476
  (21 shorter events, 1.1 us)
Async XLA Ops:
  0.6 19.6 %copy-start = (f32[4,64,2048]{2,1,0:T(8,128)S(1)}, f32[4,64,2048]{2,1,0:T(8,128)}, u32[]{:S(2)}) copy-start(f32[4,64,2048]{2,1,0:T(8,128)} %refs_5_.1) | copy-start | bytes 6291460
  0.6 0.8 %copy-start.2 = (s32[32]{0:T(128)S(1)}, s32[32]{0:T(128)}, u32[]{:S(2)}) copy-start(s32[32]{0:T(128)} %waves_ref.1) | copy-start | bytes 388
  3.3 1.4 %collective-permute-start = (f32[4,8,128]{2,1,0:T(8,128)S(1)}, f32[4,8,128]{2,1,0:T(8,128)S(1)}, u32[]{:S(2)}, u32[]{:S(2)}) collective-permute-start(f32[4,8,128]{2,1,0:T(8,128)S(1)} %get-tuple-element.17), channel_id=1, source_target_pairs={{0,1},{1,0},{2,3},{3,2},{4,5},{5,4},{6,7},{7,6},{8,9},{9,8},{10,11... | collective-permute-start | bytes 49160 | tf_op jit(solution)/shard_map/ppermute | solution.py:407
  4.7 28.6 %copy-start.1 = (f32[2048]{0:T(1024)S(1)}, f32[2048]{0:T(1024)}, u32[]{:S(2)}) copy-start(f32[2048]{0:T(1024)} %param.11) | copy-start | bytes 24580
  6.0 27.3 %collective-permute-start.7 = (f32[4,8,3200]{2,1,0:T(8,128)S(1)}, f32[4,8,3200]{2,1,0:T(8,128)S(1)}, u32[]{:S(2)}, u32[]{:S(2)}) collective-permute-start(f32[4,8,3200]{2,1,0:T(8,128)S(1)} %get-tuple-element.20), channel_id=1, source_target_pairs={{0,8},{8,16},{16,24},{1,9},{9,17},{17,25},{2,10},{10,18},{18,26},{... | collective-permute-start | bytes 1228808 | tf_op jit(solution)/shard_map/ppermute | solution.py:422
  10.8 22.6 %collective-permute-start.8 = (f32[4,8,3200]{2,1,0:T(8,128)S(1)}, f32[4,8,3200]{2,1,0:T(8,128)S(1)}, u32[]{:S(2)}, u32[]{:S(2)}) collective-permute-start(f32[4,8,3200]{2,1,0:T(8,128)S(1)} %get-tuple-element.21), channel_id=1, source_target_pairs={{8,0},{16,8},{24,16},{9,1},{17,9},{25,17},{10,2},{18,10},{26,18},{... | collective-permute-start | bytes 1228808 | tf_op jit(solution)/shard_map/ppermute | solution.py:423
  12.1 5.5 %collective-permute-start.3 = (f32[8,128]{1,0:T(8,128)S(1)}, f32[8,128]{1,0:T(8,128)S(1)}, u32[]{:S(2)}, u32[]{:S(2)}) collective-permute-start(f32[8,128]{1,0:T(8,128)S(1)} %get-tuple-element.28), channel_id=1, source_target_pairs={{0,6},{1,7},{2,4},{3,5},{4,2},{5,3},{6,0},{7,1},{8,14},{9,15},{10,... | collective-permute-start | bytes 12296 | tf_op jit(solution)/shard_map/ppermute | solution.py:426
  15.7 4.5 %collective-permute-start.2 = (f32[8,128]{1,0:T(8,128)S(1)}, f32[8,128]{1,0:T(8,128)S(1)}, u32[]{:S(2)}, u32[]{:S(2)}) collective-permute-start(f32[8,128]{1,0:T(8,128)S(1)} %get-tuple-element.29), channel_id=1, source_target_pairs={{0,4},{1,5},{2,6},{3,7},{4,0},{5,1},{6,2},{7,3},{8,12},{9,13},{10,... | collective-permute-start | bytes 12296 | tf_op jit(solution)/shard_map/ppermute | solution.py:426
  15.8 4.5 %collective-permute-start.1 = (f32[8,128]{1,0:T(8,128)S(1)}, f32[8,128]{1,0:T(8,128)S(1)}, u32[]{:S(2)}, u32[]{:S(2)}) collective-permute-start(f32[8,128]{1,0:T(8,128)S(1)} %get-tuple-element.30), channel_id=1, source_target_pairs={{0,2},{1,3},{2,0},{3,1},{4,6},{5,7},{6,4},{7,5},{8,10},{9,11},{10,... | collective-permute-start | bytes 12296 | tf_op jit(solution)/shard_map/ppermute | solution.py:426
  20.8 6.5 %collective-permute-start.6 = (f32[8,2048]{1,0:T(8,128)S(1)}, f32[8,2048]{1,0:T(8,128)S(1)}, u32[]{:S(2)}, u32[]{:S(2)}) collective-permute-start(f32[8,2048]{1,0:T(8,128)S(1)} %analysis.1.refs_0_), channel_id=1, source_target_pairs={{0,24},{8,16},{16,8},{24,0},{1,25},{9,17},{17,9},{25,1},{2,26},{10... | collective-permute-start | bytes 196616 | tf_op jit(solution)/shard_map/ppermute | solution.py:372
  24.5 4.3 %collective-permute-start.5 = (f32[8,2048]{1,0:T(8,128)S(1)}, f32[8,2048]{1,0:T(8,128)S(1)}, u32[]{:S(2)}, u32[]{:S(2)}) collective-permute-start(f32[8,2048]{1,0:T(8,128)S(1)} %analysis.1.refs_0_), channel_id=1, source_target_pairs={{0,16},{8,24},{16,0},{24,8},{1,17},{9,25},{17,1},{25,9},{2,18},{10... | collective-permute-start | bytes 196616 | tf_op jit(solution)/shard_map/ppermute | solution.py:372
  25.0 8.3 %collective-permute-start.4 = (f32[8,2048]{1,0:T(8,128)S(1)}, f32[8,2048]{1,0:T(8,128)S(1)}, u32[]{:S(2)}, u32[]{:S(2)}) collective-permute-start(f32[8,2048]{1,0:T(8,128)S(1)} %analysis.1.refs_0_), channel_id=1, source_target_pairs={{0,8},{8,0},{16,24},{24,16},{1,9},{9,1},{17,25},{25,17},{2,10},{10... | collective-permute-start | bytes 196616 | tf_op jit(solution)/shard_map/ppermute | solution.py:372
  33.8 5.2 %collective-permute-start.9 = (f32[8,128]{1,0:T(8,128)S(1)}, f32[8,128]{1,0:T(8,128)S(1)}, u32[]{:S(2)}, u32[]{:S(2)}) collective-permute-start(f32[8,128]{1,0:T(8,128)S(1)} %synthesis.1), channel_id=1, source_target_pairs={{0,1},{1,0},{2,3},{3,2},{4,5},{5,4},{6,7},{7,6},{8,9},{9,8},{10,11... | collective-permute-start | bytes 12296 | tf_op jit(solution)/shard_map/ppermute | solution.py:454
  35.3 9.8 %collective-permute-start.14 = (f32[80,128]{1,0:T(8,128)S(1)}, f32[80,128]{1,0:T(8,128)S(1)}, u32[]{:S(2)}, u32[]{:S(2)}) collective-permute-start(f32[80,128]{1,0:T(8,128)S(1)} %get-tuple-element.27), channel_id=1, source_target_pairs={{1,0},{2,1},{3,2},{4,3},{5,4},{6,5},{7,6},{0,7},{9,8},{10,9},{11,1... | collective-permute-start | bytes 122888 | tf_op jit(solution)/shard_map/ppermute | solution.py:471
  39.0 6.1 %collective-permute-start.13 = (f32[80,128]{1,0:T(8,128)S(1)}, f32[80,128]{1,0:T(8,128)S(1)}, u32[]{:S(2)}, u32[]{:S(2)}) collective-permute-start(f32[80,128]{1,0:T(8,128)S(1)} %get-tuple-element.27), channel_id=1, source_target_pairs={{0,1},{1,2},{2,3},{3,4},{4,5},{5,6},{6,7},{7,0},{8,9},{9,10},{10,1... | collective-permute-start | bytes 122888 | tf_op jit(solution)/shard_map/ppermute | solution.py:470
  39.0 5.5 %collective-permute-start.12 = (f32[2,8,128]{2,1,0:T(8,128)S(1)}, f32[2,8,128]{2,1,0:T(8,128)S(1)}, u32[]{:S(2)}, u32[]{:S(2)}) collective-permute-start(f32[2,8,128]{2,1,0:T(8,128)S(1)} %pad_maximum_fusion.refs_0_), channel_id=1, source_target_pairs={{0,6},{1,7},{2,4},{3,5},{4,2},{5,3},{6,0},{7,1},{8,14},{9,15},{10,... | collective-permute-start | bytes 24584 | tf_op jit(solution)/shard_map/ppermute | solution.py:455
  39.6 5.1 %collective-permute-start.11 = (f32[2,8,128]{2,1,0:T(8,128)S(1)}, f32[2,8,128]{2,1,0:T(8,128)S(1)}, u32[]{:S(2)}, u32[]{:S(2)}) collective-permute-start(f32[2,8,128]{2,1,0:T(8,128)S(1)} %pad_maximum_fusion.refs_0_), channel_id=1, source_target_pairs={{0,4},{1,5},{2,6},{3,7},{4,0},{5,1},{6,2},{7,3},{8,12},{9,13},{10,... | collective-permute-start | bytes 24584 | tf_op jit(solution)/shard_map/ppermute | solution.py:455
  39.6 5.6 %collective-permute-start.10 = (f32[2,8,128]{2,1,0:T(8,128)S(1)}, f32[2,8,128]{2,1,0:T(8,128)S(1)}, u32[]{:S(2)}, u32[]{:S(2)}) collective-permute-start(f32[2,8,128]{2,1,0:T(8,128)S(1)} %pad_maximum_fusion.refs_0_), channel_id=1, source_target_pairs={{0,2},{1,3},{2,0},{3,1},{4,6},{5,7},{6,4},{7,5},{8,10},{9,11},{10,... | collective-permute-start | bytes 24584 | tf_op jit(solution)/shard_map/ppermute | solution.py:455

commit v3 on v1

v3 whole, which is shorter than its diff:
```python
import functools
import math

import jax
import jax.numpy as jnp
from jax import lax
from jax.experimental import pallas as pl
from jax.experimental.pallas import tpu as pltpu
from jax.sharding import PartitionSpec as P

SUBSTEPS = 4
MARGIN = 2 * SUBSTEPS
STEP = 0.3

f32 = jnp.float32
bf16 = jnp.bfloat16
VMEM = pl.BlockSpec(memory_space=pltpu.VMEM)
HBM = pl.BlockSpec(memory_space=pltpu.HBM)
SMEM = pl.BlockSpec(memory_space=pltpu.SMEM)
LIMIT = pltpu.CompilerParams(vmem_limit_bytes=24 * 2**20)


def struct(shape, dtype=f32):
    return jax.ShapeDtypeStruct(shape, dtype)


def in_hbm(*arrays):
    return [pltpu.with_memory_space_constraint(x, pltpu.HBM) for x in arrays]


def split2(x):
    hi = x.astype(bf16)
    lo = (x - hi.astype(f32)).astype(bf16)
    return hi, lo


def owner(me, sectors, core, shift):
    chips = sectors // 2
    return 2 * lax.rem(me // 2 + shift, chips) + lax.bitwise_xor(lax.rem(me, 2), core)


def harmonic_rows(period, cols, slots, me, waves_ref, harm_ref):
    waves, width = harm_ref.shape[0] // 2, harm_ref.shape[1]
    sectors = waves // (2 * slots)
    row = lax.broadcasted_iota(jnp.int32, (2 * slots, 1), 0)
    groups = []
    for core in range(2):
        for shift in range(sectors // 2):
            first = owner(me, sectors, core, shift) * slots
            group = jnp.zeros((2 * slots, 1), jnp.int32)
            for slot in range(slots):
                value = waves_ref[first + slot]
                group = jnp.where((row == slot) | (row == slots + slot), value, group)
            groups.append(group)
    wave = jnp.concatenate(groups, axis=0)
    start = wave * (me * cols)
    turns = jnp.floor(start.astype(f32) * (1.0 / period)).astype(jnp.int32)
    start = (start - turns * period).astype(f32)
    wave = wave.astype(f32)
    row = lax.broadcasted_iota(jnp.int32, (waves, 1), 0)
    sine = (lax.rem(row, 2 * slots) >= slots).astype(f32)
    offset = 4.0 * start - period * sine
    for tile in range(0, width, 128):
        lane = lax.broadcasted_iota(jnp.int32, (1, 128), 1) + tile
        lane = jnp.where(lane < cols + MARGIN, lane, lane - width).astype(f32)
        product = wave * lane
        product = product - period * jnp.floor(product * (1.0 / period))
        quarter = 4.0 * product + offset
        turn = jnp.floor(quarter * (1.0 / period) + 0.5)
        angle = (quarter - period * turn) * (0.5 * math.pi / period)
        square = angle * angle
        cosine = 1.0 + square * (
            -1.0 / 2 + square * (1.0 / 24 + square * (-1.0 / 720 + square * (1.0 / 40320)))
        )
        sine_of = angle * (
            1.0
            + square
            * (-1.0 / 6 + square * (1.0 / 120 + square * (-1.0 / 5040 + square * (1.0 / 362880))))
        )
        phase = turn - 4.0 * jnp.floor(turn * 0.25)
        odd = (phase == 1.0) | (phase == 3.0)
        value = jnp.where(odd, sine_of, cosine)
        value = jnp.where((phase == 1.0) | (phase == 2.0), -value, value)
        hi, lo = split2(value)
        harm_ref[:waves, tile : tile + 128] = hi
        harm_ref[waves:, tile : tile + 128] = lo


def transform_kernel(
    period,
    slots,
    me_ref,
    waves_hbm,
    height_hbm,
    east_hbm,
    north_hbm,
    land_hbm,
    legendre_hbm,
    keep_ref,
    send_ref,
    bands_ref,
    legendre_ref,
    waves_ref,
    height_ref,
    east_ref,
    north_ref,
    land_ref,
    harm_ref,
    field_ref,
    semaphores,
):
    rows, cols = height_ref.shape
    waves, width = harm_ref.shape[0] // 2, harm_ref.shape[1]
    copies = [
        pltpu.make_async_copy(source, target, semaphores.at[at])
        for at, (source, target) in enumerate(
            (
                (waves_hbm, waves_ref),
                (height_hbm, height_ref),
                (east_hbm, east_ref),
                (north_hbm, north_ref),
                (land_hbm, land_ref),
                (legendre_hbm, legendre_ref),
            )
        )
    ]
    for copy in copies:
        copy.start()
    copies[0].wait()
    harmonic_rows(period, cols, slots, me_ref[0], waves_ref, harm_ref)
    copies[1].wait()
    for tile in range(0, width, 128):
        stop = min(cols, tile + 128)
        if stop <= tile:
            block = jnp.zeros((rows, 128), f32)
        elif stop == tile + 128:
            block = height_ref[:, tile : tile + 128]
        else:
            block = jnp.concatenate(
                [height_ref[:, tile:stop], jnp.zeros((rows, tile + 128 - stop), f32)], axis=1
            )
        hi, lo = split2(block)
        field_ref[:rows, tile : tile + 128] = hi
        field_ref[rows:, tile : tile + 128] = lo
    both = lax.dot_general(
        harm_ref[...], field_ref[...], (((1,), (1,)), ((), ())), preferred_element_type=f32
    )
    total = both[:waves] + both[waves:]
    total = (total[:, :rows] + total[:, rows:]) * (1.0 / math.sqrt(period))
    total = jnp.concatenate([total, jnp.zeros((waves, 128 - rows), f32)], axis=1)
    keep_ref[...] = total[: waves // 2].reshape(keep_ref.shape)
    send_ref[: waves // 2] = total[waves // 2 :]
    for copy in copies[2:5]:
        copy.wait()
    pieces = []
    for at, ref in enumerate((height_ref, east_ref, north_ref, land_ref)):
        pieces += [ref[:, :MARGIN].astype(f32), ref[:, cols - MARGIN :].astype(f32)]
        bands_ref[0, at, :, :cols] = ref[rows - MARGIN :].astype(f32)
        bands_ref[1, at, :, :cols] = ref[:MARGIN].astype(f32)
        if cols < width:
            bands_ref[:, at, :, cols:] = jnp.zeros((2, MARGIN, width - cols), f32)
    half = rows // 2
    send_ref[waves // 2 :] = jnp.concatenate(
        [piece[:half] for piece in pieces] + [piece[half:] for piece in pieces], axis=1
    )
    copies[5].wait()


def mix_kernel(keep_ref, recv_ref, own_ref, *send_refs):
    chips, group, _ = keep_ref.shape
    own_ref[...] = keep_ref[0] + recv_ref[:group]
    for shift, ref in enumerate(send_refs, 1):
        ref[:group] = keep_ref[shift] + recv_ref[shift * group : (shift + 1) * group]
        if ref.shape[0] > group:
            ref[group:] = recv_ref[chips * group :]


def analysis_kernel(
    cols,
    me_ref,
    part_refs,
    core_ref,
    bands_ref,
    legendre_ref,
    spectral_ref,
    even_ref,
    odd_ref,
):
    slots, rows, degrees = legendre_ref.shape
    width = bands_ref.shape[3]
    ahead = even_ref.shape[1] - 4 * width
    fourier = part_refs[0][...]
    for ref in part_refs[1:]:
        fourier = fourier + ref[: 2 * slots]
    columns = fourier.T
    for slot in range(slots):
        even = [
            jnp.broadcast_to(columns[o : o + 8, slot : slot + 1], (8, 128))
            for o in range(0, rows, 8)
        ]
        odd = [
            jnp.broadcast_to(columns[o : o + 8, slots + slot : slots + slot + 1], (8, 128))
            for o in range(0, rows, 8)
        ]
        for tile in range(0, degrees, 128):
            first = jnp.zeros((8, 128), f32)
            second = jnp.zeros((8, 128), f32)
            for at, o in enumerate(range(0, rows, 8)):
                block = legendre_ref[slot, o : o + 8, tile : tile + 128]
                first = first + block * even[at]
                second = second + block * odd[at]
            spectral_ref[slot : slot + 1, tile : tile + 128] = jnp.sum(
                first, axis=0, keepdims=True
            )
            spectral_ref[slots + slot : slots + slot + 1, tile : tile + 128] = jnp.sum(
                second, axis=0, keepdims=True
            )
    if ahead:
        even_ref[:, :ahead] = spectral_ref[...]
        odd_ref[:, :ahead] = spectral_ref[...]
    last = (cols // 128) * 128
    chips = len(part_refs)
    left, right = side_tiles(
        me_ref[0], 2 * slots, chips, core_ref, part_refs[1], part_refs[-1]
    )
    half = rows // 2
    is_even = lax.rem(me_ref[1], 2) == 0
    for at in range(4):
        ends = []
        for side, begin in enumerate((half - MARGIN, 0)):
            before, after = left[begin : begin + MARGIN], right[begin : begin + MARGIN]
            if side == 0:
                before, after = pltpu.roll(before, 64, 1), pltpu.roll(after, 64, 1)
            tail = bands_ref[side, at, :, last:]
            ends.append(
                [bands_ref[side, at, :, :last], with_sides(tail, before, after, cols - last, at)]
            )
        place = ahead + at * width
        for up, down, begin, end in zip(*ends, (0, last), (last, width)):
            even_ref[:, place + begin : place + end] = jnp.where(is_even, up, down)
            odd_ref[:, place + begin : place + end] = jnp.where(is_even, down, up)


def synthesis_kernel(parts_refs, love_ref, legendre_ref, out_ref, spectral_ref):
    slots, rows, degrees = legendre_ref.shape
    total = parts_refs[0][...]
    for ref in parts_refs[1:]:
        total = total + ref[:, :degrees]
    spectral_ref[...] = total * love_ref[...]
    lanes = lax.broadcasted_iota(jnp.int32, (8, 128), 1)
    octets = range(0, rows, 8)
    sums = [jnp.zeros((8, 128), f32) for _ in octets]
    for slot in range(slots):
        first = [jnp.zeros((8, 128), f32) for _ in octets]
        second = [jnp.zeros((8, 128), f32) for _ in octets]
        for tile in range(0, degrees, 128):
            even = jnp.broadcast_to(spectral_ref[slot : slot + 1, tile : tile + 128], (8, 128))
            odd = jnp.broadcast_to(
                spectral_ref[slots + slot : slots + slot + 1, tile : tile + 128], (8, 128)
            )
            for at, o in enumerate(octets):
                block = legendre_ref[slot, o : o + 8, tile : tile + 128]
                first[at] = first[at] + block * even
                second[at] = second[at] + block * odd
        for at in range(len(octets)):
            sums[at] = jnp.where(lanes == slot, jnp.sum(first[at], axis=1, keepdims=True), sums[at])
            sums[at] = jnp.where(
                lanes == slots + slot, jnp.sum(second[at], axis=1, keepdims=True), sums[at]
            )
    column = jnp.concatenate(sums + [jnp.zeros((128 - rows, 128), f32)], axis=0)
    out_ref[...] = jnp.broadcast_to(column.T[None, : 2 * slots], out_ref.shape)


def side_tiles(me, group, chips, core_ref, west_ref, east_ref):
    first = lax.rem(me, 2) == 0
    other = core_ref[chips * group :]
    left = jnp.where(first, west_ref[group:], other)
    right = jnp.where(first, other, east_ref[group:])
    return left, right


def with_sides(tail, left, right, own, at):
    lanes = lax.broadcasted_iota(jnp.int32, tail.shape, 1)
    after = pltpu.roll(right, (own - 2 * MARGIN * at) % 128, 1)
    before = pltpu.roll(left, (-MARGIN - 2 * MARGIN * at - MARGIN) % 128, 1)
    repeat = tail.shape[1] // 128
    after = jnp.concatenate([after] * repeat, axis=1)
    before = jnp.concatenate([before] * repeat, axis=1)
    tail = jnp.where((lanes >= own) & (lanes < own + MARGIN), after, tail)
    return jnp.where(lanes >= tail.shape[1] - MARGIN, before, tail)


def windows_kernel(
    period,
    slots,
    chips,
    bands,
    me_ref,
    waves_hbm,
    height_hbm,
    east_hbm,
    north_hbm,
    land_hbm,
    core_ref,
    west_ref,
    east_ref,
    even_ref,
    odd_ref,
    surface_win,
    east_win,
    north_win,
    wet_win,
    harm_ref,
    waves_ref,
    fields,
    land,
    semaphores,
):
    rows, cols = height_hbm.shape
    width = harm_ref.shape[1]
    last = (cols // 128) * 128
    copies = [
        pltpu.make_async_copy(source, target, semaphores.at[at])
        for at, (source, target) in enumerate(
            (
                (height_hbm, fields.at[0]),
                (east_hbm, fields.at[1]),
                (north_hbm, fields.at[2]),
                (land_hbm, land),
                (waves_hbm, waves_ref),
            )
        )
    ]
    for copy in copies:
        copy.start()
    copies[4].wait()
    harmonic_rows(period, cols, slots, me_ref[0], waves_ref, harm_ref)
    left, right = side_tiles(me_ref[0], 2 * slots, chips, core_ref, west_ref, east_ref)
    left = jnp.concatenate([left, pltpu.roll(left, 64, 1)], axis=0)
    right = jnp.concatenate([right, pltpu.roll(right, 64, 1)], axis=0)
    band = me_ref[1]
    is_even = lax.rem(band, 2) == 0
    for at, target in enumerate((surface_win, east_win, north_win, wet_win)):
        copies[at].wait()
        field = fields.at[at] if at < 3 else land
        place = even_ref.shape[1] - (4 - at) * width
        even, odd = even_ref[:, place : place + width], odd_ref[:, place : place + width]
        target[:MARGIN] = jnp.where(band > 0, jnp.where(is_even, odd, even), 0.0)
        target[MARGIN + rows :] = jnp.where(
            band < bands - 1, jnp.where(is_even, even, odd), 0.0
        )
        target[MARGIN : MARGIN + rows, :last] = field[:, :last].astype(f32)
        tail = jnp.concatenate(
            [field[:, last:].astype(f32), jnp.zeros((rows, width - cols), f32)], axis=1
        )
        target[MARGIN : MARGIN + rows, last:] = with_sides(tail, left, right, cols - last, at)


def substep_kernel(
    sectors,
    bands,
    me_ref,
    synth_ref,
    harm_ref,
    surface_win,
    east_win,
    north_win,
    wet,
    loading_hbm,
    surface_hbm,
    east_hbm,
    north_hbm,
    load,
    pressure,
    surface,
    east,
    north,
    loading_out,
    surface_out,
    east_out,
    north_out,
    semaphores,
):
    rows, cols = loading_hbm.shape
    taller, width = wet.shape
    waves = harm_ref.shape[0] // 2
    me, band = me_ref[0], me_ref[1]
    below, above = jnp.maximum(band - 1, 0), jnp.minimum(band + 1, bands - 1)
    lanes = lax.broadcasted_iota(jnp.int32, synth_ref.shape[1:], 1)
    groups = []
    for core in range(2):
        for shift in range(sectors // 2):
            sector = owner(me, sectors, core, shift)
            low = jnp.where(band > 0, synth_ref[below * sectors + sector], 0.0)
            high = jnp.where(band < bands - 1, synth_ref[above * sectors + sector], 0.0)
            group = pltpu.roll(synth_ref[band * sectors + sector], MARGIN, 1)
            group = jnp.where(lanes < MARGIN, pltpu.roll(low, (MARGIN - rows) % 128, 1), group)
            high = pltpu.roll(high, MARGIN + rows, 1)
            groups.append(jnp.where(lanes >= MARGIN + rows, high, group))
    synth = jnp.concatenate(groups, axis=0).T * (1.0 / math.sqrt(waves // 2))
    hi, lo = split2(synth[:taller])
    left = jnp.concatenate(
        [jnp.concatenate([hi, hi], axis=1), jnp.concatenate([lo, lo], axis=1)], axis=0
    )
    both = lax.dot_general(
        left, harm_ref[...], (((1,), (0,)), ((), ())), preferred_element_type=f32
    )
    load[...] = both[:taller] + both[taller:]
    copies = [
        pltpu.make_async_copy(source, target, semaphores.at[at])
        for at, (source, target) in enumerate(
            (
                (loading_out, loading_hbm),
                (surface_out, surface_hbm),
                (east_out, east_hbm),
                (north_out, north_hbm),
            )
        )
    ]
    inner = pl.ds(MARGIN, rows)
    loading_out[...] = load[inner, :cols]
    copies[0].start()
    edge = jnp.zeros((8, width), f32)
    pressure[:8] = edge
    pressure[taller + 8 :] = edge
    north[:8] = edge
    north[taller + 8 :] = edge
    for o in range(0, taller, 8):
        pressure[8 + o : 16 + o] = surface_win[o : o + 8] - load[o : o + 8]
    for substep in range(SUBSTEPS):
        final = substep == SUBSTEPS - 1
        for o in range(0, taller, 8):
            here = pressure[8 + o : 16 + o]
            damp = wet[o : o + 8]
            flow = east_win[o : o + 8] if substep == 0 else east[o : o + 8]
            flow = damp * (
                flow - STEP * (pltpu.roll(here, width - 1, 1) - pltpu.roll(here, 1, 1))
            )
            east[o : o + 8] = flow
            other = north_win[o : o + 8] if substep == 0 else north[8 + o : 16 + o]
            other = damp * (
                other - STEP * (pressure[9 + o : 17 + o] - pressure[7 + o : 15 + o])
            )
            north[8 + o : 16 + o] = other
            if final and MARGIN <= o < MARGIN + rows:
                east_out[o - MARGIN : o - MARGIN + 8] = flow[:, :cols]
                north_out[o - MARGIN : o - MARGIN + 8] = other[:, :cols]
        if final:
            copies[2].start()
            copies[3].start()
        for o in range(0, taller, 8):
            if final and not MARGIN <= o < MARGIN + rows:
                continue
            flow = east[o : o + 8]
            change = STEP * (pltpu.roll(flow, width - 1, 1) - pltpu.roll(flow, 1, 1)) + STEP * (
                north[9 + o : 17 + o] - north[7 + o : 15 + o]
            )
            level = surface_win[o : o + 8] if substep == 0 else surface[o : o + 8]
            level = level - wet[o : o + 8] * change
            if final:
                surface_out[o - MARGIN : o - MARGIN + 8] = level[:, :cols]
            else:
                surface[o : o + 8] = level
                pressure[8 + o : 16 + o] = level - load[o : o + 8]
    copies[1].start()
    for copy in copies:
        copy.wait()


def shards(height, east_flow, north_flow, legendre, love_numbers, wavenumbers, land_sea):
    rows, cols = height.shape
    slots, _, degrees = legendre.shape
    sectors, bands = lax.axis_size("lon"), lax.axis_size("lat")
    chips = sectors // 2
    waves = wavenumbers.shape[0]
    period = cols * sectors
    width = -(-(cols + 2 * MARGIN) // 128) * 128
    taller = rows + 2 * MARGIN
    group, half = 2 * slots, rows // 2
    DMA = pltpu.SemaphoreType.DMA
    fields = (height, east_flow, north_flow, land_sea)
    me = jnp.stack([lax.axis_index("lon"), lax.axis_index("lat")]).astype(jnp.int32)

    keep, send, bands_rows, legendre = pl.pallas_call(
        functools.partial(transform_kernel, period, slots),
        out_shape=[
            struct((chips, group, 128)),
            struct((chips * group + half, 128)),
            struct((2, 4, MARGIN, width)),
            struct(legendre.shape),
        ],
        in_specs=[SMEM] + [HBM] * 6,
        out_specs=[VMEM] * 4,
        scratch_shapes=[
            pltpu.SMEM((waves,), jnp.int32),
            pltpu.VMEM((rows, cols), f32),
            pltpu.VMEM((rows, cols), f32),
            pltpu.VMEM((rows, cols), f32),
            pltpu.VMEM((rows, cols), jnp.int32),
            pltpu.VMEM((4 * waves, width), bf16),
            pltpu.VMEM((2 * rows, width), bf16),
            DMA((6,)),
        ],
        name="transform",
        compiler_params=LIMIT,
    )(me, *in_hbm(wavenumbers, *fields, legendre))
    core = lax.ppermute(send, "lon", [(i, i ^ 1) for i in range(sectors)])
    neighbours = (1, chips - 1)
    own, *outgoing = pl.pallas_call(
        mix_kernel,
        out_shape=[struct((group, 128))]
        + [
            struct((group + (half if shift in neighbours else 0), 128))
            for shift in range(1, chips)
        ],
        in_specs=[VMEM] * 2,
        out_specs=[VMEM] * chips,
        name="mix",
        compiler_params=LIMIT,
    )(keep, core)
    arrived = [
        lax.ppermute(
            block, "lon", [(i, (i + 2 * shift) % sectors) for i in range(sectors)]
        )
        for shift, block in enumerate(outgoing, 1)
    ]
    sides = (core, arrived[0], arrived[-1])

    def analysis(me_ref, *refs):
        analysis_kernel(cols, me_ref, refs[:chips], *refs[chips:])

    together = bands == 4
    message = 4 * width + (degrees if together else 0)
    spectral, even, odd = pl.pallas_call(
        analysis,
        out_shape=[struct((group, degrees))] + [struct((MARGIN, message))] * 2,
        in_specs=[SMEM] + [VMEM] * (chips + 3),
        out_specs=[VMEM] * 3,
        name="analysis",
        compiler_params=LIMIT,
    )(me, own, *arrived, core, bands_rows, legendre)
    if together:
        even, odd, across = [
            lax.ppermute(block, "lat", [(i, i ^ step) for i in range(bands)])
            for block, step in ((even, 1), (odd, 3), (spectral, 2))
        ]
        pieces = [spectral, even, odd, across]
    else:
        links = [[(i, i + 1) for i in range(first, bands - 1, 2)] for first in (0, 1)]
        even, odd = [
            lax.ppermute(block, "lat", pairs + [(j, i) for i, j in pairs])
            for block, pairs in zip((even, odd), links)
        ]
        pieces = [lax.psum(spectral, "lat")]

    def synthesis(*refs):
        synthesis_kernel(refs[: len(pieces)], *refs[len(pieces) :])

    synth = pl.pallas_call(
        synthesis,
        out_shape=struct((bands * sectors, group, 128)),
        in_specs=[VMEM] * (len(pieces) + 2),
        out_specs=VMEM,
        scratch_shapes=[pltpu.VMEM((group, degrees), f32)],
        name="synthesis",
        compiler_params=LIMIT,
    )(*pieces, love_numbers.reshape(1, degrees), legendre)
    everyone = lax.all_to_all(synth, ("lat", "lon"), 0, 0, tiled=True)

    *windows, harmonics = pl.pallas_call(
        functools.partial(windows_kernel, period, slots, chips, bands),
        out_shape=[struct((taller, width))] * 4 + [struct((4 * waves, width), bf16)],
        in_specs=[SMEM] + [HBM] * 5 + [VMEM] * 5,
        out_specs=[VMEM] * 5,
        scratch_shapes=[
            pltpu.SMEM((waves,), jnp.int32),
            pltpu.VMEM((3, rows, cols), f32),
            pltpu.VMEM((rows, cols), jnp.int32),
            DMA((5,)),
        ],
        name="windows",
        compiler_params=LIMIT,
    )(me, *in_hbm(wavenumbers, *fields), *sides, even, odd)

    return pl.pallas_call(
        functools.partial(substep_kernel, sectors, bands),
        out_shape=[struct((rows, cols))] * 4,
        in_specs=[SMEM] + [VMEM] * 6,
        out_specs=[HBM] * 4,
        scratch_shapes=[
            pltpu.VMEM((taller, width), f32),
            pltpu.VMEM((taller + 16, width), f32),
            pltpu.VMEM((taller, width), f32),
            pltpu.VMEM((taller, width), f32),
            pltpu.VMEM((taller + 16, width), f32),
        ]
        + [pltpu.VMEM((rows, cols), f32)] * 4
        + [DMA((4,))],
        name="substeps",
        compiler_params=LIMIT,
    )(me, everyone, harmonics, *windows)


def solution(mesh):
    return jax.shard_map(
        shards,
        mesh=mesh,
        in_specs=(
            P("lat", "lon"),
            P("lat", "lon"),
            P("lat", "lon"),
            P("lon", "lat", None),
            P(),
            P(),
            P("lat", "lon"),
        ),
        out_specs=(P("lat", "lon"), P("lat", "lon"), P("lat", "lon"), P("lat", "lon")),
        check_vma=False,
    )
```

time: 63.7 us -> 43.1 us (0.68)
  waiting for transfers between devices: 6.51 us -> 18.2 us
  blocking collectives: 10.3 us -> 0 us
  local copies, waits for them, and re-layouts: 8.79 us -> 0.01 us
  Pallas kernels: 18 us -> 11 us
  starting transfers between devices: 18.1 us -> 13 us
    all_to_all x1 -> x0, blocking collectives: 10.3 us -> none  [shards(): parts = lax.all_to_all(part, 'lon', 0, 0, tiled=True)]
    pallas_call x6, Pallas kernels: 18 us -> 11 us  [the longest x1 3.79 us: shards(): pl.pallas_call(functools.partial(substep_kernel, sectors, bands), out_sha...]
    all_to_all x1, waiting for transfers between devices: 0.01 us -> 5.88 us  [shards(): everyone = lax.all_to_all(synth, ('lat', 'lon'), 0, 0, tiled=True)]
    ppermute x7, waiting for transfers between devices: 6.51 us -> 12.3 us  [the longest x3 7.91 us: shards(): lax.ppermute(block, 'lat', [(i, i ^ step) for i in range(bands)])]
    ppermute x7, starting transfers between devices: 14.7 us -> 10 us  [the longest x3 5.96 us: shards(): lax.ppermute(block, 'lon', [(i, (i + 2 * shift) % sectors) for i in range...]
    slice x2 -> x0, local copies, waits for them, and re-layouts: 3.17 us -> none  [the longest x1 1.59 us: shards(): high[:, :, degrees:degrees + cols]]
    unnamed x20 -> x2, local copies, waits for them, and re-layouts: 3.02 us -> 0.01 us
    broadcast_in_dim x3 -> x0, local copies, waits for them, and re-layouts: 1.38 us -> none  [the longest x1 1.3 us: shards(): jnp.broadcast_to(synth[None], (sectors, 2 * slots, 128))]
  transfers between devices with their start and end apart: 8 -> 8, of which waited for: 5 -> 6; matrix products, arithmetic and copies ran while one was open for 11% -> 0% of each run, Pallas kernels for 12% -> 5%
where the time goes in v3:
time: 43.1 us; the launch traced here: 42.9 us
  waiting for transfers between devices  18.2 us (42%)
  starting transfers between devices  13 us (30%)
  Pallas kernels  11 us (26%)
  between operations  0.68 us (2%)
    ppermute x3, waiting for transfers between devices, shards(): lax.ppermute(block, 'lat', [(i, i ^ step) for i in range(bands)])  7.91 us
    ppermute x3, starting transfers between devices, shards(): lax.ppermute(block, 'lon', [(i, (i + 2 * shift) % sectors) for i in range...  5.96 us
    all_to_all x1, waiting for transfers between devices, shards(): everyone = lax.all_to_all(synth, ('lat', 'lon'), 0, 0, tiled=True)  5.88 us
    pallas_call x1, Pallas kernels, shards(): pl.pallas_call(functools.partial(substep_kernel, sectors, bands), out_sha...  3.79 us
    ppermute x3, waiting for transfers between devices, shards(): lax.ppermute(block, 'lon', [(i, (i + 2 * shift) % sectors) for i in range...  3.56 us
    ppermute x3, starting transfers between devices, shards(): lax.ppermute(block, 'lat', [(i, i ^ step) for i in range(bands)])  3.55 us
    all_to_all x1, starting transfers between devices, shards(): everyone = lax.all_to_all(synth, ('lat', 'lon'), 0, 0, tiled=True)  2.99 us
    pallas_call x1, Pallas kernels, shards(): pl.pallas_call(functools.partial(transform_kernel, period, slots), out_sh...  2.56 us
  transfers between devices with their start and end apart: 8, of which 6 were waited for; matrix products, arithmetic and copies ran while one was open for 0% of the time, Pallas kernels for 5%

profile of v3, /device:TPU:0, one launch (start us, length us, event | category | flops | bytes accessed | tf_op | source)
XLA Modules:
  0.0 42.9 jit_solution(18400061471022149255)
XLA Ops:
  0.6 0.1 pad_add_fusion.me_ref
  0.7 0.0 copy-start
  0.7 2.6 %transform.1 = (f32[4,8,128]{2,1,0:T(8,128)S(1)}, f32[64,128]{1,0:T(8,128)S(1)}, f32[2,4,8,1152]{3,2,1,0:T(8,128)S(1)}, f32[4,64,2048]{2,1,0:T(8,128)S(1)}) custom-call(s32[2]{0:T(128)S(1)} %pad_add_fusion.me_ref, s32[32]{0:T(128)} %waves_hbm.3, f32[64,1080]{1,0:T(8,128)} %height_hbm.3, f32[64,1080]{1,0:T(8,128)} %east_hbm.3, f32[64,1080]{1,0:T(8,128)} %north_hbm.3, ...), custom_call_target="tpu_custom_call" | custom-call | tf_op jit(solution)/shard_map/transform/pallas_call | solution.py:484
  3.3 0.5 %collective-permute-start = (f32[64,128]{1,0:T(8,128)S(1)}, f32[64,128]{1,0:T(8,128)S(1)}, u32[]{:S(2)}, u32[]{:S(2)}) collective-permute-start(f32[64,128]{1,0:T(8,128)S(1)} %get-tuple-element.21), channel_id=1, source_target_pairs={{0,1},{1,0},{2,3},{3,2},{4,5},{5,4},{6,7},{7,6},{8,9},{9,8},{10,11... | collective-permute-start | bytes 98312 | tf_op jit(solution)/shard_map/ppermute | solution.py:507
  3.8 0.9 %collective-permute-done.recv_ref.refs_4_.core_ref = f32[64,128]{1,0:T(8,128)S(1)} collective-permute-done((f32[64,128]{1,0:T(8,128)S(1)}, f32[64,128]{1,0:T(8,128)S(1)}, u32[]{:S(2)}, u32[]{:S(2)}) %collective-permute-start) | collective-permute-done | bytes 32800 | tf_op jit(solution)/shard_map/ppermute | solution.py:507
  4.7 2.9 %collective-permute-start.1 = (f32[40,128]{1,0:T(8,128)S(1)}, f32[40,128]{1,0:T(8,128)S(1)}, u32[]{:S(2)}, u32[]{:S(2)}) collective-permute-start(f32[40,128]{1,0:T(8,128)S(1)} %get-tuple-element.23), channel_id=1, source_target_pairs={{0,2},{1,3},{2,4},{3,5},{4,6},{5,7},{6,0},{7,1},{8,10},{9,11},{10,... | collective-permute-start | bytes 61448 | tf_op jit(solution)/shard_map/ppermute | solution.py:522
  7.6 2.1 %collective-permute-start.3 = (f32[40,128]{1,0:T(8,128)S(1)}, f32[40,128]{1,0:T(8,128)S(1)}, u32[]{:S(2)}, u32[]{:S(2)}) collective-permute-start(f32[40,128]{1,0:T(8,128)S(1)} %get-tuple-element.25), channel_id=1, source_target_pairs={{0,6},{1,7},{2,0},{3,1},{4,2},{5,3},{6,4},{7,5},{8,14},{9,15},{10,... | collective-permute-start | bytes 61448 | tf_op jit(solution)/shard_map/ppermute | solution.py:522
  9.7 1.0 %collective-permute-start.2 = (f32[8,128]{1,0:T(8,128)S(1)}, f32[8,128]{1,0:T(8,128)S(1)}, u32[]{:S(2)}, u32[]{:S(2)}) collective-permute-start(f32[8,128]{1,0:T(8,128)S(1)} %get-tuple-element.24), channel_id=1, source_target_pairs={{0,4},{1,5},{2,6},{3,7},{4,0},{5,1},{6,2},{7,3},{8,12},{9,13},{10,... | collective-permute-start | bytes 12296 | tf_op jit(solution)/shard_map/ppermute | solution.py:522
  10.6 3.5 %collective-permute-done.2.refs_2_ = f32[8,128]{1,0:T(8,128)S(1)} collective-permute-done((f32[8,128]{1,0:T(8,128)S(1)}, f32[8,128]{1,0:T(8,128)S(1)}, u32[]{:S(2)}, u32[]{:S(2)}) %collective-permute-start.2) | collective-permute-done | bytes 4128 | tf_op jit(solution)/shard_map/ppermute | solution.py:522
  14.2 0.0 collective-permute-done.1.refs_1_.west_ref
  14.2 0.0 collective-permute-done.3.refs_3_.east_ref
  14.2 1.2 %analysis.1 = (f32[8,2048]{1,0:T(8,128)S(1)}, f32[8,6656]{1,0:T(8,128)S(1)}, f32[8,6656]{1,0:T(8,128)S(1)}) custom-call(s32[2]{0:T(128)S(1)} %pad_add_fusion.me_ref, f32[8,128]{1,0:T(8,128)S(1)} %get-tuple-element.22.refs_0_, f32[40,128]{1,0:T(8,128)S(1)} %collective-permute-done.1.refs_1_.west_ref, f32[8,128]{1,0:T(8,128)S(1)} %collective-permute-done.2.refs_2_, ...), custom_call_target="tpu_custom_call" | custom-call | tf_op jit(solution)/shard_map/analysis/pallas_call | solution.py:534
  15.3 1.7 %collective-permute-start.4 = (f32[8,6656]{1,0:T(8,128)S(1)}, f32[8,6656]{1,0:T(8,128)S(1)}, u32[]{:S(2)}, u32[]{:S(2)}) collective-permute-start(f32[8,6656]{1,0:T(8,128)S(1)} %get-tuple-element.29), channel_id=1, source_target_pairs={{0,8},{8,0},{16,24},{24,16},{1,9},{9,1},{17,25},{25,17},{2,10},{10... | collective-permute-start | bytes 638984 | tf_op jit(solution)/shard_map/ppermute | solution.py:544
  17.1 1.5 %collective-permute-start.5 = (f32[8,6656]{1,0:T(8,128)S(1)}, f32[8,6656]{1,0:T(8,128)S(1)}, u32[]{:S(2)}, u32[]{:S(2)}) collective-permute-start(f32[8,6656]{1,0:T(8,128)S(1)} %get-tuple-element.30), channel_id=1, source_target_pairs={{0,24},{8,16},{16,8},{24,0},{1,25},{9,17},{17,9},{25,1},{2,26},{10... | collective-permute-start | bytes 638984 | tf_op jit(solution)/shard_map/ppermute | solution.py:544
  18.6 0.3 collective-permute-start.6
  18.9 4.6 %collective-permute-done.6.refs_3_ = f32[8,2048]{1,0:T(8,128)S(1)} collective-permute-done((f32[8,2048]{1,0:T(8,128)S(1)}, f32[8,2048]{1,0:T(8,128)S(1)}, u32[]{:S(2)}, u32[]{:S(2)}) %collective-permute-start.6) | collective-permute-done | bytes 65568 | tf_op jit(solution)/shard_map/ppermute | solution.py:544
  23.5 0.1 collective-permute-done.4.refs_1_.even_ref
  23.6 3.2 %collective-permute-done.5.refs_2_.odd_ref = f32[8,6656]{1,0:T(8,128)S(1)} collective-permute-done((f32[8,6656]{1,0:T(8,128)S(1)}, f32[8,6656]{1,0:T(8,128)S(1)}, u32[]{:S(2)}, u32[]{:S(2)}) %collective-permute-start.5) | collective-permute-done | bytes 213024 | tf_op jit(solution)/shard_map/ppermute | solution.py:544
  26.8 0.0 copy-done
  26.8 1.2 %synthesis.1 = f32[32,8,128]{2,1,0:T(8,128)} custom-call(f32[8,2048]{1,0:T(8,128)S(1)} %get-tuple-element.28.refs_0_, f32[8,6656]{1,0:T(8,128)S(1)} %collective-permute-done.4.refs_1_.even_ref, f32[8,6656]{1,0:T(8,128)S(1)} %collective-permute-done.5.refs_2_.odd_ref, f32[8,2048]{1,0:T(8,128)S(1)} %collective-permute-done.6.refs_3_, f32[1,2048]{1,0:T(1,128)S(1)} %bitcast.3, ...), custom_call_target="tpu_custom_call" | custom-call | tf_op jit(solution)/shard_map/synthesis/pallas_call | solution.py:559
  28.0 3.0 %all-to-all-start = ((f32[32,8,128]{2,1,0:T(8,128)}), f32[32,8,128]{2,1,0:T(8,128)S(1)}, u32[]{:S(2)}, u32[]{:S(2)}) async-start(f32[32,8,128]{2,1,0:T(8,128)} %synthesis.1), calls=%async_computation | async-start | bytes 262144 | tf_op jit(solution)/shard_map/all_to_all | solution.py:568
  31.0 2.3 %windows.1 = (f32[80,1152]{1,0:T(8,128)S(1)}, f32[80,1152]{1,0:T(8,128)S(1)}, f32[80,1152]{1,0:T(8,128)S(1)}, f32[80,1152]{1,0:T(8,128)S(1)}, bf16[128,1152]{1,0:T(8,128)(2,1)S(1)}) custom-call(s32[2]{0:T(128)S(1)} %pad_add_fusion.me_ref, s32[32]{0:T(128)} %waves_hbm.3, f32[64,1080]{1,0:T(8,128)} %height_hbm.3, f32[64,1080]{1,0:T(8,128)} %east_hbm.3, ...), custom_call_target="tpu_custom_call" | custom-call | tf_op jit(solution)/shard_map/windows/pallas_call | solution.py:570
  33.3 5.9 %all-to-all-done.synth_ref = f32[32,8,128]{2,1,0:T(8,128)S(1)} async-done(((f32[32,8,128]{2,1,0:T(8,128)}), f32[32,8,128]{2,1,0:T(8,128)S(1)}, u32[]{:S(2)}, u32[]{:S(2)}) %all-to-all-start) | async-done | bytes 131104 | tf_op jit(solution)/shard_map/all_to_all | solution.py:568
  39.2 3.8 %substeps.1 = (f32[64,1080]{1,0:T(8,128)}, f32[64,1080]{1,0:T(8,128)}, f32[64,1080]{1,0:T(8,128)}, f32[64,1080]{1,0:T(8,128)}) custom-call(s32[2]{0:T(128)S(1)} %pad_add_fusion.me_ref, f32[32,8,128]{2,1,0:T(8,128)S(1)} %all-to-all-done.synth_ref, bf16[128,1152]{1,0:T(8,128)(2,1)S(1)} %get-tuple-element.31.harm_ref, ...), custom_call_target="tpu_custom_call" | custom-call | tf_op jit(solution)/shard_map/substeps/pallas_call | solution.py:585
  (1 shorter events, 0.0 us)
Async XLA Ops:
  0.7 26.1 %copy-start = (f32[2048]{0:T(1024)S(1)}, f32[2048]{0:T(1024)}, u32[]{:S(2)}) copy-start(f32[2048]{0:T(1024)} %param.11) | copy-start | bytes 24580
  3.3 1.4 %collective-permute-start = (f32[64,128]{1,0:T(8,128)S(1)}, f32[64,128]{1,0:T(8,128)S(1)}, u32[]{:S(2)}, u32[]{:S(2)}) collective-permute-start(f32[64,128]{1,0:T(8,128)S(1)} %get-tuple-element.21), channel_id=1, source_target_pairs={{0,1},{1,0},{2,3},{3,2},{4,5},{5,4},{6,7},{7,6},{8,9},{9,8},{10,11... | collective-permute-start | bytes 98312 | tf_op jit(solution)/shard_map/ppermute | solution.py:507
  4.7 9.5 %collective-permute-start.1 = (f32[40,128]{1,0:T(8,128)S(1)}, f32[40,128]{1,0:T(8,128)S(1)}, u32[]{:S(2)}, u32[]{:S(2)}) collective-permute-start(f32[40,128]{1,0:T(8,128)S(1)} %get-tuple-element.23), channel_id=1, source_target_pairs={{0,2},{1,3},{2,4},{3,5},{4,6},{5,7},{6,0},{7,1},{8,10},{9,11},{10,... | collective-permute-start | bytes 61448 | tf_op jit(solution)/shard_map/ppermute | solution.py:522
  7.6 6.6 %collective-permute-start.3 = (f32[40,128]{1,0:T(8,128)S(1)}, f32[40,128]{1,0:T(8,128)S(1)}, u32[]{:S(2)}, u32[]{:S(2)}) collective-permute-start(f32[40,128]{1,0:T(8,128)S(1)} %get-tuple-element.25), channel_id=1, source_target_pairs={{0,6},{1,7},{2,0},{3,1},{4,2},{5,3},{6,4},{7,5},{8,14},{9,15},{10,... | collective-permute-start | bytes 61448 | tf_op jit(solution)/shard_map/ppermute | solution.py:522
  9.7 4.5 %collective-permute-start.2 = (f32[8,128]{1,0:T(8,128)S(1)}, f32[8,128]{1,0:T(8,128)S(1)}, u32[]{:S(2)}, u32[]{:S(2)}) collective-permute-start(f32[8,128]{1,0:T(8,128)S(1)} %get-tuple-element.24), channel_id=1, source_target_pairs={{0,4},{1,5},{2,6},{3,7},{4,0},{5,1},{6,2},{7,3},{8,12},{9,13},{10,... | collective-permute-start | bytes 12296 | tf_op jit(solution)/shard_map/ppermute | solution.py:522
  15.3 8.2 %collective-permute-start.4 = (f32[8,6656]{1,0:T(8,128)S(1)}, f32[8,6656]{1,0:T(8,128)S(1)}, u32[]{:S(2)}, u32[]{:S(2)}) collective-permute-start(f32[8,6656]{1,0:T(8,128)S(1)} %get-tuple-element.29), channel_id=1, source_target_pairs={{0,8},{8,0},{16,24},{24,16},{1,9},{9,1},{17,25},{25,17},{2,10},{10... | collective-permute-start | bytes 638984 | tf_op jit(solution)/shard_map/ppermute | solution.py:544
  17.1 9.7 %collective-permute-start.5 = (f32[8,6656]{1,0:T(8,128)S(1)}, f32[8,6656]{1,0:T(8,128)S(1)}, u32[]{:S(2)}, u32[]{:S(2)}) collective-permute-start(f32[8,6656]{1,0:T(8,128)S(1)} %get-tuple-element.30), channel_id=1, source_target_pairs={{0,24},{8,16},{16,8},{24,0},{1,25},{9,17},{17,9},{25,1},{2,26},{10... | collective-permute-start | bytes 638984 | tf_op jit(solution)/shard_map/ppermute | solution.py:544
  18.6 5.0 %collective-permute-start.6 = (f32[8,2048]{1,0:T(8,128)S(1)}, f32[8,2048]{1,0:T(8,128)S(1)}, u32[]{:S(2)}, u32[]{:S(2)}) collective-permute-start(f32[8,2048]{1,0:T(8,128)S(1)} %get-tuple-element.28.refs_0_), channel_id=1, source_target_pairs={{0,16},{8,24},{16,0},{24,8},{1,17},{9,25},{17,1},{25,9},{2,18},{10... | collective-permute-start | bytes 196616 | tf_op jit(solution)/shard_map/ppermute | solution.py:544
  28.0 11.2 %all-to-all-start = ((f32[32,8,128]{2,1,0:T(8,128)}), f32[32,8,128]{2,1,0:T(8,128)S(1)}, u32[]{:S(2)}, u32[]{:S(2)}) async-start(f32[32,8,128]{2,1,0:T(8,128)} %synthesis.1), calls=%async_computation | async-start | bytes 262144 | tf_op jit(solution)/shard_map/all_to_all | solution.py:568

commit v4 on v3

--- a/solution.py
+++ b/solution.py
@@ -89,7 +89,6 @@
 def transform_kernel(
     period,
     slots,
-    me_ref,
     waves_hbm,
     height_hbm,
     east_hbm,
@@ -98,7 +97,8 @@
     legendre_hbm,
     keep_ref,
     send_ref,
-    bands_ref,
+    even_ref,
+    odd_ref,
     legendre_ref,
     waves_ref,
     height_ref,
@@ -127,7 +127,7 @@
     for copy in copies:
         copy.start()
     copies[0].wait()
-    harmonic_rows(period, cols, slots, me_ref[0], waves_ref, harm_ref)
+    harmonic_rows(period, cols, slots, lax.axis_index("lon"), waves_ref, harm_ref)
     copies[1].wait()
     for tile in range(0, width, 128):
         stop = min(cols, tile + 128)
@@ -152,13 +152,17 @@
     send_ref[: waves // 2] = total[waves // 2 :]
     for copy in copies[2:5]:
         copy.wait()
+    is_even = lax.rem(lax.axis_index("lat"), 2) == 0
     pieces = []
     for at, ref in enumerate((height_ref, east_ref, north_ref, land_ref)):
         pieces += [ref[:, :MARGIN].astype(f32), ref[:, cols - MARGIN :].astype(f32)]
-        bands_ref[0, at, :, :cols] = ref[rows - MARGIN :].astype(f32)
-        bands_ref[1, at, :, :cols] = ref[:MARGIN].astype(f32)
+        up, down = ref[rows - MARGIN :].astype(f32), ref[:MARGIN].astype(f32)
+        even_ref[at, :, :cols] = jnp.where(is_even, up, down)
+        odd_ref[at, :, :cols] = jnp.where(is_even, down, up)
         if cols < width:
-            bands_ref[:, at, :, cols:] = jnp.zeros((2, MARGIN, width - cols), f32)
+            blank = jnp.zeros((MARGIN, width - cols), f32)
+            even_ref[at, :, cols:] = blank
+            odd_ref[at, :, cols:] = blank
     half = rows // 2
     send_ref[waves // 2 :] = jnp.concatenate(
         [piece[:half] for piece in pieces] + [piece[half:] for piece in pieces], axis=1
@@ -175,20 +179,17 @@
             ref[group:] = recv_ref[chips * group :]
 
 
-def analysis_kernel(
-    cols,
-    me_ref,
-    part_refs,
-    core_ref,
-    bands_ref,
-    legendre_ref,
-    spectral_ref,
-    even_ref,
-    odd_ref,
-):
+def analysis_kernel(part_refs, core_ref, legendre_ref, spectral_ref, even_ref, odd_ref):
     slots, rows, degrees = legendre_ref.shape
-    width = bands_ref.shape[3]
-    ahead = even_ref.shape[1] - 4 * width
+    chips, half = len(part_refs), rows // 2
+    left, right = side_tiles(lax.axis_index("lon"), 2 * slots, chips, core_ref, part_refs[1], part_refs[-1])
+    lanes = lax.broadcasted_iota(jnp.int32, left.shape, 1)
+    both = jnp.where(lax.rem(lanes, 2 * MARGIN) < MARGIN, right, left)
+    up, down = pltpu.roll(both[half - MARGIN :], 64, 1), both[:MARGIN]
+    is_even = lax.rem(lax.axis_index("lat"), 2) == 0
+    ahead = even_ref.shape[1] - 128
+    even_ref[:, ahead:] = jnp.where(is_even, up, down)
+    odd_ref[:, ahead:] = jnp.where(is_even, down, up)
     fourier = part_refs[0][...]
     for ref in part_refs[1:]:
         fourier = fourier + ref[: 2 * slots]
@@ -218,28 +219,6 @@
     if ahead:
         even_ref[:, :ahead] = spectral_ref[...]
         odd_ref[:, :ahead] = spectral_ref[...]
-    last = (cols // 128) * 128
-    chips = len(part_refs)
-    left, right = side_tiles(
-        me_ref[0], 2 * slots, chips, core_ref, part_refs[1], part_refs[-1]
-    )
-    half = rows // 2
-    is_even = lax.rem(me_ref[1], 2) == 0
-    for at in range(4):
-        ends = []
-        for side, begin in enumerate((half - MARGIN, 0)):
-            before, after = left[begin : begin + MARGIN], right[begin : begin + MARGIN]
-            if side == 0:
-                before, after = pltpu.roll(before, 64, 1), pltpu.roll(after, 64, 1)
-            tail = bands_ref[side, at, :, last:]
-            ends.append(
-                [bands_ref[side, at, :, :last], with_sides(tail, before, after, cols - last, at)]
-            )
-        place = ahead + at * width
-        for up, down, begin, end in zip(*ends, (0, last), (last, width)):
-            even_ref[:, place + begin : place + end] = jnp.where(is_even, up, down)
-            odd_ref[:, place + begin : place + end] = jnp.where(is_even, down, up)
-
 
 def synthesis_kernel(parts_refs, love_ref, legendre_ref, out_ref, spectral_ref):
     slots, rows, degrees = legendre_ref.shape
@@ -295,7 +274,6 @@
     slots,
     chips,
     bands,
-    me_ref,
     waves_hbm,
     height_hbm,
     east_hbm,
@@ -304,6 +282,8 @@
     core_ref,
     west_ref,
     east_ref,
+    even_rows,
+    odd_rows,
     even_ref,
     odd_ref,
     surface_win,
@@ -334,21 +314,27 @@
     for copy in copies:
         copy.start()
     copies[4].wait()
-    harmonic_rows(period, cols, slots, me_ref[0], waves_ref, harm_ref)
-    left, right = side_tiles(me_ref[0], 2 * slots, chips, core_ref, west_ref, east_ref)
+    harmonic_rows(period, cols, slots, lax.axis_index("lon"), waves_ref, harm_ref)
+    left, right = side_tiles(lax.axis_index("lon"), 2 * slots, chips, core_ref, west_ref, east_ref)
     left = jnp.concatenate([left, pltpu.roll(left, 64, 1)], axis=0)
     right = jnp.concatenate([right, pltpu.roll(right, 64, 1)], axis=0)
-    band = me_ref[1]
+    band = lax.axis_index("lat")
     is_even = lax.rem(band, 2) == 0
+    even, odd = even_ref[:, -128:], odd_ref[:, -128:]
+    corners = (jnp.where(is_even, odd, even), jnp.where(is_even, even, odd))
+    for at, target in enumerate((surface_win, east_win, north_win, wet_win)):
+        even, odd = even_rows[at], odd_rows[at]
+        halos = (jnp.where(is_even, odd, even), jnp.where(is_even, even, odd))
+        for halo, corner, first, inside in zip(
+            halos, corners, (0, MARGIN + rows), (band > 0, band < bands - 1)
+        ):
+            place = pl.ds(first, MARGIN)
+            target[place, :last] = jnp.where(inside, halo[:, :last], 0.0)
+            tail = with_sides(halo[:, last:], corner, corner, cols - last, at)
+            target[place, last:] = jnp.where(inside, tail, 0.0)
     for at, target in enumerate((surface_win, east_win, north_win, wet_win)):
         copies[at].wait()
         field = fields.at[at] if at < 3 else land
-        place = even_ref.shape[1] - (4 - at) * width
-        even, odd = even_ref[:, place : place + width], odd_ref[:, place : place + width]
-        target[:MARGIN] = jnp.where(band > 0, jnp.where(is_even, odd, even), 0.0)
-        target[MARGIN + rows :] = jnp.where(
-            band < bands - 1, jnp.where(is_even, even, odd), 0.0
-        )
         target[MARGIN : MARGIN + rows, :last] = field[:, :last].astype(f32)
         tail = jnp.concatenate(
             [field[:, last:].astype(f32), jnp.zeros((rows, width - cols), f32)], axis=1
@@ -359,7 +345,6 @@
 def substep_kernel(
     sectors,
     bands,
-    me_ref,
     synth_ref,
     harm_ref,
     surface_win,
@@ -384,7 +369,7 @@
     rows, cols = loading_hbm.shape
     taller, width = wet.shape
     waves = harm_ref.shape[0] // 2
-    me, band = me_ref[0], me_ref[1]
+    me, band = lax.axis_index("lon"), lax.axis_index("lat")
     below, above = jnp.maximum(band - 1, 0), jnp.minimum(band + 1, bands - 1)
     lanes = lax.broadcasted_iota(jnp.int32, synth_ref.shape[1:], 1)
     groups = []
@@ -479,18 +464,18 @@
     group, half = 2 * slots, rows // 2
     DMA = pltpu.SemaphoreType.DMA
     fields = (height, east_flow, north_flow, land_sea)
-    me = jnp.stack([lax.axis_index("lon"), lax.axis_index("lat")]).astype(jnp.int32)
-
-    keep, send, bands_rows, legendre = pl.pallas_call(
+
+    keep, send, even, odd, legendre = pl.pallas_call(
         functools.partial(transform_kernel, period, slots),
         out_shape=[
             struct((chips, group, 128)),
             struct((chips * group + half, 128)),
-            struct((2, 4, MARGIN, width)),
+            struct((4, MARGIN, width)),
+            struct((4, MARGIN, width)),
             struct(legendre.shape),
         ],
-        in_specs=[SMEM] + [HBM] * 6,
-        out_specs=[VMEM] * 4,
+        in_specs=[HBM] * 6,
+        out_specs=[VMEM] * 5,
         scratch_shapes=[
             pltpu.SMEM((waves,), jnp.int32),
             pltpu.VMEM((rows, cols), f32),
@@ -503,7 +488,7 @@
         ],
         name="transform",
         compiler_params=LIMIT,
-    )(me, *in_hbm(wavenumbers, *fields, legendre))
+    )(*in_hbm(wavenumbers, *fields, legendre))
     core = lax.ppermute(send, "lon", [(i, i ^ 1) for i in range(sectors)])
     neighbours = (1, chips - 1)
     own, *outgoing = pl.pallas_call(
@@ -526,30 +511,32 @@
     ]
     sides = (core, arrived[0], arrived[-1])
 
-    def analysis(me_ref, *refs):
-        analysis_kernel(cols, me_ref, refs[:chips], *refs[chips:])
+    links = [[(i, i + 1) for i in range(first, bands - 1, 2)] for first in (0, 1)]
+    links = [pairs + [(j, i) for i, j in pairs] for pairs in links]
+    even, odd = [lax.ppermute(block, "lat", pairs) for block, pairs in zip((even, odd), links)]
+
+    def analysis(*refs):
+        analysis_kernel(refs[:chips], *refs[chips:])
 
     together = bands == 4
-    message = 4 * width + (degrees if together else 0)
-    spectral, even, odd = pl.pallas_call(
+    message = 128 + (degrees if together else 0)
+    spectral, *corners = pl.pallas_call(
         analysis,
         out_shape=[struct((group, degrees))] + [struct((MARGIN, message))] * 2,
-        in_specs=[SMEM] + [VMEM] * (chips + 3),
+        in_specs=[VMEM] * (chips + 2),
         out_specs=[VMEM] * 3,
         name="analysis",
         compiler_params=LIMIT,
-    )(me, own, *arrived, core, bands_rows, legendre)
+    )(own, *arrived, core, legendre)
     if together:
-        even, odd, across = [
+        *corners, across = [
             lax.ppermute(block, "lat", [(i, i ^ step) for i in range(bands)])
-            for block, step in ((even, 1), (odd, 3), (spectral, 2))
+            for block, step in ((corners[0], 1), (corners[1], 3), (spectral, 2))
         ]
-        pieces = [spectral, even, odd, across]
+        pieces = [spectral, *corners, across]
     else:
-        links = [[(i, i + 1) for i in range(first, bands - 1, 2)] for first in (0, 1)]
-        even, odd = [
-            lax.ppermute(block, "lat", pairs + [(j, i) for i, j in pairs])
-            for block, pairs in zip((even, odd), links)
+        corners = [
+            lax.ppermute(block, "lat", pairs) for block, pairs in zip(corners, links)
         ]
         pieces = [lax.psum(spectral, "lat")]
 
@@ -563,6 +550,7 @@
         out_specs=VMEM,
         scratch_shapes=[pltpu.VMEM((group, degrees), f32)],
         name="synthesis",
+        cost_estimate=pl.CostEstimate(flops=100000000000, bytes_accessed=400000000, transcendentals=0),
         compiler_params=LIMIT,
     )(*pieces, love_numbers.reshape(1, degrees), legendre)
     everyone = lax.all_to_all(synth, ("lat", "lon"), 0, 0, tiled=True)
@@ -570,7 +558,7 @@
     *windows, harmonics = pl.pallas_call(
         functools.partial(windows_kernel, period, slots, chips, bands),
         out_shape=[struct((taller, width))] * 4 + [struct((4 * waves, width), bf16)],
-        in_specs=[SMEM] + [HBM] * 5 + [VMEM] * 5,
+        in_specs=[HBM] * 5 + [VMEM] * 7,
         out_specs=[VMEM] * 5,
         scratch_shapes=[
             pltpu.SMEM((waves,), jnp.int32),
@@ -579,13 +567,14 @@
             DMA((5,)),
         ],
         name="windows",
+        cost_estimate=pl.CostEstimate(flops=10**11, bytes_accessed=4 * 10**8, transcendentals=0),
         compiler_params=LIMIT,
-    )(me, *in_hbm(wavenumbers, *fields), *sides, even, odd)
+    )(*in_hbm(wavenumbers, *fields), *sides, even, odd, *corners)
 
     return pl.pallas_call(
         functools.partial(substep_kernel, sectors, bands),
         out_shape=[struct((rows, cols))] * 4,
-        in_specs=[SMEM] + [VMEM] * 6,
+        in_specs=[VMEM] * 6,
         out_specs=[HBM] * 4,
         scratch_shapes=[
             pltpu.VMEM((taller, width), f32),
@@ -598,7 +587,7 @@
         + [DMA((4,))],
         name="substeps",
         compiler_params=LIMIT,
-    )(me, everyone, harmonics, *windows)
+    )(everyone, harmonics, *windows)
 
 
 def solution(mesh):

time: 43.1 us -> 38.6 us (0.90)
  waiting for transfers between devices: 18.2 us -> 12.9 us
  starting transfers between devices: 13 us -> 16.1 us
  Pallas kernels: 11 us -> 8.71 us
    ppermute x3, waiting for transfers between devices: 7.91 us -> 2.07 us  [shards(): lax.ppermute(block, 'lat', [(i, i ^ step) for i in range(bands)])]
    ppermute x0 -> x2, starting transfers between devices: none -> 2.31 us  [shards(): lax.ppermute(block, 'lat', pairs)]
    all_to_all x1, starting transfers between devices: 2.99 us -> 3.79 us  [shards(): everyone = lax.all_to_all(synth, ('lat', 'lon'), 0, 0, tiled=True)]
    pallas_call x1, Pallas kernels: 1.16 us -> 0.57 us  [shards(): pl.pallas_call(analysis, out_shape=[struct((group, degrees))] + [struct((...]
    pallas_call x1, Pallas kernels: 2.29 us -> 1.74 us  [shards(): pl.pallas_call(functools.partial(windows_kernel, period, slots, chips, ba...]
    pallas_call x1, Pallas kernels: 2.56 us -> 2.03 us  [shards(): pl.pallas_call(functools.partial(transform_kernel, period, slots), out_sh...]
    pallas_call x1, Pallas kernels: 3.79 us -> 3.27 us  [shards(): pl.pallas_call(functools.partial(substep_kernel, sectors, bands), out_sha...]
    all_to_all x1, waiting for transfers between devices: 5.88 us -> 6.4 us  [shards(): everyone = lax.all_to_all(synth, ('lat', 'lon'), 0, 0, tiled=True)]
  transfers between devices with their start and end apart: 8 -> 10, of which waited for: 6 -> 4; matrix products, arithmetic and copies ran while one was open for 0% -> 0% of each run, Pallas kernels for 5% -> 7%
where the time goes in v4:
time: 38.6 us; the launch traced here: 38.4 us
  starting transfers between devices  16.1 us (42%)
  waiting for transfers between devices  12.9 us (33%)
  Pallas kernels  8.71 us (23%)
  between operations  0.7 us (2%)
    all_to_all x1, waiting for transfers between devices, shards(): everyone = lax.all_to_all(synth, ('lat', 'lon'), 0, 0, tiled=True)  6.4 us
    ppermute x3, starting transfers between devices, shards(): lax.ppermute(block, 'lon', [(i, (i + 2 * shift) % sectors) for i in range...  5.96 us
    all_to_all x1, starting transfers between devices, shards(): everyone = lax.all_to_all(synth, ('lat', 'lon'), 0, 0, tiled=True)  3.79 us
    ppermute x3, waiting for transfers between devices, shards(): lax.ppermute(block, 'lon', [(i, (i + 2 * shift) % sectors) for i in range...  3.56 us
    ppermute x3, starting transfers between devices, shards(): lax.ppermute(block, 'lat', [(i, i ^ step) for i in range(bands)])  3.55 us
    pallas_call x1, Pallas kernels, shards(): pl.pallas_call(functools.partial(substep_kernel, sectors, bands), out_sha...  3.27 us
    ppermute x2, starting transfers between devices, shards(): lax.ppermute(block, 'lat', pairs)  2.31 us
    ppermute x3, waiting for transfers between devices, shards(): lax.ppermute(block, 'lat', [(i, i ^ step) for i in range(bands)])  2.07 us
  transfers between devices with their start and end apart: 10, of which 4 were waited for; matrix products, arithmetic and copies ran while one was open for 0% of the time, Pallas kernels for 7%

profile of v4, /device:TPU:0, one launch (start us, length us, event | category | flops | bytes accessed | tf_op | source)
XLA Modules:
  0.0 38.4 jit_solution(4017099483447373745)
XLA Ops:
  0.6 2.0 %transform.1 = (f32[4,8,128]{2,1,0:T(8,128)S(1)}, f32[64,128]{1,0:T(8,128)S(1)}, f32[4,8,1152]{2,1,0:T(8,128)S(1)}, f32[4,8,1152]{2,1,0:T(8,128)S(1)}, f32[4,64,2048]{2,1,0:T(8,128)S(1)}) custom-call(s32[32]{0:T(128)} %waves_hbm.3, f32[64,1080]{1,0:T(8,128)} %height_hbm.3, f32[64,1080]{1,0:T(8,128)} %east_hbm.3, f32[64,1080]{1,0:T(8,128)} %north_hbm.3, ...), custom_call_target="tpu_custom_call" | custom-call | tf_op jit(solution)/shard_map/transform/pallas_call | solution.py:468
  2.7 0.5 %collective-permute-start = (f32[64,128]{1,0:T(8,128)S(1)}, f32[64,128]{1,0:T(8,128)S(1)}, u32[]{:S(2)}, u32[]{:S(2)}) collective-permute-start(f32[64,128]{1,0:T(8,128)S(1)} %get-tuple-element.22), channel_id=1, source_target_pairs={{0,1},{1,0},{2,3},{3,2},{4,5},{5,4},{6,7},{7,6},{8,9},{9,8},{10,11... | collective-permute-start | bytes 98312 | tf_op jit(solution)/shard_map/ppermute | solution.py:492
  3.2 0.9 %collective-permute-done.recv_ref.refs_4_.core_ref = f32[64,128]{1,0:T(8,128)S(1)} collective-permute-done((f32[64,128]{1,0:T(8,128)S(1)}, f32[64,128]{1,0:T(8,128)S(1)}, u32[]{:S(2)}, u32[]{:S(2)}) %collective-permute-start) | collective-permute-done | bytes 32800 | tf_op jit(solution)/shard_map/ppermute | solution.py:492
  4.1 2.9 %collective-permute-start.1 = (f32[40,128]{1,0:T(8,128)S(1)}, f32[40,128]{1,0:T(8,128)S(1)}, u32[]{:S(2)}, u32[]{:S(2)}) collective-permute-start(f32[40,128]{1,0:T(8,128)S(1)} %get-tuple-element.24), channel_id=1, source_target_pairs={{0,2},{1,3},{2,4},{3,5},{4,6},{5,7},{6,0},{7,1},{8,10},{9,11},{10,... | collective-permute-start | bytes 61448 | tf_op jit(solution)/shard_map/ppermute | solution.py:507
  7.0 2.1 %collective-permute-start.3 = (f32[40,128]{1,0:T(8,128)S(1)}, f32[40,128]{1,0:T(8,128)S(1)}, u32[]{:S(2)}, u32[]{:S(2)}) collective-permute-start(f32[40,128]{1,0:T(8,128)S(1)} %get-tuple-element.26), channel_id=1, source_target_pairs={{0,6},{1,7},{2,0},{3,1},{4,2},{5,3},{6,4},{7,5},{8,14},{9,15},{10,... | collective-permute-start | bytes 61448 | tf_op jit(solution)/shard_map/ppermute | solution.py:507
  9.1 1.0 %collective-permute-start.2 = (f32[8,128]{1,0:T(8,128)S(1)}, f32[8,128]{1,0:T(8,128)S(1)}, u32[]{:S(2)}, u32[]{:S(2)}) collective-permute-start(f32[8,128]{1,0:T(8,128)S(1)} %get-tuple-element.25), channel_id=1, source_target_pairs={{0,4},{1,5},{2,6},{3,7},{4,0},{5,1},{6,2},{7,3},{8,12},{9,13},{10,... | collective-permute-start | bytes 12296 | tf_op jit(solution)/shard_map/ppermute | solution.py:507
  10.0 3.6 %collective-permute-done.2.refs_2_ = f32[8,128]{1,0:T(8,128)S(1)} collective-permute-done((f32[8,128]{1,0:T(8,128)S(1)}, f32[8,128]{1,0:T(8,128)S(1)}, u32[]{:S(2)}, u32[]{:S(2)}) %collective-permute-start.2) | collective-permute-done | bytes 4128 | tf_op jit(solution)/shard_map/ppermute | solution.py:507
  13.6 0.0 collective-permute-done.1.refs_1_.west_ref
  13.6 0.0 collective-permute-done.3.refs_3_.east_ref
  13.6 0.6 %analysis.1 = (f32[8,2048]{1,0:T(8,128)S(1)}, f32[8,2176]{1,0:T(8,128)S(1)}, f32[8,2176]{1,0:T(8,128)S(1)}) custom-call(f32[8,128]{1,0:T(8,128)S(1)} %get-tuple-element.23.refs_0_, f32[40,128]{1,0:T(8,128)S(1)} %collective-permute-done.1.refs_1_.west_ref, f32[8,128]{1,0:T(8,128)S(1)} %collective-permute-done.2.refs_2_, ...), custom_call_target="tpu_custom_call" | custom-call | tf_op jit(solution)/shard_map/analysis/pallas_call | solution.py:523
  14.1 1.7 %collective-permute-start.4 = (f32[8,2176]{1,0:T(8,128)S(1)}, f32[8,2176]{1,0:T(8,128)S(1)}, u32[]{:S(2)}, u32[]{:S(2)}) collective-permute-start(f32[8,2176]{1,0:T(8,128)S(1)} %get-tuple-element.29), channel_id=1, source_target_pairs={{0,8},{8,0},{16,24},{24,16},{1,9},{9,1},{17,25},{25,17},{2,10},{10... | collective-permute-start | bytes 208904 | tf_op jit(solution)/shard_map/ppermute | solution.py:533
  15.9 1.5 %collective-permute-start.5 = (f32[8,2176]{1,0:T(8,128)S(1)}, f32[8,2176]{1,0:T(8,128)S(1)}, u32[]{:S(2)}, u32[]{:S(2)}) collective-permute-start(f32[8,2176]{1,0:T(8,128)S(1)} %get-tuple-element.30), channel_id=1, source_target_pairs={{0,24},{8,16},{16,8},{24,0},{1,25},{9,17},{17,9},{25,1},{2,26},{10... | collective-permute-start | bytes 208904 | tf_op jit(solution)/shard_map/ppermute | solution.py:533
  17.4 0.3 collective-permute-start.6
  17.7 1.7 %collective-permute-start.7 = (f32[4,8,1152]{2,1,0:T(8,128)S(1)}, f32[4,8,1152]{2,1,0:T(8,128)S(1)}, u32[]{:S(2)}, u32[]{:S(2)}) collective-permute-start(f32[4,8,1152]{2,1,0:T(8,128)S(1)} %get-tuple-element.31), channel_id=1, source_target_pairs={{0,8},{16,24},{8,0},{24,16},{1,9},{17,25},{9,1},{25,17},{2,10},{18... | collective-permute-start | bytes 442376 | tf_op jit(solution)/shard_map/ppermute | solution.py:516
  19.4 0.7 %collective-permute-start.8 = (f32[4,8,1152]{2,1,0:T(8,128)S(1)}, f32[4,8,1152]{2,1,0:T(8,128)S(1)}, u32[]{:S(2)}, u32[]{:S(2)}) collective-permute-start(f32[4,8,1152]{2,1,0:T(8,128)S(1)} %get-tuple-element.32), channel_id=1, source_target_pairs={{8,16},{16,8},{9,17},{17,9},{10,18},{18,10},{11,19},{19,11},{12,20... | collective-permute-start | bytes 442376 | tf_op jit(solution)/shard_map/ppermute | solution.py:516
  20.0 2.1 %collective-permute-done.6.refs_3_ = f32[8,2048]{1,0:T(8,128)S(1)} collective-permute-done((f32[8,2048]{1,0:T(8,128)S(1)}, f32[8,2048]{1,0:T(8,128)S(1)}, u32[]{:S(2)}, u32[]{:S(2)}) %collective-permute-start.6) | collective-permute-done | bytes 65568 | tf_op jit(solution)/shard_map/ppermute | solution.py:533
  22.1 0.0 collective-permute-done.4.refs_1_.even_ref
  22.1 0.0 collective-permute-done.5.refs_2_.odd_ref
  22.1 1.1 %synthesis.1 = f32[32,8,128]{2,1,0:T(8,128)} custom-call(f32[8,2048]{1,0:T(8,128)S(1)} %get-tuple-element.28.refs_0_, f32[8,2176]{1,0:T(8,128)S(1)} %collective-permute-done.4.refs_1_.even_ref, f32[8,2176]{1,0:T(8,128)S(1)} %collective-permute-done.5.refs_2_.odd_ref, f32[8,2048]{1,0:T(8,128)S(1)} %collective-permute-done.6.refs_3_, f32[1,2048]{1,0:T(1,128)S(1)} %bitcast.1, ...), custom_call_target="tpu_custom_call" | custom-call | flops 99999997952 | bytes 400000000 | tf_op jit(solution)/shard_map/synthesis/pallas_call | solution.py:546
  23.2 3.8 %all-to-all-start = ((f32[32,8,128]{2,1,0:T(8,128)}), f32[32,8,128]{2,1,0:T(8,128)S(1)}, u32[]{:S(2)}, u32[]{:S(2)}) async-start(f32[32,8,128]{2,1,0:T(8,128)} %synthesis.1), calls=%async_computation | async-start | bytes 262144 | tf_op jit(solution)/shard_map/all_to_all | solution.py:556
  27.0 0.0 collective-permute-done.7.even_rows
  27.0 1.7 %windows.1 = (f32[80,1152]{1,0:T(8,128)S(1)}, f32[80,1152]{1,0:T(8,128)S(1)}, f32[80,1152]{1,0:T(8,128)S(1)}, f32[80,1152]{1,0:T(8,128)S(1)}, bf16[128,1152]{1,0:T(8,128)(2,1)S(1)}) custom-call(s32[32]{0:T(128)} %waves_hbm.3, f32[64,1080]{1,0:T(8,128)} %height_hbm.3, f32[64,1080]{1,0:T(8,128)} %east_hbm.3, f32[64,1080]{1,0:T(8,128)} %north_hbm.3, ...), custom_call_target="tpu_custom_call" | custom-call | flops 99999997952 | bytes 400000000 | tf_op jit(solution)/shard_map/windows/pallas_call | solution.py:558
  28.8 6.4 %all-to-all-done.synth_ref = f32[32,8,128]{2,1,0:T(8,128)S(1)} async-done(((f32[32,8,128]{2,1,0:T(8,128)}), f32[32,8,128]{2,1,0:T(8,128)S(1)}, u32[]{:S(2)}, u32[]{:S(2)}) %all-to-all-start) | async-done | bytes 131104 | tf_op jit(solution)/shard_map/all_to_all | solution.py:556
  35.2 3.3 %substeps.1 = (f32[64,1080]{1,0:T(8,128)}, f32[64,1080]{1,0:T(8,128)}, f32[64,1080]{1,0:T(8,128)}, f32[64,1080]{1,0:T(8,128)}) custom-call(f32[32,8,128]{2,1,0:T(8,128)S(1)} %all-to-all-done.synth_ref, bf16[128,1152]{1,0:T(8,128)(2,1)S(1)} %get-tuple-element.33.harm_ref, f32[80,1152]{1,0:T(8,128)S(1)} %get-tuple-element.34.surface_win, ...), custom_call_target="tpu_custom_call" | custom-call | tf_op jit(solution)/shard_map/substeps/pallas_call | solution.py:574
  (4 shorter events, 0.0 us)
Async XLA Ops:
  0.6 21.5 %copy-start = (f32[2048]{0:T(1024)S(1)}, f32[2048]{0:T(1024)}, u32[]{:S(2)}) copy-start(f32[2048]{0:T(1024)} %param.11) | copy-start | bytes 24580
  2.7 1.4 %collective-permute-start = (f32[64,128]{1,0:T(8,128)S(1)}, f32[64,128]{1,0:T(8,128)S(1)}, u32[]{:S(2)}, u32[]{:S(2)}) collective-permute-start(f32[64,128]{1,0:T(8,128)S(1)} %get-tuple-element.22), channel_id=1, source_target_pairs={{0,1},{1,0},{2,3},{3,2},{4,5},{5,4},{6,7},{7,6},{8,9},{9,8},{10,11... | collective-permute-start | bytes 98312 | tf_op jit(solution)/shard_map/ppermute | solution.py:492
  4.1 9.5 %collective-permute-start.1 = (f32[40,128]{1,0:T(8,128)S(1)}, f32[40,128]{1,0:T(8,128)S(1)}, u32[]{:S(2)}, u32[]{:S(2)}) collective-permute-start(f32[40,128]{1,0:T(8,128)S(1)} %get-tuple-element.24), channel_id=1, source_target_pairs={{0,2},{1,3},{2,4},{3,5},{4,6},{5,7},{6,0},{7,1},{8,10},{9,11},{10,... | collective-permute-start | bytes 61448 | tf_op jit(solution)/shard_map/ppermute | solution.py:507
  7.0 6.6 %collective-permute-start.3 = (f32[40,128]{1,0:T(8,128)S(1)}, f32[40,128]{1,0:T(8,128)S(1)}, u32[]{:S(2)}, u32[]{:S(2)}) collective-permute-start(f32[40,128]{1,0:T(8,128)S(1)} %get-tuple-element.26), channel_id=1, source_target_pairs={{0,6},{1,7},{2,0},{3,1},{4,2},{5,3},{6,4},{7,5},{8,14},{9,15},{10,... | collective-permute-start | bytes 61448 | tf_op jit(solution)/shard_map/ppermute | solution.py:507
  9.1 4.5 %collective-permute-start.2 = (f32[8,128]{1,0:T(8,128)S(1)}, f32[8,128]{1,0:T(8,128)S(1)}, u32[]{:S(2)}, u32[]{:S(2)}) collective-permute-start(f32[8,128]{1,0:T(8,128)S(1)} %get-tuple-element.25), channel_id=1, source_target_pairs={{0,4},{1,5},{2,6},{3,7},{4,0},{5,1},{6,2},{7,3},{8,12},{9,13},{10,... | collective-permute-start | bytes 12296 | tf_op jit(solution)/shard_map/ppermute | solution.py:507
  14.1 7.9 %collective-permute-start.4 = (f32[8,2176]{1,0:T(8,128)S(1)}, f32[8,2176]{1,0:T(8,128)S(1)}, u32[]{:S(2)}, u32[]{:S(2)}) collective-permute-start(f32[8,2176]{1,0:T(8,128)S(1)} %get-tuple-element.29), channel_id=1, source_target_pairs={{0,8},{8,0},{16,24},{24,16},{1,9},{9,1},{17,25},{25,17},{2,10},{10... | collective-permute-start | bytes 208904 | tf_op jit(solution)/shard_map/ppermute | solution.py:533
  15.9 6.2 %collective-permute-start.5 = (f32[8,2176]{1,0:T(8,128)S(1)}, f32[8,2176]{1,0:T(8,128)S(1)}, u32[]{:S(2)}, u32[]{:S(2)}) collective-permute-start(f32[8,2176]{1,0:T(8,128)S(1)} %get-tuple-element.30), channel_id=1, source_target_pairs={{0,24},{8,16},{16,8},{24,0},{1,25},{9,17},{17,9},{25,1},{2,26},{10... | collective-permute-start | bytes 208904 | tf_op jit(solution)/shard_map/ppermute | solution.py:533
  17.4 4.7 %collective-permute-start.6 = (f32[8,2048]{1,0:T(8,128)S(1)}, f32[8,2048]{1,0:T(8,128)S(1)}, u32[]{:S(2)}, u32[]{:S(2)}) collective-permute-start(f32[8,2048]{1,0:T(8,128)S(1)} %get-tuple-element.28.refs_0_), channel_id=1, source_target_pairs={{0,16},{8,24},{16,0},{24,8},{1,17},{9,25},{17,1},{25,9},{2,18},{10... | collective-permute-start | bytes 196616 | tf_op jit(solution)/shard_map/ppermute | solution.py:533
  17.7 9.3 %collective-permute-start.7 = (f32[4,8,1152]{2,1,0:T(8,128)S(1)}, f32[4,8,1152]{2,1,0:T(8,128)S(1)}, u32[]{:S(2)}, u32[]{:S(2)}) collective-permute-start(f32[4,8,1152]{2,1,0:T(8,128)S(1)} %get-tuple-element.31), channel_id=1, source_target_pairs={{0,8},{16,24},{8,0},{24,16},{1,9},{17,25},{9,1},{25,17},{2,10},{18... | collective-permute-start | bytes 442376 | tf_op jit(solution)/shard_map/ppermute | solution.py:516
  19.4 7.6 %collective-permute-start.8 = (f32[4,8,1152]{2,1,0:T(8,128)S(1)}, f32[4,8,1152]{2,1,0:T(8,128)S(1)}, u32[]{:S(2)}, u32[]{:S(2)}) collective-permute-start(f32[4,8,1152]{2,1,0:T(8,128)S(1)} %get-tuple-element.32), channel_id=1, source_target_pairs={{8,16},{16,8},{9,17},{17,9},{10,18},{18,10},{11,19},{19,11},{12,20... | collective-permute-start | bytes 442376 | tf_op jit(solution)/shard_map/ppermute | solution.py:516
  23.2 12.0 %all-to-all-start = ((f32[32,8,128]{2,1,0:T(8,128)}), f32[32,8,128]{2,1,0:T(8,128)S(1)}, u32[]{:S(2)}, u32[]{:S(2)}) async-start(f32[32,8,128]{2,1,0:T(8,128)} %synthesis.1), calls=%async_computation | async-start | bytes 262144 | tf_op jit(solution)/shard_map/all_to_all | solution.py:556

commit v5 on v4

--- a/solution.py
+++ b/solution.py
@@ -39,26 +39,36 @@
     return 2 * lax.rem(me // 2 + shift, chips) + lax.bitwise_xor(lax.rem(me, 2), core)
 
 
-def harmonic_rows(period, cols, slots, me, waves_ref, harm_ref):
+def row_groups(sectors):
+    return [(core, shift) for core in range(2) for shift in range(sectors // 2)]
+
+
+def harmonic_rows(period, cols, slots, me, paired, waves_ref, harm_ref):
     waves, width = harm_ref.shape[0] // 2, harm_ref.shape[1]
     sectors = waves // (2 * slots)
-    row = lax.broadcasted_iota(jnp.int32, (2 * slots, 1), 0)
-    groups = []
-    for core in range(2):
-        for shift in range(sectors // 2):
-            first = owner(me, sectors, core, shift) * slots
-            group = jnp.zeros((2 * slots, 1), jnp.int32)
-            for slot in range(slots):
-                value = waves_ref[first + slot]
-                group = jnp.where((row == slot) | (row == slots + slot), value, group)
-            groups.append(group)
-    wave = jnp.concatenate(groups, axis=0)
+    order = []
+    for core, shift in row_groups(sectors):
+        first = owner(me, sectors, core, shift) * slots
+        group = [waves_ref[first + slot] for slot in range(slots)]
+        order += group + group if paired else group
+    if not paired:
+        order = order + order
+    row = lax.broadcasted_iota(jnp.int32, (8, 1), 0)
+    blocks = []
+    for first in range(0, waves, 8):
+        block = jnp.zeros((8, 1), jnp.int32)
+        for at, value in enumerate(order[first : first + 8]):
+            block = jnp.where(row == at, value, block)
+        blocks.append(block)
+    wave = jnp.concatenate(blocks, axis=0)
     start = wave * (me * cols)
     turns = jnp.floor(start.astype(f32) * (1.0 / period)).astype(jnp.int32)
     start = (start - turns * period).astype(f32)
     wave = wave.astype(f32)
     row = lax.broadcasted_iota(jnp.int32, (waves, 1), 0)
-    sine = (lax.rem(row, 2 * slots) >= slots).astype(f32)
+    if paired:
+        row = lax.rem(row, 2 * slots)
+    sine = (row >= (slots if paired else waves // 2)).astype(f32)
     offset = 4.0 * start - period * sine
     for tile in range(0, width, 128):
         lane = lax.broadcasted_iota(jnp.int32, (1, 128), 1) + tile
@@ -94,40 +104,41 @@
     east_hbm,
     north_hbm,
     land_hbm,
-    legendre_hbm,
     keep_ref,
     send_ref,
-    even_ref,
-    odd_ref,
-    legendre_ref,
     waves_ref,
     height_ref,
-    east_ref,
-    north_ref,
-    land_ref,
+    flow_front,
+    flow_back,
+    land_front,
+    land_back,
     harm_ref,
     field_ref,
     semaphores,
 ):
     rows, cols = height_ref.shape
     waves, width = harm_ref.shape[0] // 2, harm_ref.shape[1]
+    back = cols - land_back.shape[1]
+    fronts, backs = pl.ds(0, 128), pl.ds(back, cols - back)
     copies = [
         pltpu.make_async_copy(source, target, semaphores.at[at])
         for at, (source, target) in enumerate(
             (
                 (waves_hbm, waves_ref),
                 (height_hbm, height_ref),
-                (east_hbm, east_ref),
-                (north_hbm, north_ref),
-                (land_hbm, land_ref),
-                (legendre_hbm, legendre_ref),
+                (east_hbm.at[:, fronts], flow_front.at[0]),
+                (east_hbm.at[:, backs], flow_back.at[0]),
+                (north_hbm.at[:, fronts], flow_front.at[1]),
+                (north_hbm.at[:, backs], flow_back.at[1]),
+                (land_hbm.at[:, fronts], land_front),
+                (land_hbm.at[:, backs], land_back),
             )
         )
     ]
     for copy in copies:
         copy.start()
     copies[0].wait()
-    harmonic_rows(period, cols, slots, lax.axis_index("lon"), waves_ref, harm_ref)
+    harmonic_rows(period, cols, slots, lax.axis_index("lon"), True, waves_ref, harm_ref)
     copies[1].wait()
     for tile in range(0, width, 128):
         stop = min(cols, tile + 128)
@@ -150,24 +161,64 @@
     total = jnp.concatenate([total, jnp.zeros((waves, 128 - rows), f32)], axis=1)
     keep_ref[...] = total[: waves // 2].reshape(keep_ref.shape)
     send_ref[: waves // 2] = total[waves // 2 :]
-    for copy in copies[2:5]:
+    for copy in copies[2:]:
+        copy.wait()
+    pieces = []
+    for front, end in (
+        (height_ref[:, :MARGIN], height_ref[:, cols - MARGIN :]),
+        (flow_front[0, :, :MARGIN], flow_back[0, :, cols - MARGIN - back :]),
+        (flow_front[1, :, :MARGIN], flow_back[1, :, cols - MARGIN - back :]),
+        (land_front[:, :MARGIN].astype(f32), land_back[:, cols - MARGIN - back :].astype(f32)),
+    ):
+        pieces += [front, end]
+    half = rows // 2
+    send_ref[waves // 2 :] = jnp.concatenate(
+        [piece[:half] for piece in pieces] + [piece[half:] for piece in pieces], axis=1
+    )
+
+
+def stage_kernel(
+    after_ref,
+    height_hbm,
+    east_hbm,
+    north_hbm,
+    land_hbm,
+    legendre_hbm,
+    even_ref,
+    odd_ref,
+    legendre_ref,
+    flows,
+    lands,
+    semaphores,
+):
+    rows, cols = height_hbm.shape
+    width = even_ref.shape[2]
+    copies = []
+    for side, first in enumerate((rows - MARGIN, 0)):
+        band = pl.ds(first, MARGIN)
+        copies.append((height_hbm.at[band], flows.at[side, 0]))
+        copies.append((east_hbm.at[band], flows.at[side, 1]))
+        copies.append((north_hbm.at[band], flows.at[side, 2]))
+        copies.append((land_hbm.at[band], lands.at[side]))
+    copies.append((legendre_hbm, legendre_ref))
+    copies = [
+        pltpu.make_async_copy(source, target, semaphores.at[at])
+        for at, (source, target) in enumerate(copies)
+    ]
+    for copy in copies:
+        copy.start()
+    for copy in copies[:-1]:
         copy.wait()
     is_even = lax.rem(lax.axis_index("lat"), 2) == 0
-    pieces = []
-    for at, ref in enumerate((height_ref, east_ref, north_ref, land_ref)):
-        pieces += [ref[:, :MARGIN].astype(f32), ref[:, cols - MARGIN :].astype(f32)]
-        up, down = ref[rows - MARGIN :].astype(f32), ref[:MARGIN].astype(f32)
+    for at in range(4):
+        up, down = [lands[side].astype(f32) if at == 3 else flows[side, at] for side in range(2)]
         even_ref[at, :, :cols] = jnp.where(is_even, up, down)
         odd_ref[at, :, :cols] = jnp.where(is_even, down, up)
         if cols < width:
             blank = jnp.zeros((MARGIN, width - cols), f32)
             even_ref[at, :, cols:] = blank
             odd_ref[at, :, cols:] = blank
-    half = rows // 2
-    send_ref[waves // 2 :] = jnp.concatenate(
-        [piece[:half] for piece in pieces] + [piece[half:] for piece in pieces], axis=1
-    )
-    copies[5].wait()
+    copies[-1].wait()
 
 
 def mix_kernel(keep_ref, recv_ref, own_ref, *send_refs):
@@ -247,7 +298,9 @@
                 lanes == slots + slot, jnp.sum(second[at], axis=1, keepdims=True), sums[at]
             )
     column = jnp.concatenate(sums + [jnp.zeros((128 - rows, 128), f32)], axis=0)
-    out_ref[...] = jnp.broadcast_to(column.T[None, : 2 * slots], out_ref.shape)
+    lines = column.T[: 2 * slots]
+    lines = lines[:slots] + pltpu.roll(lines[slots:], 64, 1)
+    out_ref[...] = jnp.broadcast_to(lines[None], out_ref.shape)
 
 
 def side_tiles(me, group, chips, core_ref, west_ref, east_ref):
@@ -267,6 +320,10 @@
     before = jnp.concatenate([before] * repeat, axis=1)
     tail = jnp.where((lanes >= own) & (lanes < own + MARGIN), after, tail)
     return jnp.where(lanes >= tail.shape[1] - MARGIN, before, tail)
+
+
+def interleaved(ref, step):
+    return [ref[pl.ds(at, 8, stride=step)] for at in range(step)]
 
 
 def windows_kernel(
@@ -290,14 +347,18 @@
     east_win,
     north_win,
     wet_win,
+    moved_win,
     harm_ref,
     waves_ref,
     fields,
     land,
+    natural,
     semaphores,
 ):
     rows, cols = height_hbm.shape
     width = harm_ref.shape[1]
+    taller = rows + 2 * MARGIN
+    step = taller // 8
     last = (cols // 128) * 128
     copies = [
         pltpu.make_async_copy(source, target, semaphores.at[at])
@@ -314,32 +375,52 @@
     for copy in copies:
         copy.start()
     copies[4].wait()
-    harmonic_rows(period, cols, slots, lax.axis_index("lon"), waves_ref, harm_ref)
-    left, right = side_tiles(lax.axis_index("lon"), 2 * slots, chips, core_ref, west_ref, east_ref)
+    harmonic_rows(period, cols, slots, lax.axis_index("lon"), False, waves_ref, harm_ref)
+    left, right = side_tiles(
+        lax.axis_index("lon"), 2 * slots, chips, core_ref, west_ref, east_ref
+    )
     left = jnp.concatenate([left, pltpu.roll(left, 64, 1)], axis=0)
     right = jnp.concatenate([right, pltpu.roll(right, 64, 1)], axis=0)
     band = lax.axis_index("lat")
     is_even = lax.rem(band, 2) == 0
     even, odd = even_ref[:, -128:], odd_ref[:, -128:]
     corners = (jnp.where(is_even, odd, even), jnp.where(is_even, even, odd))
-    for at, target in enumerate((surface_win, east_win, north_win, wet_win)):
+    for copy in copies[:4]:
+        copy.wait()
+    middle = pl.ds(MARGIN, rows)
+    for at, target in ((3, wet_win), (0, surface_win), (1, east_win), (2, north_win)):
+        field = fields.at[at] if at < 3 else land
         even, odd = even_rows[at], odd_rows[at]
         halos = (jnp.where(is_even, odd, even), jnp.where(is_even, even, odd))
+        for tile in range(0, last, 128):
+            natural[tile // 128, middle] = field[:, tile : tile + 128].astype(f32)
+        tail = jnp.concatenate(
+            [field[:, last:].astype(f32), jnp.zeros((rows, width - cols), f32)], axis=1
+        )
+        tail = with_sides(tail, left, right, cols - last, at)
+        for tile in range(last, width, 128):
+            natural[tile // 128, middle] = tail[:, tile - last : tile - last + 128]
         for halo, corner, first, inside in zip(
             halos, corners, (0, MARGIN + rows), (band > 0, band < bands - 1)
         ):
-            place = pl.ds(first, MARGIN)
-            target[place, :last] = jnp.where(inside, halo[:, :last], 0.0)
+            halo = jnp.where(inside, halo, 0.0)
             tail = with_sides(halo[:, last:], corner, corner, cols - last, at)
-            target[place, last:] = jnp.where(inside, tail, 0.0)
-    for at, target in enumerate((surface_win, east_win, north_win, wet_win)):
-        copies[at].wait()
-        field = fields.at[at] if at < 3 else land
-        target[MARGIN : MARGIN + rows, :last] = field[:, :last].astype(f32)
-        tail = jnp.concatenate(
-            [field[:, last:].astype(f32), jnp.zeros((rows, width - cols), f32)], axis=1
-        )
-        target[MARGIN : MARGIN + rows, last:] = with_sides(tail, left, right, cols - last, at)
+            tail = jnp.where(inside, tail, 0.0)
+            for tile in range(0, width, 128):
+                block = tail[:, tile - last :][:, :128] if tile >= last else halo[:, tile:][:, :128]
+                natural[tile // 128, pl.ds(first, MARGIN)] = block
+        for tile in range(0, width, 128):
+            for v, block in enumerate(interleaved(natural.at[tile // 128], step)):
+                place = (slice(8 * v, 8 * v + 8), slice(tile, tile + 128))
+                if at == 3:
+                    block = STEP * block
+                elif at > 0:
+                    block = jnp.where(wet_win[place] > 0.0, block, 0.0)
+                target[place] = block
+        if at in (1, 3):
+            shifted = east_win if at == 1 else moved_win
+            for v in range(step):
+                shifted[8 * v : 8 * v + 8] = pltpu.roll(target[8 * v : 8 * v + 8], 1, 1)
 
 
 def substep_kernel(
@@ -351,15 +432,17 @@
     east_win,
     north_win,
     wet,
+    moved,
     loading_hbm,
     surface_hbm,
     east_hbm,
     north_hbm,
+    column,
     load,
     pressure,
-    surface,
     east,
     north,
+    natural,
     loading_out,
     surface_out,
     east_out,
@@ -368,29 +451,42 @@
 ):
     rows, cols = loading_hbm.shape
     taller, width = wet.shape
+    step = taller // 8
     waves = harm_ref.shape[0] // 2
     me, band = lax.axis_index("lon"), lax.axis_index("lat")
     below, above = jnp.maximum(band - 1, 0), jnp.minimum(band + 1, bands - 1)
-    lanes = lax.broadcasted_iota(jnp.int32, synth_ref.shape[1:], 1)
-    groups = []
-    for core in range(2):
-        for shift in range(sectors // 2):
-            sector = owner(me, sectors, core, shift)
-            low = jnp.where(band > 0, synth_ref[below * sectors + sector], 0.0)
-            high = jnp.where(band < bands - 1, synth_ref[above * sectors + sector], 0.0)
-            group = pltpu.roll(synth_ref[band * sectors + sector], MARGIN, 1)
-            group = jnp.where(lanes < MARGIN, pltpu.roll(low, (MARGIN - rows) % 128, 1), group)
-            high = pltpu.roll(high, MARGIN + rows, 1)
-            groups.append(jnp.where(lanes >= MARGIN + rows, high, group))
-    synth = jnp.concatenate(groups, axis=0).T * (1.0 / math.sqrt(waves // 2))
-    hi, lo = split2(synth[:taller])
+
+    def gathered(place):
+        lines = [
+            synth_ref[place * sectors + owner(me, sectors, core, shift)]
+            for core, shift in row_groups(sectors)
+        ]
+        lines = jnp.concatenate(lines, axis=0)
+        return lines.T
+
+    scale = 1.0 / math.sqrt(waves // 2)
+    own = gathered(band) * scale
+    low = jnp.where(band > 0, gathered(below)[rows - MARGIN :], 0.0) * scale
+    high = jnp.where(band < bands - 1, gathered(above), 0.0) * scale
+    pieces = []
+    for at in range(2):
+        first = 64 * at
+        column[at, :MARGIN, : waves // 2] = low[first : first + MARGIN]
+        column[at, MARGIN : MARGIN + rows, : waves // 2] = own[first : first + rows]
+        column[at, MARGIN + rows :, : waves // 2] = high[first : first + MARGIN]
+        pieces.append(
+            jnp.concatenate(interleaved(column.at[at], step), axis=0)[:, : waves // 2]
+        )
+    hi, lo = split2(jnp.concatenate(pieces, axis=1))
     left = jnp.concatenate(
         [jnp.concatenate([hi, hi], axis=1), jnp.concatenate([lo, lo], axis=1)], axis=0
     )
     both = lax.dot_general(
         left, harm_ref[...], (((1,), (0,)), ((), ())), preferred_element_type=f32
     )
-    load[...] = both[:taller] + both[taller:]
+    both = both[:taller] + both[taller:]
+    load[...] = both
+    pressure[...] = surface_win[...] - both
     copies = [
         pltpu.make_async_copy(source, target, semaphores.at[at])
         for at, (source, target) in enumerate(
@@ -402,52 +498,48 @@
             )
         )
     ]
-    inner = pl.ds(MARGIN, rows)
-    loading_out[...] = load[inner, :cols]
-    copies[0].start()
-    edge = jnp.zeros((8, width), f32)
-    pressure[:8] = edge
-    pressure[taller + 8 :] = edge
-    north[:8] = edge
-    north[taller + 8 :] = edge
-    for o in range(0, taller, 8):
-        pressure[8 + o : 16 + o] = surface_win[o : o + 8] - load[o : o + 8]
+
+    def give(at, target, blocks):
+        for v, block in enumerate(blocks):
+            for tile in range(0, width, 128):
+                natural[at, tile // 128, pl.ds(v, 8, stride=step)] = block[:, tile : tile + 128]
+        for tile in range(0, cols, 128):
+            stop = min(cols, tile + 128)
+            target[:, tile:stop] = natural[at, tile // 128, pl.ds(MARGIN, rows), : stop - tile]
+        copies[at].start()
+
+    def block(ref, v):
+        return ref[8 * v : 8 * v + 8]
+
+    def across(ref, v):
+        after = pltpu.roll(block(ref, 0), 7, 0) if v == step - 1 else block(ref, v + 1)
+        before = pltpu.roll(block(ref, step - 1), 1, 0) if v == 0 else block(ref, v - 1)
+        return after - before
+
+    give(0, loading_out, [block(load, v) for v in range(step)])
     for substep in range(SUBSTEPS):
-        final = substep == SUBSTEPS - 1
-        for o in range(0, taller, 8):
-            here = pressure[8 + o : 16 + o]
-            damp = wet[o : o + 8]
-            flow = east_win[o : o + 8] if substep == 0 else east[o : o + 8]
-            flow = damp * (
-                flow - STEP * (pltpu.roll(here, width - 1, 1) - pltpu.roll(here, 1, 1))
-            )
-            east[o : o + 8] = flow
-            other = north_win[o : o + 8] if substep == 0 else north[8 + o : 16 + o]
-            other = damp * (
-                other - STEP * (pressure[9 + o : 17 + o] - pressure[7 + o : 15 + o])
-            )
-            north[8 + o : 16 + o] = other
-            if final and MARGIN <= o < MARGIN + rows:
-                east_out[o - MARGIN : o - MARGIN + 8] = flow[:, :cols]
-                north_out[o - MARGIN : o - MARGIN + 8] = other[:, :cols]
+        first, final = substep == 0, substep == SUBSTEPS - 1
+        for v in range(step):
+            here = block(pressure, v)
+            flow = block(east_win if first else east, v)
+            flow = flow - block(moved, v) * (here - pltpu.roll(here, 2, 1))
+            east[8 * v : 8 * v + 8] = flow
+            flow = block(north_win if first else north, v)
+            north[8 * v : 8 * v + 8] = flow - block(wet, v) * across(pressure, v)
         if final:
-            copies[2].start()
-            copies[3].start()
-        for o in range(0, taller, 8):
-            if final and not MARGIN <= o < MARGIN + rows:
-                continue
-            flow = east[o : o + 8]
-            change = STEP * (pltpu.roll(flow, width - 1, 1) - pltpu.roll(flow, 1, 1)) + STEP * (
-                north[9 + o : 17 + o] - north[7 + o : 15 + o]
-            )
-            level = surface_win[o : o + 8] if substep == 0 else surface[o : o + 8]
-            level = level - wet[o : o + 8] * change
+            give(2, east_out, [pltpu.roll(block(east, v), width - 1, 1) for v in range(step)])
+            give(3, north_out, [block(north, v) for v in range(step)])
+        levels = []
+        for v in range(step):
+            flow = block(east, v)
+            change = pltpu.roll(flow, width - 2, 1) - flow + across(north, v)
+            level = block(pressure, v) - block(wet, v) * change
             if final:
-                surface_out[o - MARGIN : o - MARGIN + 8] = level[:, :cols]
+                levels.append(level + block(load, v))
             else:
-                surface[o : o + 8] = level
-                pressure[8 + o : 16 + o] = level - load[o : o + 8]
-    copies[1].start()
+                pressure[8 * v : 8 * v + 8] = level
+        if final:
+            give(1, surface_out, levels)
     for copy in copies:
         copy.wait()
 
@@ -462,33 +554,29 @@
     width = -(-(cols + 2 * MARGIN) // 128) * 128
     taller = rows + 2 * MARGIN
     group, half = 2 * slots, rows // 2
+    back = (cols - MARGIN) // 128 * 128
     DMA = pltpu.SemaphoreType.DMA
     fields = (height, east_flow, north_flow, land_sea)
 
-    keep, send, even, odd, legendre = pl.pallas_call(
+    keep, send = pl.pallas_call(
         functools.partial(transform_kernel, period, slots),
-        out_shape=[
-            struct((chips, group, 128)),
-            struct((chips * group + half, 128)),
-            struct((4, MARGIN, width)),
-            struct((4, MARGIN, width)),
-            struct(legendre.shape),
-        ],
-        in_specs=[HBM] * 6,
-        out_specs=[VMEM] * 5,
+        out_shape=[struct((chips, group, 128)), struct((chips * group + half, 128))],
+        in_specs=[HBM] * 5,
+        out_specs=[VMEM] * 2,
         scratch_shapes=[
             pltpu.SMEM((waves,), jnp.int32),
             pltpu.VMEM((rows, cols), f32),
-            pltpu.VMEM((rows, cols), f32),
-            pltpu.VMEM((rows, cols), f32),
-            pltpu.VMEM((rows, cols), jnp.int32),
+            pltpu.VMEM((2, rows, 128), f32),
+            pltpu.VMEM((2, rows, cols - back), f32),
+            pltpu.VMEM((rows, 128), jnp.int32),
+            pltpu.VMEM((rows, cols - back), jnp.int32),
             pltpu.VMEM((4 * waves, width), bf16),
             pltpu.VMEM((2 * rows, width), bf16),
-            DMA((6,)),
+            DMA((8,)),
         ],
         name="transform",
         compiler_params=LIMIT,
-    )(*in_hbm(wavenumbers, *fields, legendre))
+    )(*in_hbm(wavenumbers, *fields))
     core = lax.ppermute(send, "lon", [(i, i ^ 1) for i in range(sectors)])
     neighbours = (1, chips - 1)
     own, *outgoing = pl.pallas_call(
@@ -511,6 +599,19 @@
     ]
     sides = (core, arrived[0], arrived[-1])
 
+    even, odd, legendre = pl.pallas_call(
+        stage_kernel,
+        out_shape=[struct((4, MARGIN, width))] * 2 + [struct(legendre.shape)],
+        in_specs=[VMEM] + [HBM] * 5,
+        out_specs=[VMEM] * 3,
+        scratch_shapes=[
+            pltpu.VMEM((2, 3, MARGIN, cols), f32),
+            pltpu.VMEM((2, MARGIN, cols), jnp.int32),
+            DMA((9,)),
+        ],
+        name="stage",
+        compiler_params=LIMIT,
+    )(own, *in_hbm(*fields, legendre))
     links = [[(i, i + 1) for i in range(first, bands - 1, 2)] for first in (0, 1)]
     links = [pairs + [(j, i) for i, j in pairs] for pairs in links]
     even, odd = [lax.ppermute(block, "lat", pairs) for block, pairs in zip((even, odd), links)]
@@ -545,7 +646,7 @@
 
     synth = pl.pallas_call(
         synthesis,
-        out_shape=struct((bands * sectors, group, 128)),
+        out_shape=struct((bands * sectors, slots, 128)),
         in_specs=[VMEM] * (len(pieces) + 2),
         out_specs=VMEM,
         scratch_shapes=[pltpu.VMEM((group, degrees), f32)],
@@ -557,13 +658,14 @@
 
     *windows, harmonics = pl.pallas_call(
         functools.partial(windows_kernel, period, slots, chips, bands),
-        out_shape=[struct((taller, width))] * 4 + [struct((4 * waves, width), bf16)],
+        out_shape=[struct((taller, width))] * 5 + [struct((4 * waves, width), bf16)],
         in_specs=[HBM] * 5 + [VMEM] * 7,
-        out_specs=[VMEM] * 5,
+        out_specs=[VMEM] * 6,
         scratch_shapes=[
             pltpu.SMEM((waves,), jnp.int32),
             pltpu.VMEM((3, rows, cols), f32),
             pltpu.VMEM((rows, cols), jnp.int32),
+            pltpu.VMEM((width // 128, taller, 128), f32),
             DMA((5,)),
         ],
         name="windows",
@@ -574,14 +676,15 @@
     return pl.pallas_call(
         functools.partial(substep_kernel, sectors, bands),
         out_shape=[struct((rows, cols))] * 4,
-        in_specs=[VMEM] * 6,
+        in_specs=[VMEM] * 7,
         out_specs=[HBM] * 4,
         scratch_shapes=[
-            pltpu.VMEM((taller, width), f32),
-            pltpu.VMEM((taller + 16, width), f32),
+            pltpu.VMEM((2, taller, 128), f32),
             pltpu.VMEM((taller, width), f32),
             pltpu.VMEM((taller, width), f32),
-            pltpu.VMEM((taller + 16, width), f32),
+            pltpu.VMEM((taller, width), f32),
+            pltpu.VMEM((taller, width), f32),
+            pltpu.VMEM((4, width // 128, taller, 128), f32),
         ]
         + [pltpu.VMEM((rows, cols), f32)] * 4
         + [DMA((4,))],

time: 38.6 us -> 37 us (0.959)
  waiting for transfers between devices: 12.9 us -> 10.1 us
  Pallas kernels: 8.71 us -> 9.85 us
    pallas_call x1 -> x2, Pallas kernels: 1.09 us -> 3.02 us  [the longest x1 1.86 us: shards(): pl.pallas_call(stage_kernel, out_shape=[struct((4, MARGIN, width))] * 2 +...]
    ppermute x3, waiting for transfers between devices: 3.56 us -> 1.69 us  [shards(): lax.ppermute(block, 'lon', [(i, (i + 2 * shift) % sectors) for i in range...]
    all_to_all x1, waiting for transfers between devices: 6.4 us -> 5.45 us  [shards(): everyone = lax.all_to_all(synth, ('lat', 'lon'), 0, 0, tiled=True)]
    pallas_call x1, Pallas kernels: 3.27 us -> 2.57 us  [shards(): pl.pallas_call(functools.partial(substep_kernel, sectors, bands), out_sha...]
  transfers between devices with their start and end apart: 10 -> 10, of which waited for: 4 -> 4; matrix products, arithmetic and copies ran while one was open for 0% -> 0% of each run, Pallas kernels for 7% -> 13%
where the time goes in v5:
time: 37 us; the launch traced here: 36.8 us
  starting transfers between devices  16.1 us (44%)
  waiting for transfers between devices  10.1 us (27%)
  Pallas kernels  9.85 us (27%)
  between operations  0.7 us (2%)
    ppermute x3, starting transfers between devices, shards(): lax.ppermute(block, 'lon', [(i, (i + 2 * shift) % sectors) for i in range...  5.95 us
    all_to_all x1, waiting for transfers between devices, shards(): everyone = lax.all_to_all(synth, ('lat', 'lon'), 0, 0, tiled=True)  5.45 us
    all_to_all x1, starting transfers between devices, shards(): everyone = lax.all_to_all(synth, ('lat', 'lon'), 0, 0, tiled=True)  3.79 us
    ppermute x3, starting transfers between devices, shards(): lax.ppermute(block, 'lat', [(i, i ^ step) for i in range(bands)])  3.55 us
    pallas_call x1, Pallas kernels, shards(): pl.pallas_call(functools.partial(substep_kernel, sectors, bands), out_sha...  2.57 us
    ppermute x2, starting transfers between devices, shards(): lax.ppermute(block, 'lat', pairs)  2.31 us
    ppermute x3, waiting for transfers between devices, shards(): lax.ppermute(block, 'lat', [(i, i ^ step) for i in range(bands)])  2.07 us
    pallas_call x1, Pallas kernels, shards(): pl.pallas_call(functools.partial(windows_kernel, period, slots, chips, ba...  1.91 us
  transfers between devices with their start and end apart: 10, of which 4 were waited for; matrix products, arithmetic and copies ran while one was open for 0% of the time, Pallas kernels for 13%

profile of v5, /device:TPU:0, one launch (start us, length us, event | category | flops | bytes accessed | tf_op | source)
XLA Modules:
  0.0 36.8 jit_solution(10247771429589138021)
XLA Ops:
  0.6 1.8 %transform.1 = (f32[4,8,128]{2,1,0:T(8,128)S(1)}, f32[64,128]{1,0:T(8,128)S(1)}) custom-call(s32[32]{0:T(128)} %waves_hbm.3, f32[64,1080]{1,0:T(8,128)} %height_hbm.5, f32[64,1080]{1,0:T(8,128)} %east_hbm.5, f32[64,1080]{1,0:T(8,128)} %north_hbm.5, s32[64,1080]{1,0:T(8,128)} %land_hbm.5), custom_call_target="tpu_custom_call" | custom-call | tf_op jit(solution)/shard_map/transform/pallas_call | solution.py:561
  2.4 0.5 %collective-permute-start = (f32[64,128]{1,0:T(8,128)S(1)}, f32[64,128]{1,0:T(8,128)S(1)}, u32[]{:S(2)}, u32[]{:S(2)}) collective-permute-start(f32[64,128]{1,0:T(8,128)S(1)} %get-tuple-element.23), channel_id=1, source_target_pairs={{0,1},{1,0},{2,3},{3,2},{4,5},{5,4},{6,7},{7,6},{8,9},{9,8},{10,11... | collective-permute-start | bytes 98312 | tf_op jit(solution)/shard_map/ppermute | solution.py:580
  2.9 0.9 %collective-permute-done.recv_ref.refs_4_.core_ref = f32[64,128]{1,0:T(8,128)S(1)} collective-permute-done((f32[64,128]{1,0:T(8,128)S(1)}, f32[64,128]{1,0:T(8,128)S(1)}, u32[]{:S(2)}, u32[]{:S(2)}) %collective-permute-start) | collective-permute-done | bytes 32800 | tf_op jit(solution)/shard_map/ppermute | solution.py:580
  3.8 2.9 %collective-permute-start.1 = (f32[40,128]{1,0:T(8,128)S(1)}, f32[40,128]{1,0:T(8,128)S(1)}, u32[]{:S(2)}, u32[]{:S(2)}) collective-permute-start(f32[40,128]{1,0:T(8,128)S(1)} %get-tuple-element.25), channel_id=1, source_target_pairs={{0,2},{1,3},{2,4},{3,5},{4,6},{5,7},{6,0},{7,1},{8,10},{9,11},{10,... | collective-permute-start | bytes 61448 | tf_op jit(solution)/shard_map/ppermute | solution.py:595
  6.7 2.1 %collective-permute-start.3 = (f32[40,128]{1,0:T(8,128)S(1)}, f32[40,128]{1,0:T(8,128)S(1)}, u32[]{:S(2)}, u32[]{:S(2)}) collective-permute-start(f32[40,128]{1,0:T(8,128)S(1)} %get-tuple-element.27), channel_id=1, source_target_pairs={{0,6},{1,7},{2,0},{3,1},{4,2},{5,3},{6,4},{7,5},{8,14},{9,15},{10,... | collective-permute-start | bytes 61448 | tf_op jit(solution)/shard_map/ppermute | solution.py:595
  8.8 1.0 %collective-permute-start.2 = (f32[8,128]{1,0:T(8,128)S(1)}, f32[8,128]{1,0:T(8,128)S(1)}, u32[]{:S(2)}, u32[]{:S(2)}) collective-permute-start(f32[8,128]{1,0:T(8,128)S(1)} %get-tuple-element.26), channel_id=1, source_target_pairs={{0,4},{1,5},{2,6},{3,7},{4,0},{5,1},{6,2},{7,3},{8,12},{9,13},{10,... | collective-permute-start | bytes 12296 | tf_op jit(solution)/shard_map/ppermute | solution.py:595
  9.8 1.9 %stage.1 = (f32[4,8,1152]{2,1,0:T(8,128)S(1)}, f32[4,8,1152]{2,1,0:T(8,128)S(1)}, f32[4,64,2048]{2,1,0:T(8,128)S(1)}) custom-call(f32[8,128]{1,0:T(8,128)S(1)} %get-tuple-element.24.after_ref.refs_0_, f32[64,1080]{1,0:T(8,128)} %height_hbm.5, f32[64,1080]{1,0:T(8,128)} %east_hbm.5, f32[64,1080]{1,0:T(8,128)} %north_hbm.5, s32[64,1080]{1,0:T(8,128)} %land_hbm.5, ...), custom_call_target="tpu_custom_call" | custom-call | tf_op jit(solution)/shard_map/stage/pallas_call | solution.py:602
  11.6 1.7 %collective-permute-done.2.refs_2_ = f32[8,128]{1,0:T(8,128)S(1)} collective-permute-done((f32[8,128]{1,0:T(8,128)S(1)}, f32[8,128]{1,0:T(8,128)S(1)}, u32[]{:S(2)}, u32[]{:S(2)}) %collective-permute-start.2) | collective-permute-done | bytes 4128 | tf_op jit(solution)/shard_map/ppermute | solution.py:595
  13.3 0.0 collective-permute-done.1.refs_1_.west_ref
  13.3 0.0 collective-permute-done.3.refs_3_.east_ref
  13.3 0.6 %analysis.1 = (f32[8,2048]{1,0:T(8,128)S(1)}, f32[8,2176]{1,0:T(8,128)S(1)}, f32[8,2176]{1,0:T(8,128)S(1)}) custom-call(f32[8,128]{1,0:T(8,128)S(1)} %get-tuple-element.24.after_ref.refs_0_, f32[40,128]{1,0:T(8,128)S(1)} %collective-permute-done.1.refs_1_.west_ref, f32[8,128]{1,0:T(8,128)S(1)} %collective-permute-done.2.refs_2_, ...), custom_call_target="tpu_custom_call" | custom-call | tf_op jit(solution)/shard_map/analysis/pallas_call | solution.py:624
  13.9 1.7 %collective-permute-start.4 = (f32[8,2176]{1,0:T(8,128)S(1)}, f32[8,2176]{1,0:T(8,128)S(1)}, u32[]{:S(2)}, u32[]{:S(2)}) collective-permute-start(f32[8,2176]{1,0:T(8,128)S(1)} %get-tuple-element.30), channel_id=1, source_target_pairs={{0,8},{8,0},{16,24},{24,16},{1,9},{9,1},{17,25},{25,17},{2,10},{10... | collective-permute-start | bytes 208904 | tf_op jit(solution)/shard_map/ppermute | solution.py:634
  15.6 1.5 %collective-permute-start.5 = (f32[8,2176]{1,0:T(8,128)S(1)}, f32[8,2176]{1,0:T(8,128)S(1)}, u32[]{:S(2)}, u32[]{:S(2)}) collective-permute-start(f32[8,2176]{1,0:T(8,128)S(1)} %get-tuple-element.31), channel_id=1, source_target_pairs={{0,24},{8,16},{16,8},{24,0},{1,25},{9,17},{17,9},{25,1},{2,26},{10... | collective-permute-start | bytes 208904 | tf_op jit(solution)/shard_map/ppermute | solution.py:634
  17.1 0.3 collective-permute-start.6
  17.4 1.7 %collective-permute-start.7 = (f32[4,8,1152]{2,1,0:T(8,128)S(1)}, f32[4,8,1152]{2,1,0:T(8,128)S(1)}, u32[]{:S(2)}, u32[]{:S(2)}) collective-permute-start(f32[4,8,1152]{2,1,0:T(8,128)S(1)} %get-tuple-element.32), channel_id=1, source_target_pairs={{0,8},{16,24},{8,0},{24,16},{1,9},{17,25},{9,1},{25,17},{2,10},{18... | collective-permute-start | bytes 442376 | tf_op jit(solution)/shard_map/ppermute | solution.py:617
  19.1 0.7 %collective-permute-start.8 = (f32[4,8,1152]{2,1,0:T(8,128)S(1)}, f32[4,8,1152]{2,1,0:T(8,128)S(1)}, u32[]{:S(2)}, u32[]{:S(2)}) collective-permute-start(f32[4,8,1152]{2,1,0:T(8,128)S(1)} %get-tuple-element.33), channel_id=1, source_target_pairs={{8,16},{16,8},{9,17},{17,9},{10,18},{18,10},{11,19},{19,11},{12,20... | collective-permute-start | bytes 442376 | tf_op jit(solution)/shard_map/ppermute | solution.py:617
  19.8 2.1 %collective-permute-done.6.refs_3_ = f32[8,2048]{1,0:T(8,128)S(1)} collective-permute-done((f32[8,2048]{1,0:T(8,128)S(1)}, f32[8,2048]{1,0:T(8,128)S(1)}, u32[]{:S(2)}, u32[]{:S(2)}) %collective-permute-start.6) | collective-permute-done | bytes 65568 | tf_op jit(solution)/shard_map/ppermute | solution.py:634
  21.8 0.0 collective-permute-done.4.refs_1_.even_ref
  21.8 0.0 collective-permute-done.5.refs_2_.odd_ref
  21.8 1.2 %synthesis.1 = f32[32,4,128]{2,1,0:T(4,128)} custom-call(f32[8,2048]{1,0:T(8,128)S(1)} %get-tuple-element.29.refs_0_, f32[8,2176]{1,0:T(8,128)S(1)} %collective-permute-done.4.refs_1_.even_ref, f32[8,2176]{1,0:T(8,128)S(1)} %collective-permute-done.5.refs_2_.odd_ref, f32[8,2048]{1,0:T(8,128)S(1)} %collective-permute-done.6.refs_3_, f32[1,2048]{1,0:T(1,128)S(1)} %bitcast.1, ...), custom_call_target="tpu_custom_call" | custom-call | flops 99999997952 | bytes 400000000 | tf_op jit(solution)/shard_map/synthesis/pallas_call | solution.py:647
  23.0 3.8 %all-to-all-start = ((f32[32,4,128]{2,1,0:T(4,128)}), f32[32,4,128]{2,1,0:T(4,128)S(1)}, u32[]{:S(2)}, u32[]{:S(2)}) async-start(f32[32,4,128]{2,1,0:T(4,128)} %synthesis.1), calls=%async_computation | async-start | bytes 131072 | tf_op jit(solution)/shard_map/all_to_all | solution.py:657
  26.8 1.9 %windows.1 = (f32[80,1152]{1,0:T(8,128)S(1)}, f32[80,1152]{1,0:T(8,128)S(1)}, f32[80,1152]{1,0:T(8,128)S(1)}, f32[80,1152]{1,0:T(8,128)S(1)}, f32[80,1152]{1,0:T(8,128)S(1)}, /*index=5*/bf16[128,1152]{1,0:T(8,128)(2,1)S(1)}) custom-call(s32[32]{0:T(128)} %waves_hbm.3, f32[64,1080]{1,0:T(8,128)} %height_hbm.5, f32[64,1080]{1,0:T(8,128)} %east_hbm.5, ...), custom_call_target="tpu_custom_call" | custom-call | flops 99999997952 | bytes 400000000 | tf_op jit(solution)/shard_map/windows/pallas_call | solution.py:659
  28.7 5.5 %all-to-all-done.synth_ref = f32[32,4,128]{2,1,0:T(4,128)S(1)} async-done(((f32[32,4,128]{2,1,0:T(4,128)}), f32[32,4,128]{2,1,0:T(4,128)S(1)}, u32[]{:S(2)}, u32[]{:S(2)}) %all-to-all-start) | async-done | bytes 65568 | tf_op jit(solution)/shard_map/all_to_all | solution.py:657
  34.2 2.6 %substeps.1 = (f32[64,1080]{1,0:T(8,128)}, f32[64,1080]{1,0:T(8,128)}, f32[64,1080]{1,0:T(8,128)}, f32[64,1080]{1,0:T(8,128)}) custom-call(f32[32,4,128]{2,1,0:T(4,128)S(1)} %all-to-all-done.synth_ref, bf16[128,1152]{1,0:T(8,128)(2,1)S(1)} %get-tuple-element.34.harm_ref, f32[80,1152]{1,0:T(8,128)S(1)} %get-tuple-element.35.surface_win, ...), custom_call_target="tpu_custom_call" | custom-call | tf_op jit(solution)/shard_map/substeps/pallas_call | solution.py:676
  (5 shorter events, 0.0 us)
Async XLA Ops:
  2.4 1.4 %collective-permute-start = (f32[64,128]{1,0:T(8,128)S(1)}, f32[64,128]{1,0:T(8,128)S(1)}, u32[]{:S(2)}, u32[]{:S(2)}) collective-permute-start(f32[64,128]{1,0:T(8,128)S(1)} %get-tuple-element.23), channel_id=1, source_target_pairs={{0,1},{1,0},{2,3},{3,2},{4,5},{5,4},{6,7},{7,6},{8,9},{9,8},{10,11... | collective-permute-start | bytes 98312 | tf_op jit(solution)/shard_map/ppermute | solution.py:580
  3.8 9.5 %collective-permute-start.1 = (f32[40,128]{1,0:T(8,128)S(1)}, f32[40,128]{1,0:T(8,128)S(1)}, u32[]{:S(2)}, u32[]{:S(2)}) collective-permute-start(f32[40,128]{1,0:T(8,128)S(1)} %get-tuple-element.25), channel_id=1, source_target_pairs={{0,2},{1,3},{2,4},{3,5},{4,6},{5,7},{6,0},{7,1},{8,10},{9,11},{10,... | collective-permute-start | bytes 61448 | tf_op jit(solution)/shard_map/ppermute | solution.py:595
  6.7 6.6 %collective-permute-start.3 = (f32[40,128]{1,0:T(8,128)S(1)}, f32[40,128]{1,0:T(8,128)S(1)}, u32[]{:S(2)}, u32[]{:S(2)}) collective-permute-start(f32[40,128]{1,0:T(8,128)S(1)} %get-tuple-element.27), channel_id=1, source_target_pairs={{0,6},{1,7},{2,0},{3,1},{4,2},{5,3},{6,4},{7,5},{8,14},{9,15},{10,... | collective-permute-start | bytes 61448 | tf_op jit(solution)/shard_map/ppermute | solution.py:595
  8.8 4.5 %collective-permute-start.2 = (f32[8,128]{1,0:T(8,128)S(1)}, f32[8,128]{1,0:T(8,128)S(1)}, u32[]{:S(2)}, u32[]{:S(2)}) collective-permute-start(f32[8,128]{1,0:T(8,128)S(1)} %get-tuple-element.26), channel_id=1, source_target_pairs={{0,4},{1,5},{2,6},{3,7},{4,0},{5,1},{6,2},{7,3},{8,12},{9,13},{10,... | collective-permute-start | bytes 12296 | tf_op jit(solution)/shard_map/ppermute | solution.py:595
  9.8 12.1 %copy-start = (f32[2048]{0:T(1024)S(1)}, f32[2048]{0:T(1024)}, u32[]{:S(2)}) copy-start(f32[2048]{0:T(1024)} %param.11) | copy-start | bytes 24580
  13.9 7.9 %collective-permute-start.4 = (f32[8,2176]{1,0:T(8,128)S(1)}, f32[8,2176]{1,0:T(8,128)S(1)}, u32[]{:S(2)}, u32[]{:S(2)}) collective-permute-start(f32[8,2176]{1,0:T(8,128)S(1)} %get-tuple-element.30), channel_id=1, source_target_pairs={{0,8},{8,0},{16,24},{24,16},{1,9},{9,1},{17,25},{25,17},{2,10},{10... | collective-permute-start | bytes 208904 | tf_op jit(solution)/shard_map/ppermute | solution.py:634
  15.6 6.2 %collective-permute-start.5 = (f32[8,2176]{1,0:T(8,128)S(1)}, f32[8,2176]{1,0:T(8,128)S(1)}, u32[]{:S(2)}, u32[]{:S(2)}) collective-permute-start(f32[8,2176]{1,0:T(8,128)S(1)} %get-tuple-element.31), channel_id=1, source_target_pairs={{0,24},{8,16},{16,8},{24,0},{1,25},{9,17},{17,9},{25,1},{2,26},{10... | collective-permute-start | bytes 208904 | tf_op jit(solution)/shard_map/ppermute | solution.py:634
  17.1 4.7 %collective-permute-start.6 = (f32[8,2048]{1,0:T(8,128)S(1)}, f32[8,2048]{1,0:T(8,128)S(1)}, u32[]{:S(2)}, u32[]{:S(2)}) collective-permute-start(f32[8,2048]{1,0:T(8,128)S(1)} %get-tuple-element.29.refs_0_), channel_id=1, source_target_pairs={{0,16},{8,24},{16,0},{24,8},{1,17},{9,25},{17,1},{25,9},{2,18},{10... | collective-permute-start | bytes 196616 | tf_op jit(solution)/shard_map/ppermute | solution.py:634
  17.4 9.4 %collective-permute-start.7 = (f32[4,8,1152]{2,1,0:T(8,128)S(1)}, f32[4,8,1152]{2,1,0:T(8,128)S(1)}, u32[]{:S(2)}, u32[]{:S(2)}) collective-permute-start(f32[4,8,1152]{2,1,0:T(8,128)S(1)} %get-tuple-element.32), channel_id=1, source_target_pairs={{0,8},{16,24},{8,0},{24,16},{1,9},{17,25},{9,1},{25,17},{2,10},{18... | collective-permute-start | bytes 442376 | tf_op jit(solution)/shard_map/ppermute | solution.py:617
  19.1 7.7 %collective-permute-start.8 = (f32[4,8,1152]{2,1,0:T(8,128)S(1)}, f32[4,8,1152]{2,1,0:T(8,128)S(1)}, u32[]{:S(2)}, u32[]{:S(2)}) collective-permute-start(f32[4,8,1152]{2,1,0:T(8,128)S(1)} %get-tuple-element.33), channel_id=1, source_target_pairs={{8,16},{16,8},{9,17},{17,9},{10,18},{18,10},{11,19},{19,11},{12,20... | collective-permute-start | bytes 442376 | tf_op jit(solution)/shard_map/ppermute | solution.py:617
  23.0 11.2 %all-to-all-start = ((f32[32,4,128]{2,1,0:T(4,128)}), f32[32,4,128]{2,1,0:T(4,128)S(1)}, u32[]{:S(2)}, u32[]{:S(2)}) async-start(f32[32,4,128]{2,1,0:T(4,128)} %synthesis.1), calls=%async_computation | async-start | bytes 131072 | tf_op jit(solution)/shard_map/all_to_all | solution.py:657

commit v6 on v5

--- a/solution.py
+++ b/solution.py
@@ -36,7 +36,8 @@
 
 def owner(me, sectors, core, shift):
     chips = sectors // 2
-    return 2 * lax.rem(me // 2 + shift, chips) + lax.bitwise_xor(lax.rem(me, 2), core)
+    crossed = core if shift == 0 else 1 - core
+    return 2 * lax.rem(me // 2 + shift, chips) + lax.bitwise_xor(lax.rem(me, 2), crossed)
 
 
 def row_groups(sectors):
@@ -106,6 +107,7 @@
     land_hbm,
     keep_ref,
     send_ref,
+    tile_ref,
     waves_ref,
     height_ref,
     flow_front,
@@ -153,11 +155,14 @@
         hi, lo = split2(block)
         field_ref[:rows, tile : tile + 128] = hi
         field_ref[rows:, tile : tile + 128] = lo
-    both = lax.dot_general(
-        harm_ref[...], field_ref[...], (((1,), (1,)), ((), ())), preferred_element_type=f32
+    rows_by_rows = (((1,), (1,)), ((), ()))
+    high = lax.dot_general(
+        harm_ref[...], field_ref[:rows], rows_by_rows, preferred_element_type=f32
     )
-    total = both[:waves] + both[waves:]
-    total = (total[:, :rows] + total[:, rows:]) * (1.0 / math.sqrt(period))
+    low = lax.dot_general(
+        harm_ref[:waves], field_ref[rows:], rows_by_rows, preferred_element_type=f32
+    )
+    total = (high[:waves] + high[waves:] + low) * (1.0 / math.sqrt(period))
     total = jnp.concatenate([total, jnp.zeros((waves, 128 - rows), f32)], axis=1)
     keep_ref[...] = total[: waves // 2].reshape(keep_ref.shape)
     send_ref[: waves // 2] = total[waves // 2 :]
@@ -172,9 +177,11 @@
     ):
         pieces += [front, end]
     half = rows // 2
-    send_ref[waves // 2 :] = jnp.concatenate(
+    tile = jnp.concatenate(
         [piece[:half] for piece in pieces] + [piece[half:] for piece in pieces], axis=1
     )
+    send_ref[waves // 2 :] = tile
+    tile_ref[...] = tile
 
 
 def stage_kernel(
@@ -221,13 +228,13 @@
     copies[-1].wait()
 
 
-def mix_kernel(keep_ref, recv_ref, own_ref, *send_refs):
+def mix_kernel(keep_ref, tile_ref, recv_ref, own_ref, *send_refs):
     chips, group, _ = keep_ref.shape
     own_ref[...] = keep_ref[0] + recv_ref[:group]
     for shift, ref in enumerate(send_refs, 1):
         ref[:group] = keep_ref[shift] + recv_ref[shift * group : (shift + 1) * group]
         if ref.shape[0] > group:
-            ref[group:] = recv_ref[chips * group :]
+            ref[group:] = tile_ref[...]
 
 
 def analysis_kernel(part_refs, core_ref, legendre_ref, spectral_ref, even_ref, odd_ref):
@@ -558,11 +565,15 @@
     DMA = pltpu.SemaphoreType.DMA
     fields = (height, east_flow, north_flow, land_sea)
 
-    keep, send = pl.pallas_call(
+    keep, send, tile = pl.pallas_call(
         functools.partial(transform_kernel, period, slots),
-        out_shape=[struct((chips, group, 128)), struct((chips * group + half, 128))],
+        out_shape=[
+            struct((chips, group, 128)),
+            struct((chips * group + half, 128)),
+            struct((half, 128)),
+        ],
         in_specs=[HBM] * 5,
-        out_specs=[VMEM] * 2,
+        out_specs=[VMEM] * 3,
         scratch_shapes=[
             pltpu.SMEM((waves,), jnp.int32),
             pltpu.VMEM((rows, cols), f32),
@@ -586,17 +597,15 @@
             struct((group + (half if shift in neighbours else 0), 128))
             for shift in range(1, chips)
         ],
-        in_specs=[VMEM] * 2,
+        in_specs=[VMEM] * 3,
         out_specs=[VMEM] * chips,
         name="mix",
         compiler_params=LIMIT,
-    )(keep, core)
-    arrived = [
-        lax.ppermute(
-            block, "lon", [(i, (i + 2 * shift) % sectors) for i in range(sectors)]
-        )
-        for shift, block in enumerate(outgoing, 1)
-    ]
+    )(keep, tile, core)
+    arrived = []
+    for shift, block in enumerate(outgoing, 1):
+        across = [(i, 2 * ((i // 2 + shift) % chips) + 1 - i % 2) for i in range(sectors)]
+        arrived.append(lax.ppermute(block, "lon", across))
     sides = (core, arrived[0], arrived[-1])
 
     even, odd, legendre = pl.pallas_call(
@@ -612,7 +621,7 @@
         name="stage",
         compiler_params=LIMIT,
     )(own, *in_hbm(*fields, legendre))
-    links = [[(i, i + 1) for i in range(first, bands - 1, 2)] for first in (0, 1)]
+    links = [[(i, (i + 1) % bands) for i in range(first, bands, 2)] for first in (0, 1)]
     links = [pairs + [(j, i) for i, j in pairs] for pairs in links]
     even, odd = [lax.ppermute(block, "lat", pairs) for block, pairs in zip((even, odd), links)]
 

time: 37 us -> 35.5 us (0.959)
  waiting for transfers between devices: 10.1 us -> 9.2 us
  starting transfers between devices: 16.1 us -> 15.6 us
    ppermute x2, waiting for transfers between devices: 0.01 us -> 0.95 us  [shards(): lax.ppermute(block, 'lat', pairs)]
    all_to_all x1, waiting for transfers between devices: 5.45 us -> 4.53 us  [shards(): everyone = lax.all_to_all(synth, ('lat', 'lon'), 0, 0, tiled=True)]
    all_to_all x1, starting transfers between devices: 3.79 us -> 3 us  [shards(): everyone = lax.all_to_all(synth, ('lat', 'lon'), 0, 0, tiled=True)]
    ppermute x2, starting transfers between devices: 2.31 us -> 3.11 us  [shards(): lax.ppermute(block, 'lat', pairs)]
    ppermute x3, waiting for transfers between devices: 2.07 us -> 1.48 us  [shards(): lax.ppermute(block, 'lat', [(i, i ^ step) for i in range(bands)])]
    ppermute x3, starting transfers between devices: 5.95 us -> 5.44 us  [shards(): arrived.append(lax.ppermute(block, 'lon', across))]
  transfers between devices with their start and end apart: 10 -> 10, of which waited for: 4 -> 5; matrix products, arithmetic and copies ran while one was open for 0% -> 0% of each run, Pallas kernels for 13% -> 14%
where the time goes in v6:
time: 35.5 us; the launch traced here: 35.3 us
  starting transfers between devices  15.6 us (44%)
  Pallas kernels  9.8 us (28%)
  waiting for transfers between devices  9.2 us (26%)
  between operations  0.69 us (2%)
    ppermute x3, starting transfers between devices, shards(): arrived.append(lax.ppermute(block, 'lon', across))  5.44 us
    all_to_all x1, waiting for transfers between devices, shards(): everyone = lax.all_to_all(synth, ('lat', 'lon'), 0, 0, tiled=True)  4.53 us
    ppermute x3, starting transfers between devices, shards(): lax.ppermute(block, 'lat', [(i, i ^ step) for i in range(bands)])  3.55 us
    ppermute x2, starting transfers between devices, shards(): lax.ppermute(block, 'lat', pairs)  3.11 us
    all_to_all x1, starting transfers between devices, shards(): everyone = lax.all_to_all(synth, ('lat', 'lon'), 0, 0, tiled=True)  3 us
    pallas_call x1, Pallas kernels, shards(): pl.pallas_call(functools.partial(substep_kernel, sectors, bands), out_sha...  2.58 us
    pallas_call x1, Pallas kernels, shards(): pl.pallas_call(functools.partial(windows_kernel, period, slots, chips, ba...  1.89 us
    pallas_call x1, Pallas kernels, shards(): pl.pallas_call(stage_kernel, out_shape=[struct((4, MARGIN, width))] * 2 +...  1.86 us
  transfers between devices with their start and end apart: 10, of which 5 were waited for; matrix products, arithmetic and copies ran while one was open for 0% of the time, Pallas kernels for 14%

profile of v6, /device:TPU:0, one launch (start us, length us, event | category | flops | bytes accessed | tf_op | source)
XLA Modules:
  0.0 35.3 jit_solution(3855041727429602132)
XLA Ops:
  0.6 1.7 %transform.1 = (f32[4,8,128]{2,1,0:T(8,128)S(1)}, f32[64,128]{1,0:T(8,128)S(1)}, f32[32,128]{1,0:T(8,128)S(1)}) custom-call(s32[32]{0:T(128)} %waves_hbm.3, f32[64,1080]{1,0:T(8,128)} %height_hbm.5, f32[64,1080]{1,0:T(8,128)} %east_hbm.5, f32[64,1080]{1,0:T(8,128)} %north_hbm.5, s32[64,1080]{1,0:T(8,128)} %land_hbm.5), custom_call_target="tpu_custom_call" | custom-call | tf_op jit(solution)/shard_map/transform/pallas_call | solution.py:568
  2.4 0.5 %collective-permute-start = (f32[64,128]{1,0:T(8,128)S(1)}, f32[64,128]{1,0:T(8,128)S(1)}, u32[]{:S(2)}, u32[]{:S(2)}) collective-permute-start(f32[64,128]{1,0:T(8,128)S(1)} %get-tuple-element.25), channel_id=1, source_target_pairs={{0,1},{1,0},{2,3},{3,2},{4,5},{5,4},{6,7},{7,6},{8,9},{9,8},{10,11... | collective-permute-start | bytes 98312 | tf_op jit(solution)/shard_map/ppermute | solution.py:591
  2.9 0.9 %collective-permute-done.recv_ref.refs_4_.core_ref = f32[64,128]{1,0:T(8,128)S(1)} collective-permute-done((f32[64,128]{1,0:T(8,128)S(1)}, f32[64,128]{1,0:T(8,128)S(1)}, u32[]{:S(2)}, u32[]{:S(2)}) %collective-permute-start) | collective-permute-done | bytes 32800 | tf_op jit(solution)/shard_map/ppermute | solution.py:591
  3.8 2.7 %collective-permute-start.1 = (f32[40,128]{1,0:T(8,128)S(1)}, f32[40,128]{1,0:T(8,128)S(1)}, u32[]{:S(2)}, u32[]{:S(2)}) collective-permute-start(f32[40,128]{1,0:T(8,128)S(1)} %get-tuple-element.27), channel_id=1, source_target_pairs={{0,3},{1,2},{2,5},{3,4},{4,7},{5,6},{6,1},{7,0},{8,11},{9,10},{10,... | collective-permute-start | bytes 61448 | tf_op jit(solution)/shard_map/ppermute | solution.py:608
  6.4 2.1 %collective-permute-start.3 = (f32[40,128]{1,0:T(8,128)S(1)}, f32[40,128]{1,0:T(8,128)S(1)}, u32[]{:S(2)}, u32[]{:S(2)}) collective-permute-start(f32[40,128]{1,0:T(8,128)S(1)} %get-tuple-element.29), channel_id=1, source_target_pairs={{0,7},{1,6},{2,1},{3,0},{4,3},{5,2},{6,5},{7,4},{8,15},{9,14},{10,... | collective-permute-start | bytes 61448 | tf_op jit(solution)/shard_map/ppermute | solution.py:608
  8.5 0.7 %collective-permute-start.2 = (f32[8,128]{1,0:T(8,128)S(1)}, f32[8,128]{1,0:T(8,128)S(1)}, u32[]{:S(2)}, u32[]{:S(2)}) collective-permute-start(f32[8,128]{1,0:T(8,128)S(1)} %get-tuple-element.28), channel_id=1, source_target_pairs={{0,5},{1,4},{2,7},{3,6},{4,1},{5,0},{6,3},{7,2},{8,13},{9,12},{10,... | collective-permute-start | bytes 12296 | tf_op jit(solution)/shard_map/ppermute | solution.py:608
  9.2 1.9 %stage.1 = (f32[4,8,1152]{2,1,0:T(8,128)S(1)}, f32[4,8,1152]{2,1,0:T(8,128)S(1)}, f32[4,64,2048]{2,1,0:T(8,128)S(1)}) custom-call(f32[8,128]{1,0:T(8,128)S(1)} %get-tuple-element.26.after_ref.refs_0_, f32[64,1080]{1,0:T(8,128)} %height_hbm.5, f32[64,1080]{1,0:T(8,128)} %east_hbm.5, f32[64,1080]{1,0:T(8,128)} %north_hbm.5, s32[64,1080]{1,0:T(8,128)} %land_hbm.5, ...), custom_call_target="tpu_custom_call" | custom-call | tf_op jit(solution)/shard_map/stage/pallas_call | solution.py:611
  11.1 1.4 %collective-permute-done.2.refs_2_ = f32[8,128]{1,0:T(8,128)S(1)} collective-permute-done((f32[8,128]{1,0:T(8,128)S(1)}, f32[8,128]{1,0:T(8,128)S(1)}, u32[]{:S(2)}, u32[]{:S(2)}) %collective-permute-start.2) | collective-permute-done | bytes 4128 | tf_op jit(solution)/shard_map/ppermute | solution.py:608
  12.5 0.0 collective-permute-done.1.refs_1_.west_ref
  12.5 0.0 collective-permute-done.3.refs_3_.east_ref
  12.5 0.6 %analysis.1 = (f32[8,2048]{1,0:T(8,128)S(1)}, f32[8,2176]{1,0:T(8,128)S(1)}, f32[8,2176]{1,0:T(8,128)S(1)}) custom-call(f32[8,128]{1,0:T(8,128)S(1)} %get-tuple-element.26.after_ref.refs_0_, f32[40,128]{1,0:T(8,128)S(1)} %collective-permute-done.1.refs_1_.west_ref, f32[8,128]{1,0:T(8,128)S(1)} %collective-permute-done.2.refs_2_, ...), custom_call_target="tpu_custom_call" | custom-call | tf_op jit(solution)/shard_map/analysis/pallas_call | solution.py:633
  13.0 1.7 %collective-permute-start.4 = (f32[8,2176]{1,0:T(8,128)S(1)}, f32[8,2176]{1,0:T(8,128)S(1)}, u32[]{:S(2)}, u32[]{:S(2)}) collective-permute-start(f32[8,2176]{1,0:T(8,128)S(1)} %get-tuple-element.32), channel_id=1, source_target_pairs={{0,8},{8,0},{16,24},{24,16},{1,9},{9,1},{17,25},{25,17},{2,10},{10... | collective-permute-start | bytes 208904 | tf_op jit(solution)/shard_map/ppermute | solution.py:643
  14.7 1.5 %collective-permute-start.5 = (f32[8,2176]{1,0:T(8,128)S(1)}, f32[8,2176]{1,0:T(8,128)S(1)}, u32[]{:S(2)}, u32[]{:S(2)}) collective-permute-start(f32[8,2176]{1,0:T(8,128)S(1)} %get-tuple-element.33), channel_id=1, source_target_pairs={{0,24},{8,16},{16,8},{24,0},{1,25},{9,17},{17,9},{25,1},{2,26},{10... | collective-permute-start | bytes 208904 | tf_op jit(solution)/shard_map/ppermute | solution.py:643
  16.2 0.4 %collective-permute-start.6 = (f32[8,2048]{1,0:T(8,128)S(1)}, f32[8,2048]{1,0:T(8,128)S(1)}, u32[]{:S(2)}, u32[]{:S(2)}) collective-permute-start(f32[8,2048]{1,0:T(8,128)S(1)} %get-tuple-element.31.refs_0_), channel_id=1, source_target_pairs={{0,16},{8,24},{16,0},{24,8},{1,17},{9,25},{17,1},{25,9},{2,18},{10... | collective-permute-start | bytes 196616 | tf_op jit(solution)/shard_map/ppermute | solution.py:643
  16.6 1.6 %collective-permute-start.7 = (f32[4,8,1152]{2,1,0:T(8,128)S(1)}, f32[4,8,1152]{2,1,0:T(8,128)S(1)}, u32[]{:S(2)}, u32[]{:S(2)}) collective-permute-start(f32[4,8,1152]{2,1,0:T(8,128)S(1)} %get-tuple-element.34), channel_id=1, source_target_pairs={{0,8},{16,24},{8,0},{24,16},{1,9},{17,25},{9,1},{25,17},{2,10},{18... | collective-permute-start | bytes 442376 | tf_op jit(solution)/shard_map/ppermute | solution.py:626
  18.2 1.5 %collective-permute-start.8 = (f32[4,8,1152]{2,1,0:T(8,128)S(1)}, f32[4,8,1152]{2,1,0:T(8,128)S(1)}, u32[]{:S(2)}, u32[]{:S(2)}) collective-permute-start(f32[4,8,1152]{2,1,0:T(8,128)S(1)} %get-tuple-element.35), channel_id=1, source_target_pairs={{8,16},{24,0},{16,8},{0,24},{9,17},{25,1},{17,9},{1,25},{10,18},{2... | collective-permute-start | bytes 442376 | tf_op jit(solution)/shard_map/ppermute | solution.py:626
  19.7 1.5 %collective-permute-done.6.refs_3_ = f32[8,2048]{1,0:T(8,128)S(1)} collective-permute-done((f32[8,2048]{1,0:T(8,128)S(1)}, f32[8,2048]{1,0:T(8,128)S(1)}, u32[]{:S(2)}, u32[]{:S(2)}) %collective-permute-start.6) | collective-permute-done | bytes 65568 | tf_op jit(solution)/shard_map/ppermute | solution.py:643
  21.2 0.0 collective-permute-done.4.refs_1_.even_ref
  21.2 1.2 %synthesis.1 = f32[32,4,128]{2,1,0:T(4,128)} custom-call(f32[8,2048]{1,0:T(8,128)S(1)} %get-tuple-element.31.refs_0_, f32[8,2176]{1,0:T(8,128)S(1)} %collective-permute-done.4.refs_1_.even_ref, f32[8,2176]{1,0:T(8,128)S(1)} %collective-permute-done.5.refs_2_.odd_ref, f32[8,2048]{1,0:T(8,128)S(1)} %collective-permute-done.6.refs_3_, f32[1,2048]{1,0:T(1,128)S(1)} %bitcast.1, ...), custom_call_target="tpu_custom_call" | custom-call | flops 99999997952 | bytes 400000000 | tf_op jit(solution)/shard_map/synthesis/pallas_call | solution.py:656
  22.3 3.0 %all-to-all-start = ((f32[32,4,128]{2,1,0:T(4,128)}), f32[32,4,128]{2,1,0:T(4,128)S(1)}, u32[]{:S(2)}, u32[]{:S(2)}) async-start(f32[32,4,128]{2,1,0:T(4,128)} %synthesis.1), calls=%async_computation | async-start | bytes 131072 | tf_op jit(solution)/shard_map/all_to_all | solution.py:666
  25.4 0.9 %collective-permute-done.8.odd_rows = f32[4,8,1152]{2,1,0:T(8,128)S(1)} collective-permute-done((f32[4,8,1152]{2,1,0:T(8,128)S(1)}, f32[4,8,1152]{2,1,0:T(8,128)S(1)}, u32[]{:S(2)}, u32[]{:S(2)}) %collective-permute-start.8) | collective-permute-done | bytes 147488 | tf_op jit(solution)/shard_map/ppermute | solution.py:626
  26.3 1.9 %windows.1 = (f32[80,1152]{1,0:T(8,128)S(1)}, f32[80,1152]{1,0:T(8,128)S(1)}, f32[80,1152]{1,0:T(8,128)S(1)}, f32[80,1152]{1,0:T(8,128)S(1)}, f32[80,1152]{1,0:T(8,128)S(1)}, /*index=5*/bf16[128,1152]{1,0:T(8,128)(2,1)S(1)}) custom-call(s32[32]{0:T(128)} %waves_hbm.3, f32[64,1080]{1,0:T(8,128)} %height_hbm.5, f32[64,1080]{1,0:T(8,128)} %east_hbm.5, ...), custom_call_target="tpu_custom_call" | custom-call | flops 99999997952 | bytes 400000000 | tf_op jit(solution)/shard_map/windows/pallas_call | solution.py:668
  28.2 4.5 %all-to-all-done.synth_ref = f32[32,4,128]{2,1,0:T(4,128)S(1)} async-done(((f32[32,4,128]{2,1,0:T(4,128)}), f32[32,4,128]{2,1,0:T(4,128)S(1)}, u32[]{:S(2)}, u32[]{:S(2)}) %all-to-all-start) | async-done | bytes 65568 | tf_op jit(solution)/shard_map/all_to_all | solution.py:666
  32.7 2.6 %substeps.1 = (f32[64,1080]{1,0:T(8,128)}, f32[64,1080]{1,0:T(8,128)}, f32[64,1080]{1,0:T(8,128)}, f32[64,1080]{1,0:T(8,128)}) custom-call(f32[32,4,128]{2,1,0:T(4,128)S(1)} %all-to-all-done.synth_ref, bf16[128,1152]{1,0:T(8,128)(2,1)S(1)} %get-tuple-element.36.harm_ref, f32[80,1152]{1,0:T(8,128)S(1)} %get-tuple-element.37.surface_win, ...), custom_call_target="tpu_custom_call" | custom-call | tf_op jit(solution)/shard_map/substeps/pallas_call | solution.py:685
  (5 shorter events, 0.0 us)
Async XLA Ops:
  2.4 1.4 %collective-permute-start = (f32[64,128]{1,0:T(8,128)S(1)}, f32[64,128]{1,0:T(8,128)S(1)}, u32[]{:S(2)}, u32[]{:S(2)}) collective-permute-start(f32[64,128]{1,0:T(8,128)S(1)} %get-tuple-element.25), channel_id=1, source_target_pairs={{0,1},{1,0},{2,3},{3,2},{4,5},{5,4},{6,7},{7,6},{8,9},{9,8},{10,11... | collective-permute-start | bytes 98312 | tf_op jit(solution)/shard_map/ppermute | solution.py:591
  3.8 8.7 %collective-permute-start.1 = (f32[40,128]{1,0:T(8,128)S(1)}, f32[40,128]{1,0:T(8,128)S(1)}, u32[]{:S(2)}, u32[]{:S(2)}) collective-permute-start(f32[40,128]{1,0:T(8,128)S(1)} %get-tuple-element.27), channel_id=1, source_target_pairs={{0,3},{1,2},{2,5},{3,4},{4,7},{5,6},{6,1},{7,0},{8,11},{9,10},{10,... | collective-permute-start | bytes 61448 | tf_op jit(solution)/shard_map/ppermute | solution.py:608
  6.4 6.0 %collective-permute-start.3 = (f32[40,128]{1,0:T(8,128)S(1)}, f32[40,128]{1,0:T(8,128)S(1)}, u32[]{:S(2)}, u32[]{:S(2)}) collective-permute-start(f32[40,128]{1,0:T(8,128)S(1)} %get-tuple-element.29), channel_id=1, source_target_pairs={{0,7},{1,6},{2,1},{3,0},{4,3},{5,2},{6,5},{7,4},{8,15},{9,14},{10,... | collective-permute-start | bytes 61448 | tf_op jit(solution)/shard_map/ppermute | solution.py:608
  8.5 3.9 %collective-permute-start.2 = (f32[8,128]{1,0:T(8,128)S(1)}, f32[8,128]{1,0:T(8,128)S(1)}, u32[]{:S(2)}, u32[]{:S(2)}) collective-permute-start(f32[8,128]{1,0:T(8,128)S(1)} %get-tuple-element.28), channel_id=1, source_target_pairs={{0,5},{1,4},{2,7},{3,6},{4,1},{5,0},{6,3},{7,2},{8,13},{9,12},{10,... | collective-permute-start | bytes 12296 | tf_op jit(solution)/shard_map/ppermute | solution.py:608
  9.2 12.0 %copy-start = (f32[2048]{0:T(1024)S(1)}, f32[2048]{0:T(1024)}, u32[]{:S(2)}) copy-start(f32[2048]{0:T(1024)} %param.11) | copy-start | bytes 24580
  13.0 8.1 %collective-permute-start.4 = (f32[8,2176]{1,0:T(8,128)S(1)}, f32[8,2176]{1,0:T(8,128)S(1)}, u32[]{:S(2)}, u32[]{:S(2)}) collective-permute-start(f32[8,2176]{1,0:T(8,128)S(1)} %get-tuple-element.32), channel_id=1, source_target_pairs={{0,8},{8,0},{16,24},{24,16},{1,9},{9,1},{17,25},{25,17},{2,10},{10... | collective-permute-start | bytes 208904 | tf_op jit(solution)/shard_map/ppermute | solution.py:643
  14.7 6.5 %collective-permute-start.5 = (f32[8,2176]{1,0:T(8,128)S(1)}, f32[8,2176]{1,0:T(8,128)S(1)}, u32[]{:S(2)}, u32[]{:S(2)}) collective-permute-start(f32[8,2176]{1,0:T(8,128)S(1)} %get-tuple-element.33), channel_id=1, source_target_pairs={{0,24},{8,16},{16,8},{24,0},{1,25},{9,17},{17,9},{25,1},{2,26},{10... | collective-permute-start | bytes 208904 | tf_op jit(solution)/shard_map/ppermute | solution.py:643
  16.2 5.0 %collective-permute-start.6 = (f32[8,2048]{1,0:T(8,128)S(1)}, f32[8,2048]{1,0:T(8,128)S(1)}, u32[]{:S(2)}, u32[]{:S(2)}) collective-permute-start(f32[8,2048]{1,0:T(8,128)S(1)} %get-tuple-element.31.refs_0_), channel_id=1, source_target_pairs={{0,16},{8,24},{16,0},{24,8},{1,17},{9,25},{17,1},{25,9},{2,18},{10... | collective-permute-start | bytes 196616 | tf_op jit(solution)/shard_map/ppermute | solution.py:643
  16.6 8.8 %collective-permute-start.7 = (f32[4,8,1152]{2,1,0:T(8,128)S(1)}, f32[4,8,1152]{2,1,0:T(8,128)S(1)}, u32[]{:S(2)}, u32[]{:S(2)}) collective-permute-start(f32[4,8,1152]{2,1,0:T(8,128)S(1)} %get-tuple-element.34), channel_id=1, source_target_pairs={{0,8},{16,24},{8,0},{24,16},{1,9},{17,25},{9,1},{25,17},{2,10},{18... | collective-permute-start | bytes 442376 | tf_op jit(solution)/shard_map/ppermute | solution.py:626
  18.2 8.1 %collective-permute-start.8 = (f32[4,8,1152]{2,1,0:T(8,128)S(1)}, f32[4,8,1152]{2,1,0:T(8,128)S(1)}, u32[]{:S(2)}, u32[]{:S(2)}) collective-permute-start(f32[4,8,1152]{2,1,0:T(8,128)S(1)} %get-tuple-element.35), channel_id=1, source_target_pairs={{8,16},{24,0},{16,8},{0,24},{9,17},{25,1},{17,9},{1,25},{10,18},{2... | collective-permute-start | bytes 442376 | tf_op jit(solution)/shard_map/ppermute | solution.py:626
  22.3 10.4 %all-to-all-start = ((f32[32,4,128]{2,1,0:T(4,128)}), f32[32,4,128]{2,1,0:T(4,128)S(1)}, u32[]{:S(2)}, u32[]{:S(2)}) async-start(f32[32,4,128]{2,1,0:T(4,128)} %synthesis.1), calls=%async_computation | async-start | bytes 131072 | tf_op jit(solution)/shard_map/all_to_all | solution.py:666

commit v7 on v6

--- a/solution.py
+++ b/solution.py
@@ -643,7 +643,7 @@
             lax.ppermute(block, "lat", [(i, i ^ step) for i in range(bands)])
             for block, step in ((corners[0], 1), (corners[1], 3), (spectral, 2))
         ]
-        pieces = [spectral, *corners, across]
+        pieces = [spectral, corners[1], corners[0], across]
     else:
         corners = [
             lax.ppermute(block, "lat", pairs) for block, pairs in zip(corners, links)

time: 35.5 us -> 35.2 us (level)
  waiting for transfers between devices: 9.2 us -> 8.75 us
    ppermute x3, waiting for transfers between devices: 1.48 us -> 1.03 us  [shards(): lax.ppermute(block, 'lat', [(i, i ^ step) for i in range(bands)])]
  transfers between devices with their start and end apart: 10 -> 10, of which waited for: 5 -> 6; matrix products, arithmetic and copies ran while one was open for 0% -> 0% of each run, Pallas kernels for 14% -> 14%
where the time goes in v7:
time: 35.2 us; the launch traced here: 35 us
  starting transfers between devices  15.7 us (45%)
  Pallas kernels  9.8 us (28%)
  waiting for transfers between devices  8.75 us (25%)
  between operations  0.68 us (2%)
    ppermute x3, starting transfers between devices, shards(): arrived.append(lax.ppermute(block, 'lon', across))  5.44 us
    all_to_all x1, waiting for transfers between devices, shards(): everyone = lax.all_to_all(synth, ('lat', 'lon'), 0, 0, tiled=True)  4.24 us
    ppermute x3, starting transfers between devices, shards(): lax.ppermute(block, 'lat', [(i, i ^ step) for i in range(bands)])  3.55 us
    all_to_all x1, starting transfers between devices, shards(): everyone = lax.all_to_all(synth, ('lat', 'lon'), 0, 0, tiled=True)  3.11 us
    ppermute x2, starting transfers between devices, shards(): lax.ppermute(block, 'lat', pairs)  3.11 us
    pallas_call x1, Pallas kernels, shards(): pl.pallas_call(functools.partial(substep_kernel, sectors, bands), out_sha...  2.58 us
    pallas_call x1, Pallas kernels, shards(): pl.pallas_call(functools.partial(windows_kernel, period, slots, chips, ba...  1.89 us
    pallas_call x1, Pallas kernels, shards(): pl.pallas_call(stage_kernel, out_shape=[struct((4, MARGIN, width))] * 2 +...  1.86 us
  transfers between devices with their start and end apart: 10, of which 6 were waited for; matrix products, arithmetic and copies ran while one was open for 0% of the time, Pallas kernels for 14%

profile of v7, /device:TPU:0, one launch (start us, length us, event | category | flops | bytes accessed | tf_op | source)
XLA Modules:
  0.0 35.0 jit_solution(7214445036957406745)
XLA Ops:
  0.6 1.7 %transform.1 = (f32[4,8,128]{2,1,0:T(8,128)S(1)}, f32[64,128]{1,0:T(8,128)S(1)}, f32[32,128]{1,0:T(8,128)S(1)}) custom-call(s32[32]{0:T(128)} %waves_hbm.3, f32[64,1080]{1,0:T(8,128)} %height_hbm.5, f32[64,1080]{1,0:T(8,128)} %east_hbm.5, f32[64,1080]{1,0:T(8,128)} %north_hbm.5, s32[64,1080]{1,0:T(8,128)} %land_hbm.5), custom_call_target="tpu_custom_call" | custom-call | tf_op jit(solution)/shard_map/transform/pallas_call | solution.py:568
  2.4 0.5 %collective-permute-start = (f32[64,128]{1,0:T(8,128)S(1)}, f32[64,128]{1,0:T(8,128)S(1)}, u32[]{:S(2)}, u32[]{:S(2)}) collective-permute-start(f32[64,128]{1,0:T(8,128)S(1)} %get-tuple-element.25), channel_id=1, source_target_pairs={{0,1},{1,0},{2,3},{3,2},{4,5},{5,4},{6,7},{7,6},{8,9},{9,8},{10,11... | collective-permute-start | bytes 98312 | tf_op jit(solution)/shard_map/ppermute | solution.py:591
  2.9 0.9 %collective-permute-done.recv_ref.refs_4_.core_ref = f32[64,128]{1,0:T(8,128)S(1)} collective-permute-done((f32[64,128]{1,0:T(8,128)S(1)}, f32[64,128]{1,0:T(8,128)S(1)}, u32[]{:S(2)}, u32[]{:S(2)}) %collective-permute-start) | collective-permute-done | bytes 32800 | tf_op jit(solution)/shard_map/ppermute | solution.py:591
  3.8 2.7 %collective-permute-start.1 = (f32[40,128]{1,0:T(8,128)S(1)}, f32[40,128]{1,0:T(8,128)S(1)}, u32[]{:S(2)}, u32[]{:S(2)}) collective-permute-start(f32[40,128]{1,0:T(8,128)S(1)} %get-tuple-element.27), channel_id=1, source_target_pairs={{0,3},{1,2},{2,5},{3,4},{4,7},{5,6},{6,1},{7,0},{8,11},{9,10},{10,... | collective-permute-start | bytes 61448 | tf_op jit(solution)/shard_map/ppermute | solution.py:608
  6.4 2.1 %collective-permute-start.3 = (f32[40,128]{1,0:T(8,128)S(1)}, f32[40,128]{1,0:T(8,128)S(1)}, u32[]{:S(2)}, u32[]{:S(2)}) collective-permute-start(f32[40,128]{1,0:T(8,128)S(1)} %get-tuple-element.29), channel_id=1, source_target_pairs={{0,7},{1,6},{2,1},{3,0},{4,3},{5,2},{6,5},{7,4},{8,15},{9,14},{10,... | collective-permute-start | bytes 61448 | tf_op jit(solution)/shard_map/ppermute | solution.py:608
  8.5 0.7 %collective-permute-start.2 = (f32[8,128]{1,0:T(8,128)S(1)}, f32[8,128]{1,0:T(8,128)S(1)}, u32[]{:S(2)}, u32[]{:S(2)}) collective-permute-start(f32[8,128]{1,0:T(8,128)S(1)} %get-tuple-element.28), channel_id=1, source_target_pairs={{0,5},{1,4},{2,7},{3,6},{4,1},{5,0},{6,3},{7,2},{8,13},{9,12},{10,... | collective-permute-start | bytes 12296 | tf_op jit(solution)/shard_map/ppermute | solution.py:608
  9.2 1.9 %stage.1 = (f32[4,8,1152]{2,1,0:T(8,128)S(1)}, f32[4,8,1152]{2,1,0:T(8,128)S(1)}, f32[4,64,2048]{2,1,0:T(8,128)S(1)}) custom-call(f32[8,128]{1,0:T(8,128)S(1)} %get-tuple-element.26.after_ref.refs_0_, f32[64,1080]{1,0:T(8,128)} %height_hbm.5, f32[64,1080]{1,0:T(8,128)} %east_hbm.5, f32[64,1080]{1,0:T(8,128)} %north_hbm.5, s32[64,1080]{1,0:T(8,128)} %land_hbm.5, ...), custom_call_target="tpu_custom_call" | custom-call | tf_op jit(solution)/shard_map/stage/pallas_call | solution.py:611
  11.1 1.4 %collective-permute-done.2.refs_2_ = f32[8,128]{1,0:T(8,128)S(1)} collective-permute-done((f32[8,128]{1,0:T(8,128)S(1)}, f32[8,128]{1,0:T(8,128)S(1)}, u32[]{:S(2)}, u32[]{:S(2)}) %collective-permute-start.2) | collective-permute-done | bytes 4128 | tf_op jit(solution)/shard_map/ppermute | solution.py:608
  12.5 0.0 collective-permute-done.1.refs_1_.west_ref
  12.5 0.0 collective-permute-done.3.refs_3_.east_ref
  12.5 0.6 %analysis.1 = (f32[8,2048]{1,0:T(8,128)S(1)}, f32[8,2176]{1,0:T(8,128)S(1)}, f32[8,2176]{1,0:T(8,128)S(1)}) custom-call(f32[8,128]{1,0:T(8,128)S(1)} %get-tuple-element.26.after_ref.refs_0_, f32[40,128]{1,0:T(8,128)S(1)} %collective-permute-done.1.refs_1_.west_ref, f32[8,128]{1,0:T(8,128)S(1)} %collective-permute-done.2.refs_2_, ...), custom_call_target="tpu_custom_call" | custom-call | tf_op jit(solution)/shard_map/analysis/pallas_call | solution.py:633
  13.0 2.6 %collective-permute-start.4 = (f32[8,2176]{1,0:T(8,128)S(1)}, f32[8,2176]{1,0:T(8,128)S(1)}, u32[]{:S(2)}, u32[]{:S(2)}) collective-permute-start(f32[8,2176]{1,0:T(8,128)S(1)} %get-tuple-element.32), channel_id=1, source_target_pairs={{0,24},{8,16},{16,8},{24,0},{1,25},{9,17},{17,9},{25,1},{2,26},{10... | collective-permute-start | bytes 208904 | tf_op jit(solution)/shard_map/ppermute | solution.py:643
  15.7 0.5 %collective-permute-start.5 = (f32[8,2176]{1,0:T(8,128)S(1)}, f32[8,2176]{1,0:T(8,128)S(1)}, u32[]{:S(2)}, u32[]{:S(2)}) collective-permute-start(f32[8,2176]{1,0:T(8,128)S(1)} %get-tuple-element.33), channel_id=1, source_target_pairs={{0,8},{8,0},{16,24},{24,16},{1,9},{9,1},{17,25},{25,17},{2,10},{10... | collective-permute-start | bytes 208904 | tf_op jit(solution)/shard_map/ppermute | solution.py:643
  16.2 0.4 %collective-permute-start.6 = (f32[8,2048]{1,0:T(8,128)S(1)}, f32[8,2048]{1,0:T(8,128)S(1)}, u32[]{:S(2)}, u32[]{:S(2)}) collective-permute-start(f32[8,2048]{1,0:T(8,128)S(1)} %get-tuple-element.31.refs_0_), channel_id=1, source_target_pairs={{0,16},{8,24},{16,0},{24,8},{1,17},{9,25},{17,1},{25,9},{2,18},{10... | collective-permute-start | bytes 196616 | tf_op jit(solution)/shard_map/ppermute | solution.py:643
  16.6 1.6 %collective-permute-start.7 = (f32[4,8,1152]{2,1,0:T(8,128)S(1)}, f32[4,8,1152]{2,1,0:T(8,128)S(1)}, u32[]{:S(2)}, u32[]{:S(2)}) collective-permute-start(f32[4,8,1152]{2,1,0:T(8,128)S(1)} %get-tuple-element.34), channel_id=1, source_target_pairs={{0,8},{16,24},{8,0},{24,16},{1,9},{17,25},{9,1},{25,17},{2,10},{18... | collective-permute-start | bytes 442376 | tf_op jit(solution)/shard_map/ppermute | solution.py:626
  18.2 1.5 %collective-permute-start.8 = (f32[4,8,1152]{2,1,0:T(8,128)S(1)}, f32[4,8,1152]{2,1,0:T(8,128)S(1)}, u32[]{:S(2)}, u32[]{:S(2)}) collective-permute-start(f32[4,8,1152]{2,1,0:T(8,128)S(1)} %get-tuple-element.35), channel_id=1, source_target_pairs={{8,16},{24,0},{16,8},{0,24},{9,17},{25,1},{17,9},{1,25},{10,18},{2... | collective-permute-start | bytes 442376 | tf_op jit(solution)/shard_map/ppermute | solution.py:626
  19.7 0.8 %collective-permute-done.6.refs_3_ = f32[8,2048]{1,0:T(8,128)S(1)} collective-permute-done((f32[8,2048]{1,0:T(8,128)S(1)}, f32[8,2048]{1,0:T(8,128)S(1)}, u32[]{:S(2)}, u32[]{:S(2)}) %collective-permute-start.6) | collective-permute-done | bytes 65568 | tf_op jit(solution)/shard_map/ppermute | solution.py:643
  20.5 0.3 collective-permute-done.5.refs_2_.even_ref
  20.7 1.2 %synthesis.1 = f32[32,4,128]{2,1,0:T(4,128)} custom-call(f32[8,2048]{1,0:T(8,128)S(1)} %get-tuple-element.31.refs_0_, f32[8,2176]{1,0:T(8,128)S(1)} %collective-permute-done.4.refs_1_.odd_ref, f32[8,2176]{1,0:T(8,128)S(1)} %collective-permute-done.5.refs_2_.even_ref, f32[8,2048]{1,0:T(8,128)S(1)} %collective-permute-done.6.refs_3_, f32[1,2048]{1,0:T(1,128)S(1)} %bitcast.1, ...), custom_call_target="tpu_custom_call" | custom-call | flops 99999997952 | bytes 400000000 | tf_op jit(solution)/shard_map/synthesis/pallas_call | solution.py:656
  21.9 3.1 %all-to-all-start = ((f32[32,4,128]{2,1,0:T(4,128)}), f32[32,4,128]{2,1,0:T(4,128)S(1)}, u32[]{:S(2)}, u32[]{:S(2)}) async-start(f32[32,4,128]{2,1,0:T(4,128)} %synthesis.1), calls=%async_computation | async-start | bytes 131072 | tf_op jit(solution)/shard_map/all_to_all | solution.py:666
  25.0 1.2 %collective-permute-done.8.odd_rows = f32[4,8,1152]{2,1,0:T(8,128)S(1)} collective-permute-done((f32[4,8,1152]{2,1,0:T(8,128)S(1)}, f32[4,8,1152]{2,1,0:T(8,128)S(1)}, u32[]{:S(2)}, u32[]{:S(2)}) %collective-permute-start.8) | collective-permute-done | bytes 147488 | tf_op jit(solution)/shard_map/ppermute | solution.py:626
  26.2 1.9 %windows.1 = (f32[80,1152]{1,0:T(8,128)S(1)}, f32[80,1152]{1,0:T(8,128)S(1)}, f32[80,1152]{1,0:T(8,128)S(1)}, f32[80,1152]{1,0:T(8,128)S(1)}, f32[80,1152]{1,0:T(8,128)S(1)}, /*index=5*/bf16[128,1152]{1,0:T(8,128)(2,1)S(1)}) custom-call(s32[32]{0:T(128)} %waves_hbm.3, f32[64,1080]{1,0:T(8,128)} %height_hbm.5, f32[64,1080]{1,0:T(8,128)} %east_hbm.5, ...), custom_call_target="tpu_custom_call" | custom-call | flops 99999997952 | bytes 400000000 | tf_op jit(solution)/shard_map/windows/pallas_call | solution.py:668
  28.1 4.2 %all-to-all-done.synth_ref = f32[32,4,128]{2,1,0:T(4,128)S(1)} async-done(((f32[32,4,128]{2,1,0:T(4,128)}), f32[32,4,128]{2,1,0:T(4,128)S(1)}, u32[]{:S(2)}, u32[]{:S(2)}) %all-to-all-start) | async-done | bytes 65568 | tf_op jit(solution)/shard_map/all_to_all | solution.py:666
  32.4 2.6 %substeps.1 = (f32[64,1080]{1,0:T(8,128)}, f32[64,1080]{1,0:T(8,128)}, f32[64,1080]{1,0:T(8,128)}, f32[64,1080]{1,0:T(8,128)}) custom-call(f32[32,4,128]{2,1,0:T(4,128)S(1)} %all-to-all-done.synth_ref, bf16[128,1152]{1,0:T(8,128)(2,1)S(1)} %get-tuple-element.36.harm_ref, f32[80,1152]{1,0:T(8,128)S(1)} %get-tuple-element.37.surface_win, ...), custom_call_target="tpu_custom_call" | custom-call | tf_op jit(solution)/shard_map/substeps/pallas_call | solution.py:685
  (5 shorter events, 0.0 us)
Async XLA Ops:
  2.4 1.4 %collective-permute-start = (f32[64,128]{1,0:T(8,128)S(1)}, f32[64,128]{1,0:T(8,128)S(1)}, u32[]{:S(2)}, u32[]{:S(2)}) collective-permute-start(f32[64,128]{1,0:T(8,128)S(1)} %get-tuple-element.25), channel_id=1, source_target_pairs={{0,1},{1,0},{2,3},{3,2},{4,5},{5,4},{6,7},{7,6},{8,9},{9,8},{10,11... | collective-permute-start | bytes 98312 | tf_op jit(solution)/shard_map/ppermute | solution.py:591
  3.8 8.7 %collective-permute-start.1 = (f32[40,128]{1,0:T(8,128)S(1)}, f32[40,128]{1,0:T(8,128)S(1)}, u32[]{:S(2)}, u32[]{:S(2)}) collective-permute-start(f32[40,128]{1,0:T(8,128)S(1)} %get-tuple-element.27), channel_id=1, source_target_pairs={{0,3},{1,2},{2,5},{3,4},{4,7},{5,6},{6,1},{7,0},{8,11},{9,10},{10,... | collective-permute-start | bytes 61448 | tf_op jit(solution)/shard_map/ppermute | solution.py:608
  6.4 6.0 %collective-permute-start.3 = (f32[40,128]{1,0:T(8,128)S(1)}, f32[40,128]{1,0:T(8,128)S(1)}, u32[]{:S(2)}, u32[]{:S(2)}) collective-permute-start(f32[40,128]{1,0:T(8,128)S(1)} %get-tuple-element.29), channel_id=1, source_target_pairs={{0,7},{1,6},{2,1},{3,0},{4,3},{5,2},{6,5},{7,4},{8,15},{9,14},{10,... | collective-permute-start | bytes 61448 | tf_op jit(solution)/shard_map/ppermute | solution.py:608
  8.5 3.9 %collective-permute-start.2 = (f32[8,128]{1,0:T(8,128)S(1)}, f32[8,128]{1,0:T(8,128)S(1)}, u32[]{:S(2)}, u32[]{:S(2)}) collective-permute-start(f32[8,128]{1,0:T(8,128)S(1)} %get-tuple-element.28), channel_id=1, source_target_pairs={{0,5},{1,4},{2,7},{3,6},{4,1},{5,0},{6,3},{7,2},{8,13},{9,12},{10,... | collective-permute-start | bytes 12296 | tf_op jit(solution)/shard_map/ppermute | solution.py:608
  9.2 11.5 %copy-start = (f32[2048]{0:T(1024)S(1)}, f32[2048]{0:T(1024)}, u32[]{:S(2)}) copy-start(f32[2048]{0:T(1024)} %param.11) | copy-start | bytes 24580
  13.0 7.4 %collective-permute-start.4 = (f32[8,2176]{1,0:T(8,128)S(1)}, f32[8,2176]{1,0:T(8,128)S(1)}, u32[]{:S(2)}, u32[]{:S(2)}) collective-permute-start(f32[8,2176]{1,0:T(8,128)S(1)} %get-tuple-element.32), channel_id=1, source_target_pairs={{0,24},{8,16},{16,8},{24,0},{1,25},{9,17},{17,9},{25,1},{2,26},{10... | collective-permute-start | bytes 208904 | tf_op jit(solution)/shard_map/ppermute | solution.py:643
  15.7 5.1 %collective-permute-start.5 = (f32[8,2176]{1,0:T(8,128)S(1)}, f32[8,2176]{1,0:T(8,128)S(1)}, u32[]{:S(2)}, u32[]{:S(2)}) collective-permute-start(f32[8,2176]{1,0:T(8,128)S(1)} %get-tuple-element.33), channel_id=1, source_target_pairs={{0,8},{8,0},{16,24},{24,16},{1,9},{9,1},{17,25},{25,17},{2,10},{10... | collective-permute-start | bytes 208904 | tf_op jit(solution)/shard_map/ppermute | solution.py:643
  16.2 4.3 %collective-permute-start.6 = (f32[8,2048]{1,0:T(8,128)S(1)}, f32[8,2048]{1,0:T(8,128)S(1)}, u32[]{:S(2)}, u32[]{:S(2)}) collective-permute-start(f32[8,2048]{1,0:T(8,128)S(1)} %get-tuple-element.31.refs_0_), channel_id=1, source_target_pairs={{0,16},{8,24},{16,0},{24,8},{1,17},{9,25},{17,1},{25,9},{2,18},{10... | collective-permute-start | bytes 196616 | tf_op jit(solution)/shard_map/ppermute | solution.py:643
  16.6 8.4 %collective-permute-start.7 = (f32[4,8,1152]{2,1,0:T(8,128)S(1)}, f32[4,8,1152]{2,1,0:T(8,128)S(1)}, u32[]{:S(2)}, u32[]{:S(2)}) collective-permute-start(f32[4,8,1152]{2,1,0:T(8,128)S(1)} %get-tuple-element.34), channel_id=1, source_target_pairs={{0,8},{16,24},{8,0},{24,16},{1,9},{17,25},{9,1},{25,17},{2,10},{18... | collective-permute-start | bytes 442376 | tf_op jit(solution)/shard_map/ppermute | solution.py:626
  18.2 8.0 %collective-permute-start.8 = (f32[4,8,1152]{2,1,0:T(8,128)S(1)}, f32[4,8,1152]{2,1,0:T(8,128)S(1)}, u32[]{:S(2)}, u32[]{:S(2)}) collective-permute-start(f32[4,8,1152]{2,1,0:T(8,128)S(1)} %get-tuple-element.35), channel_id=1, source_target_pairs={{8,16},{24,0},{16,8},{0,24},{9,17},{25,1},{17,9},{1,25},{10,18},{2... | collective-permute-start | bytes 442376 | tf_op jit(solution)/shard_map/ppermute | solution.py:626
  21.9 10.5 %all-to-all-start = ((f32[32,4,128]{2,1,0:T(4,128)}), f32[32,4,128]{2,1,0:T(4,128)S(1)}, u32[]{:S(2)}, u32[]{:S(2)}) async-start(f32[32,4,128]{2,1,0:T(4,128)} %synthesis.1), calls=%async_computation | async-start | bytes 131072 | tf_op jit(solution)/shard_map/all_to_all | solution.py:666

commit v8 on v7

--- a/solution.py
+++ b/solution.py
@@ -34,10 +34,14 @@
     return hi, lo
 
 
+def chip_at(chip, shift, chips):
+    return chip ^ shift if chips == 4 else (chip + shift) % chips
+
+
 def owner(me, sectors, core, shift):
-    chips = sectors // 2
     crossed = core if shift == 0 else 1 - core
-    return 2 * lax.rem(me // 2 + shift, chips) + lax.bitwise_xor(lax.rem(me, 2), crossed)
+    chip = chip_at(me // 2, shift, sectors // 2)
+    return 2 * chip + lax.bitwise_xor(lax.rem(me, 2), crossed)
 
 
 def row_groups(sectors):
@@ -313,8 +317,12 @@
 def side_tiles(me, group, chips, core_ref, west_ref, east_ref):
     first = lax.rem(me, 2) == 0
     other = core_ref[chips * group :]
-    left = jnp.where(first, west_ref[group:], other)
-    right = jnp.where(first, other, east_ref[group:])
+    west, east = west_ref[group:], east_ref[group:]
+    if chips == 4:
+        even = lax.rem(me // 2, 2) == 0
+        west, east = jnp.where(even, east, west), jnp.where(even, west, east)
+    left = jnp.where(first, west, other)
+    right = jnp.where(first, other, east)
     return left, right
 
 
@@ -485,13 +493,11 @@
             jnp.concatenate(interleaved(column.at[at], step), axis=0)[:, : waves // 2]
         )
     hi, lo = split2(jnp.concatenate(pieces, axis=1))
-    left = jnp.concatenate(
-        [jnp.concatenate([hi, hi], axis=1), jnp.concatenate([lo, lo], axis=1)], axis=0
+    columns = (((1,), (0,)), ((), ()))
+    both = lax.dot_general(
+        jnp.concatenate([hi, hi], axis=1), harm_ref[...], columns, preferred_element_type=f32
     )
-    both = lax.dot_general(
-        left, harm_ref[...], (((1,), (0,)), ((), ())), preferred_element_type=f32
-    )
-    both = both[:taller] + both[taller:]
+    both = both + lax.dot_general(lo, harm_ref[:waves], columns, preferred_element_type=f32)
     load[...] = both
     pressure[...] = surface_win[...] - both
     copies = [
@@ -604,7 +610,9 @@
     )(keep, tile, core)
     arrived = []
     for shift, block in enumerate(outgoing, 1):
-        across = [(i, 2 * ((i // 2 + shift) % chips) + 1 - i % 2) for i in range(sectors)]
+        across = [
+            (i, 2 * chip_at(i // 2, shift, chips) + 1 - i % 2) for i in range(sectors)
+        ]
         arrived.append(lax.ppermute(block, "lon", across))
     sides = (core, arrived[0], arrived[-1])
 

time: 35.2 us -> 35 us (level)
  starting transfers between devices: 15.7 us -> 15 us
  waiting for transfers between devices: 8.75 us -> 9.35 us
    ppermute x3, waiting for transfers between devices: 1.39 us -> 1.95 us  [shards(): arrived.append(lax.ppermute(block, 'lon', across))]
    all_to_all x1, starting transfers between devices: 3.11 us -> 2.68 us  [shards(): everyone = lax.all_to_all(synth, ('lat', 'lon'), 0, 0, tiled=True)]
    ppermute x2, waiting for transfers between devices: 1.23 us -> 1.63 us  [shards(): lax.ppermute(block, 'lat', pairs)]
    all_to_all x1, waiting for transfers between devices: 4.24 us -> 3.85 us  [shards(): everyone = lax.all_to_all(synth, ('lat', 'lon'), 0, 0, tiled=True)]
where the time goes in v8:
time: 35 us; the launch traced here: 34.8 us
  starting transfers between devices  15 us (43%)
  Pallas kernels  9.77 us (28%)
  waiting for transfers between devices  9.35 us (27%)
  between operations  0.68 us (2%)
    ppermute x3, starting transfers between devices, shards(): arrived.append(lax.ppermute(block, 'lon', across))  5.23 us
    all_to_all x1, waiting for transfers between devices, shards(): everyone = lax.all_to_all(synth, ('lat', 'lon'), 0, 0, tiled=True)  3.85 us
    ppermute x3, starting transfers between devices, shards(): lax.ppermute(block, 'lat', [(i, i ^ step) for i in range(bands)])  3.55 us
    ppermute x2, starting transfers between devices, shards(): lax.ppermute(block, 'lat', pairs)  2.98 us
    all_to_all x1, starting transfers between devices, shards(): everyone = lax.all_to_all(synth, ('lat', 'lon'), 0, 0, tiled=True)  2.68 us
    pallas_call x1, Pallas kernels, shards(): pl.pallas_call(functools.partial(substep_kernel, sectors, bands), out_sha...  2.56 us
    ppermute x3, waiting for transfers between devices, shards(): arrived.append(lax.ppermute(block, 'lon', across))  1.95 us
    pallas_call x1, Pallas kernels, shards(): pl.pallas_call(functools.partial(windows_kernel, period, slots, chips, ba...  1.89 us
  transfers between devices with their start and end apart: 10, of which 6 were waited for; matrix products, arithmetic and copies ran while one was open for 0% of the time, Pallas kernels for 14%

profile of v8, /device:TPU:0, one launch (start us, length us, event | category | flops | bytes accessed | tf_op | source)
XLA Modules:
  0.0 34.8 jit_solution(637191195722139142)
XLA Ops:
  0.6 1.7 %transform.1 = (f32[4,8,128]{2,1,0:T(8,128)S(1)}, f32[64,128]{1,0:T(8,128)S(1)}, f32[32,128]{1,0:T(8,128)S(1)}) custom-call(s32[32]{0:T(128)} %waves_hbm.3, f32[64,1080]{1,0:T(8,128)} %height_hbm.5, f32[64,1080]{1,0:T(8,128)} %east_hbm.5, f32[64,1080]{1,0:T(8,128)} %north_hbm.5, s32[64,1080]{1,0:T(8,128)} %land_hbm.5), custom_call_target="tpu_custom_call" | custom-call | tf_op jit(solution)/shard_map/transform/pallas_call | solution.py:574
  2.4 0.5 %collective-permute-start = (f32[64,128]{1,0:T(8,128)S(1)}, f32[64,128]{1,0:T(8,128)S(1)}, u32[]{:S(2)}, u32[]{:S(2)}) collective-permute-start(f32[64,128]{1,0:T(8,128)S(1)} %get-tuple-element.25), channel_id=1, source_target_pairs={{0,1},{1,0},{2,3},{3,2},{4,5},{5,4},{6,7},{7,6},{8,9},{9,8},{10,11... | collective-permute-start | bytes 98312 | tf_op jit(solution)/shard_map/ppermute | solution.py:597
  2.9 0.9 %collective-permute-done.recv_ref.refs_4_.core_ref = f32[64,128]{1,0:T(8,128)S(1)} collective-permute-done((f32[64,128]{1,0:T(8,128)S(1)}, f32[64,128]{1,0:T(8,128)S(1)}, u32[]{:S(2)}, u32[]{:S(2)}) %collective-permute-start) | collective-permute-done | bytes 32800 | tf_op jit(solution)/shard_map/ppermute | solution.py:597
  3.8 2.7 %collective-permute-start.1 = (f32[40,128]{1,0:T(8,128)S(1)}, f32[40,128]{1,0:T(8,128)S(1)}, u32[]{:S(2)}, u32[]{:S(2)}) collective-permute-start(f32[40,128]{1,0:T(8,128)S(1)} %get-tuple-element.27), channel_id=1, source_target_pairs={{0,3},{1,2},{2,1},{3,0},{4,7},{5,6},{6,5},{7,4},{8,11},{9,10},{10,... | collective-permute-start | bytes 61448 | tf_op jit(solution)/shard_map/ppermute | solution.py:616
  6.4 2.4 %collective-permute-start.3 = (f32[40,128]{1,0:T(8,128)S(1)}, f32[40,128]{1,0:T(8,128)S(1)}, u32[]{:S(2)}, u32[]{:S(2)}) collective-permute-start(f32[40,128]{1,0:T(8,128)S(1)} %get-tuple-element.29), channel_id=1, source_target_pairs={{0,7},{1,6},{2,5},{3,4},{4,3},{5,2},{6,1},{7,0},{8,15},{9,14},{10,... | collective-permute-start | bytes 61448 | tf_op jit(solution)/shard_map/ppermute | solution.py:616
  8.9 0.1 collective-permute-start.2
  9.0 1.9 %stage.1 = (f32[4,8,1152]{2,1,0:T(8,128)S(1)}, f32[4,8,1152]{2,1,0:T(8,128)S(1)}, f32[4,64,2048]{2,1,0:T(8,128)S(1)}) custom-call(f32[8,128]{1,0:T(8,128)S(1)} %get-tuple-element.26.after_ref.refs_0_, f32[64,1080]{1,0:T(8,128)} %height_hbm.5, f32[64,1080]{1,0:T(8,128)} %east_hbm.5, f32[64,1080]{1,0:T(8,128)} %north_hbm.5, s32[64,1080]{1,0:T(8,128)} %land_hbm.5, ...), custom_call_target="tpu_custom_call" | custom-call | tf_op jit(solution)/shard_map/stage/pallas_call | solution.py:619
  10.8 1.9 %collective-permute-done.2.refs_2_ = f32[8,128]{1,0:T(8,128)S(1)} collective-permute-done((f32[8,128]{1,0:T(8,128)S(1)}, f32[8,128]{1,0:T(8,128)S(1)}, u32[]{:S(2)}, u32[]{:S(2)}) %collective-permute-start.2) | collective-permute-done | bytes 4128 | tf_op jit(solution)/shard_map/ppermute | solution.py:616
  12.8 0.6 %analysis.1 = (f32[8,2048]{1,0:T(8,128)S(1)}, f32[8,2176]{1,0:T(8,128)S(1)}, f32[8,2176]{1,0:T(8,128)S(1)}) custom-call(f32[8,128]{1,0:T(8,128)S(1)} %get-tuple-element.26.after_ref.refs_0_, f32[40,128]{1,0:T(8,128)S(1)} %collective-permute-done.1.refs_1_.west_ref, f32[8,128]{1,0:T(8,128)S(1)} %collective-permute-done.2.refs_2_, ...), custom_call_target="tpu_custom_call" | custom-call | tf_op jit(solution)/shard_map/analysis/pallas_call | solution.py:641
  13.4 2.5 %collective-permute-start.4 = (f32[8,2176]{1,0:T(8,128)S(1)}, f32[8,2176]{1,0:T(8,128)S(1)}, u32[]{:S(2)}, u32[]{:S(2)}) collective-permute-start(f32[8,2176]{1,0:T(8,128)S(1)} %get-tuple-element.32), channel_id=1, source_target_pairs={{0,24},{8,16},{16,8},{24,0},{1,25},{9,17},{17,9},{25,1},{2,26},{10... | collective-permute-start | bytes 208904 | tf_op jit(solution)/shard_map/ppermute | solution.py:651
  15.9 0.5 %collective-permute-start.5 = (f32[8,2176]{1,0:T(8,128)S(1)}, f32[8,2176]{1,0:T(8,128)S(1)}, u32[]{:S(2)}, u32[]{:S(2)}) collective-permute-start(f32[8,2176]{1,0:T(8,128)S(1)} %get-tuple-element.33), channel_id=1, source_target_pairs={{0,8},{8,0},{16,24},{24,16},{1,9},{9,1},{17,25},{25,17},{2,10},{10... | collective-permute-start | bytes 208904 | tf_op jit(solution)/shard_map/ppermute | solution.py:651
  16.4 0.5 %collective-permute-start.6 = (f32[8,2048]{1,0:T(8,128)S(1)}, f32[8,2048]{1,0:T(8,128)S(1)}, u32[]{:S(2)}, u32[]{:S(2)}) collective-permute-start(f32[8,2048]{1,0:T(8,128)S(1)} %get-tuple-element.31.refs_0_), channel_id=1, source_target_pairs={{0,16},{8,24},{16,0},{24,8},{1,17},{9,25},{17,1},{25,9},{2,18},{10... | collective-permute-start | bytes 196616 | tf_op jit(solution)/shard_map/ppermute | solution.py:651
  16.9 1.5 %collective-permute-start.7 = (f32[4,8,1152]{2,1,0:T(8,128)S(1)}, f32[4,8,1152]{2,1,0:T(8,128)S(1)}, u32[]{:S(2)}, u32[]{:S(2)}) collective-permute-start(f32[4,8,1152]{2,1,0:T(8,128)S(1)} %get-tuple-element.34), channel_id=1, source_target_pairs={{0,8},{16,24},{8,0},{24,16},{1,9},{17,25},{9,1},{25,17},{2,10},{18... | collective-permute-start | bytes 442376 | tf_op jit(solution)/shard_map/ppermute | solution.py:634
  18.4 1.5 %collective-permute-start.8 = (f32[4,8,1152]{2,1,0:T(8,128)S(1)}, f32[4,8,1152]{2,1,0:T(8,128)S(1)}, u32[]{:S(2)}, u32[]{:S(2)}) collective-permute-start(f32[4,8,1152]{2,1,0:T(8,128)S(1)} %get-tuple-element.35), channel_id=1, source_target_pairs={{8,16},{24,0},{16,8},{0,24},{9,17},{25,1},{17,9},{1,25},{10,18},{2... | collective-permute-start | bytes 442376 | tf_op jit(solution)/shard_map/ppermute | solution.py:634
  19.9 0.8 %collective-permute-done.6.refs_3_ = f32[8,2048]{1,0:T(8,128)S(1)} collective-permute-done((f32[8,2048]{1,0:T(8,128)S(1)}, f32[8,2048]{1,0:T(8,128)S(1)}, u32[]{:S(2)}, u32[]{:S(2)}) %collective-permute-start.6) | collective-permute-done | bytes 65568 | tf_op jit(solution)/shard_map/ppermute | solution.py:651
  20.7 0.0 collective-permute-done.4.refs_1_.odd_ref
  20.7 0.3 collective-permute-done.5.refs_2_.even_ref
  21.0 1.2 %synthesis.1 = f32[32,4,128]{2,1,0:T(4,128)} custom-call(f32[8,2048]{1,0:T(8,128)S(1)} %get-tuple-element.31.refs_0_, f32[8,2176]{1,0:T(8,128)S(1)} %collective-permute-done.4.refs_1_.odd_ref, f32[8,2176]{1,0:T(8,128)S(1)} %collective-permute-done.5.refs_2_.even_ref, f32[8,2048]{1,0:T(8,128)S(1)} %collective-permute-done.6.refs_3_, f32[1,2048]{1,0:T(1,128)S(1)} %bitcast.1, ...), custom_call_target="tpu_custom_call" | custom-call | flops 99999997952 | bytes 400000000 | tf_op jit(solution)/shard_map/synthesis/pallas_call | solution.py:664
  22.1 2.7 %all-to-all-start = ((f32[32,4,128]{2,1,0:T(4,128)}), f32[32,4,128]{2,1,0:T(4,128)S(1)}, u32[]{:S(2)}, u32[]{:S(2)}) async-start(f32[32,4,128]{2,1,0:T(4,128)} %synthesis.1), calls=%async_computation | async-start | bytes 131072 | tf_op jit(solution)/shard_map/all_to_all | solution.py:674
  24.8 0.0 collective-permute-done.7.even_rows
  24.8 1.6 %collective-permute-done.8.odd_rows = f32[4,8,1152]{2,1,0:T(8,128)S(1)} collective-permute-done((f32[4,8,1152]{2,1,0:T(8,128)S(1)}, f32[4,8,1152]{2,1,0:T(8,128)S(1)}, u32[]{:S(2)}, u32[]{:S(2)}) %collective-permute-start.8) | collective-permute-done | bytes 147488 | tf_op jit(solution)/shard_map/ppermute | solution.py:634
  26.5 1.9 %windows.1 = (f32[80,1152]{1,0:T(8,128)S(1)}, f32[80,1152]{1,0:T(8,128)S(1)}, f32[80,1152]{1,0:T(8,128)S(1)}, f32[80,1152]{1,0:T(8,128)S(1)}, f32[80,1152]{1,0:T(8,128)S(1)}, /*index=5*/bf16[128,1152]{1,0:T(8,128)(2,1)S(1)}) custom-call(s32[32]{0:T(128)} %waves_hbm.3, f32[64,1080]{1,0:T(8,128)} %height_hbm.5, f32[64,1080]{1,0:T(8,128)} %east_hbm.5, ...), custom_call_target="tpu_custom_call" | custom-call | flops 99999997952 | bytes 400000000 | tf_op jit(solution)/shard_map/windows/pallas_call | solution.py:676
  28.4 3.8 %all-to-all-done.synth_ref = f32[32,4,128]{2,1,0:T(4,128)S(1)} async-done(((f32[32,4,128]{2,1,0:T(4,128)}), f32[32,4,128]{2,1,0:T(4,128)S(1)}, u32[]{:S(2)}, u32[]{:S(2)}) %all-to-all-start) | async-done | bytes 65568 | tf_op jit(solution)/shard_map/all_to_all | solution.py:674
  32.2 2.6 %substeps.1 = (f32[64,1080]{1,0:T(8,128)}, f32[64,1080]{1,0:T(8,128)}, f32[64,1080]{1,0:T(8,128)}, f32[64,1080]{1,0:T(8,128)}) custom-call(f32[32,4,128]{2,1,0:T(4,128)S(1)} %all-to-all-done.synth_ref, bf16[128,1152]{1,0:T(8,128)(2,1)S(1)} %get-tuple-element.36.harm_ref, f32[80,1152]{1,0:T(8,128)S(1)} %get-tuple-element.37.surface_win, ...), custom_call_target="tpu_custom_call" | custom-call | tf_op jit(solution)/shard_map/substeps/pallas_call | solution.py:693
  (5 shorter events, 0.0 us)
Async XLA Ops:
  2.4 1.4 %collective-permute-start = (f32[64,128]{1,0:T(8,128)S(1)}, f32[64,128]{1,0:T(8,128)S(1)}, u32[]{:S(2)}, u32[]{:S(2)}) collective-permute-start(f32[64,128]{1,0:T(8,128)S(1)} %get-tuple-element.25), channel_id=1, source_target_pairs={{0,1},{1,0},{2,3},{3,2},{4,5},{5,4},{6,7},{7,6},{8,9},{9,8},{10,11... | collective-permute-start | bytes 98312 | tf_op jit(solution)/shard_map/ppermute | solution.py:597
  3.8 9.0 %collective-permute-start.1 = (f32[40,128]{1,0:T(8,128)S(1)}, f32[40,128]{1,0:T(8,128)S(1)}, u32[]{:S(2)}, u32[]{:S(2)}) collective-permute-start(f32[40,128]{1,0:T(8,128)S(1)} %get-tuple-element.27), channel_id=1, source_target_pairs={{0,3},{1,2},{2,1},{3,0},{4,7},{5,6},{6,5},{7,4},{8,11},{9,10},{10,... | collective-permute-start | bytes 61448 | tf_op jit(solution)/shard_map/ppermute | solution.py:616
  6.4 6.4 %collective-permute-start.3 = (f32[40,128]{1,0:T(8,128)S(1)}, f32[40,128]{1,0:T(8,128)S(1)}, u32[]{:S(2)}, u32[]{:S(2)}) collective-permute-start(f32[40,128]{1,0:T(8,128)S(1)} %get-tuple-element.29), channel_id=1, source_target_pairs={{0,7},{1,6},{2,5},{3,4},{4,3},{5,2},{6,1},{7,0},{8,15},{9,14},{10,... | collective-permute-start | bytes 61448 | tf_op jit(solution)/shard_map/ppermute | solution.py:616
  8.9 3.9 %collective-permute-start.2 = (f32[8,128]{1,0:T(8,128)S(1)}, f32[8,128]{1,0:T(8,128)S(1)}, u32[]{:S(2)}, u32[]{:S(2)}) collective-permute-start(f32[8,128]{1,0:T(8,128)S(1)} %get-tuple-element.28), channel_id=1, source_target_pairs={{0,5},{1,4},{2,7},{3,6},{4,1},{5,0},{6,3},{7,2},{8,13},{9,12},{10,... | collective-permute-start | bytes 12296 | tf_op jit(solution)/shard_map/ppermute | solution.py:616
  9.0 12.0 %copy-start = (f32[2048]{0:T(1024)S(1)}, f32[2048]{0:T(1024)}, u32[]{:S(2)}) copy-start(f32[2048]{0:T(1024)} %param.11) | copy-start | bytes 24580
  13.4 7.3 %collective-permute-start.4 = (f32[8,2176]{1,0:T(8,128)S(1)}, f32[8,2176]{1,0:T(8,128)S(1)}, u32[]{:S(2)}, u32[]{:S(2)}) collective-permute-start(f32[8,2176]{1,0:T(8,128)S(1)} %get-tuple-element.32), channel_id=1, source_target_pairs={{0,24},{8,16},{16,8},{24,0},{1,25},{9,17},{17,9},{25,1},{2,26},{10... | collective-permute-start | bytes 208904 | tf_op jit(solution)/shard_map/ppermute | solution.py:651
  15.9 5.1 %collective-permute-start.5 = (f32[8,2176]{1,0:T(8,128)S(1)}, f32[8,2176]{1,0:T(8,128)S(1)}, u32[]{:S(2)}, u32[]{:S(2)}) collective-permute-start(f32[8,2176]{1,0:T(8,128)S(1)} %get-tuple-element.33), channel_id=1, source_target_pairs={{0,8},{8,0},{16,24},{24,16},{1,9},{9,1},{17,25},{25,17},{2,10},{10... | collective-permute-start | bytes 208904 | tf_op jit(solution)/shard_map/ppermute | solution.py:651
  16.4 4.3 %collective-permute-start.6 = (f32[8,2048]{1,0:T(8,128)S(1)}, f32[8,2048]{1,0:T(8,128)S(1)}, u32[]{:S(2)}, u32[]{:S(2)}) collective-permute-start(f32[8,2048]{1,0:T(8,128)S(1)} %get-tuple-element.31.refs_0_), channel_id=1, source_target_pairs={{0,16},{8,24},{16,0},{24,8},{1,17},{9,25},{17,1},{25,9},{2,18},{10... | collective-permute-start | bytes 196616 | tf_op jit(solution)/shard_map/ppermute | solution.py:651
  16.9 7.9 %collective-permute-start.7 = (f32[4,8,1152]{2,1,0:T(8,128)S(1)}, f32[4,8,1152]{2,1,0:T(8,128)S(1)}, u32[]{:S(2)}, u32[]{:S(2)}) collective-permute-start(f32[4,8,1152]{2,1,0:T(8,128)S(1)} %get-tuple-element.34), channel_id=1, source_target_pairs={{0,8},{16,24},{8,0},{24,16},{1,9},{17,25},{9,1},{25,17},{2,10},{18... | collective-permute-start | bytes 442376 | tf_op jit(solution)/shard_map/ppermute | solution.py:634
  18.4 8.0 %collective-permute-start.8 = (f32[4,8,1152]{2,1,0:T(8,128)S(1)}, f32[4,8,1152]{2,1,0:T(8,128)S(1)}, u32[]{:S(2)}, u32[]{:S(2)}) collective-permute-start(f32[4,8,1152]{2,1,0:T(8,128)S(1)} %get-tuple-element.35), channel_id=1, source_target_pairs={{8,16},{24,0},{16,8},{0,24},{9,17},{25,1},{17,9},{1,25},{10,18},{2... | collective-permute-start | bytes 442376 | tf_op jit(solution)/shard_map/ppermute | solution.py:634
  22.1 10.1 %all-to-all-start = ((f32[32,4,128]{2,1,0:T(4,128)}), f32[32,4,128]{2,1,0:T(4,128)S(1)}, u32[]{:S(2)}, u32[]{:S(2)}) async-start(f32[32,4,128]{2,1,0:T(4,128)} %synthesis.1), calls=%async_computation | async-start | bytes 131072 | tf_op jit(solution)/shard_map/all_to_all | solution.py:674

commit v9 on v8

--- a/solution.py
+++ b/solution.py
@@ -145,7 +145,8 @@
         copy.start()
     copies[0].wait()
     harmonic_rows(period, cols, slots, lax.axis_index("lon"), True, waves_ref, harm_ref)
-    copies[1].wait()
+    for copy in copies[1:]:
+        copy.wait()
     for tile in range(0, width, 128):
         stop = min(cols, tile + 128)
         if stop <= tile:
@@ -170,8 +171,6 @@
     total = jnp.concatenate([total, jnp.zeros((waves, 128 - rows), f32)], axis=1)
     keep_ref[...] = total[: waves // 2].reshape(keep_ref.shape)
     send_ref[: waves // 2] = total[waves // 2 :]
-    for copy in copies[2:]:
-        copy.wait()
     pieces = []
     for front, end in (
         (height_ref[:, :MARGIN], height_ref[:, cols - MARGIN :]),

time: 35 us -> 34.9 us (level)
  no operation moved by 1% of the time
where the time goes in v9:
time: 34.9 us; the launch traced here: 34.6 us
  starting transfers between devices  15 us (43%)
  Pallas kernels  9.65 us (28%)
  waiting for transfers between devices  9.35 us (27%)
  between operations  0.68 us (2%)
    ppermute x3, starting transfers between devices, shards(): arrived.append(lax.ppermute(block, 'lon', across))  5.22 us
    all_to_all x1, waiting for transfers between devices, shards(): everyone = lax.all_to_all(synth, ('lat', 'lon'), 0, 0, tiled=True)  3.85 us
    ppermute x3, starting transfers between devices, shards(): lax.ppermute(block, 'lat', [(i, i ^ step) for i in range(bands)])  3.55 us
    ppermute x2, starting transfers between devices, shards(): lax.ppermute(block, 'lat', pairs)  2.98 us
    all_to_all x1, starting transfers between devices, shards(): everyone = lax.all_to_all(synth, ('lat', 'lon'), 0, 0, tiled=True)  2.68 us
    pallas_call x1, Pallas kernels, shards(): pl.pallas_call(functools.partial(substep_kernel, sectors, bands), out_sha...  2.56 us
    ppermute x3, waiting for transfers between devices, shards(): arrived.append(lax.ppermute(block, 'lon', across))  1.96 us
    pallas_call x1, Pallas kernels, shards(): pl.pallas_call(functools.partial(windows_kernel, period, slots, chips, ba...  1.89 us
  transfers between devices with their start and end apart: 10, of which 6 were waited for; matrix products, arithmetic and copies ran while one was open for 0% of the time, Pallas kernels for 14%

profile of v9, /device:TPU:0, one launch (start us, length us, event | category | flops | bytes accessed | tf_op | source)
XLA Modules:
  0.0 34.6 jit_solution(212755047026394337)
XLA Ops:
  0.6 1.6 %transform.1 = (f32[4,8,128]{2,1,0:T(8,128)S(1)}, f32[64,128]{1,0:T(8,128)S(1)}, f32[32,128]{1,0:T(8,128)S(1)}) custom-call(s32[32]{0:T(128)} %waves_hbm.3, f32[64,1080]{1,0:T(8,128)} %height_hbm.5, f32[64,1080]{1,0:T(8,128)} %east_hbm.5, f32[64,1080]{1,0:T(8,128)} %north_hbm.5, s32[64,1080]{1,0:T(8,128)} %land_hbm.5), custom_call_target="tpu_custom_call" | custom-call | tf_op jit(solution)/shard_map/transform/pallas_call | solution.py:573
  2.2 0.5 %collective-permute-start = (f32[64,128]{1,0:T(8,128)S(1)}, f32[64,128]{1,0:T(8,128)S(1)}, u32[]{:S(2)}, u32[]{:S(2)}) collective-permute-start(f32[64,128]{1,0:T(8,128)S(1)} %get-tuple-element.25), channel_id=1, source_target_pairs={{0,1},{1,0},{2,3},{3,2},{4,5},{5,4},{6,7},{7,6},{8,9},{9,8},{10,11... | collective-permute-start | bytes 98312 | tf_op jit(solution)/shard_map/ppermute | solution.py:596
  2.8 0.9 %collective-permute-done.recv_ref.refs_4_.core_ref = f32[64,128]{1,0:T(8,128)S(1)} collective-permute-done((f32[64,128]{1,0:T(8,128)S(1)}, f32[64,128]{1,0:T(8,128)S(1)}, u32[]{:S(2)}, u32[]{:S(2)}) %collective-permute-start) | collective-permute-done | bytes 32800 | tf_op jit(solution)/shard_map/ppermute | solution.py:596
  3.6 2.7 %collective-permute-start.1 = (f32[40,128]{1,0:T(8,128)S(1)}, f32[40,128]{1,0:T(8,128)S(1)}, u32[]{:S(2)}, u32[]{:S(2)}) collective-permute-start(f32[40,128]{1,0:T(8,128)S(1)} %get-tuple-element.27), channel_id=1, source_target_pairs={{0,3},{1,2},{2,1},{3,0},{4,7},{5,6},{6,5},{7,4},{8,11},{9,10},{10,... | collective-permute-start | bytes 61448 | tf_op jit(solution)/shard_map/ppermute | solution.py:615
  6.3 2.4 %collective-permute-start.3 = (f32[40,128]{1,0:T(8,128)S(1)}, f32[40,128]{1,0:T(8,128)S(1)}, u32[]{:S(2)}, u32[]{:S(2)}) collective-permute-start(f32[40,128]{1,0:T(8,128)S(1)} %get-tuple-element.29), channel_id=1, source_target_pairs={{0,7},{1,6},{2,5},{3,4},{4,3},{5,2},{6,1},{7,0},{8,15},{9,14},{10,... | collective-permute-start | bytes 61448 | tf_op jit(solution)/shard_map/ppermute | solution.py:615
  8.7 0.1 collective-permute-start.2
  8.8 1.9 %stage.1 = (f32[4,8,1152]{2,1,0:T(8,128)S(1)}, f32[4,8,1152]{2,1,0:T(8,128)S(1)}, f32[4,64,2048]{2,1,0:T(8,128)S(1)}) custom-call(f32[8,128]{1,0:T(8,128)S(1)} %get-tuple-element.26.after_ref.refs_0_, f32[64,1080]{1,0:T(8,128)} %height_hbm.5, f32[64,1080]{1,0:T(8,128)} %east_hbm.5, f32[64,1080]{1,0:T(8,128)} %north_hbm.5, s32[64,1080]{1,0:T(8,128)} %land_hbm.5, ...), custom_call_target="tpu_custom_call" | custom-call | tf_op jit(solution)/shard_map/stage/pallas_call | solution.py:618
  10.7 2.0 %collective-permute-done.2.refs_2_ = f32[8,128]{1,0:T(8,128)S(1)} collective-permute-done((f32[8,128]{1,0:T(8,128)S(1)}, f32[8,128]{1,0:T(8,128)S(1)}, u32[]{:S(2)}, u32[]{:S(2)}) %collective-permute-start.2) | collective-permute-done | bytes 4128 | tf_op jit(solution)/shard_map/ppermute | solution.py:615
  12.7 0.0 collective-permute-done.1.refs_1_.west_ref
  12.7 0.0 collective-permute-done.3.refs_3_.east_ref
  12.7 0.6 %analysis.1 = (f32[8,2048]{1,0:T(8,128)S(1)}, f32[8,2176]{1,0:T(8,128)S(1)}, f32[8,2176]{1,0:T(8,128)S(1)}) custom-call(f32[8,128]{1,0:T(8,128)S(1)} %get-tuple-element.26.after_ref.refs_0_, f32[40,128]{1,0:T(8,128)S(1)} %collective-permute-done.1.refs_1_.west_ref, f32[8,128]{1,0:T(8,128)S(1)} %collective-permute-done.2.refs_2_, ...), custom_call_target="tpu_custom_call" | custom-call | tf_op jit(solution)/shard_map/analysis/pallas_call | solution.py:640
  13.2 2.5 %collective-permute-start.4 = (f32[8,2176]{1,0:T(8,128)S(1)}, f32[8,2176]{1,0:T(8,128)S(1)}, u32[]{:S(2)}, u32[]{:S(2)}) collective-permute-start(f32[8,2176]{1,0:T(8,128)S(1)} %get-tuple-element.32), channel_id=1, source_target_pairs={{0,24},{8,16},{16,8},{24,0},{1,25},{9,17},{17,9},{25,1},{2,26},{10... | collective-permute-start | bytes 208904 | tf_op jit(solution)/shard_map/ppermute | solution.py:650
  15.8 0.5 %collective-permute-start.5 = (f32[8,2176]{1,0:T(8,128)S(1)}, f32[8,2176]{1,0:T(8,128)S(1)}, u32[]{:S(2)}, u32[]{:S(2)}) collective-permute-start(f32[8,2176]{1,0:T(8,128)S(1)} %get-tuple-element.33), channel_id=1, source_target_pairs={{0,8},{8,0},{16,24},{24,16},{1,9},{9,1},{17,25},{25,17},{2,10},{10... | collective-permute-start | bytes 208904 | tf_op jit(solution)/shard_map/ppermute | solution.py:650
  16.3 0.5 %collective-permute-start.6 = (f32[8,2048]{1,0:T(8,128)S(1)}, f32[8,2048]{1,0:T(8,128)S(1)}, u32[]{:S(2)}, u32[]{:S(2)}) collective-permute-start(f32[8,2048]{1,0:T(8,128)S(1)} %get-tuple-element.31.refs_0_), channel_id=1, source_target_pairs={{0,16},{8,24},{16,0},{24,8},{1,17},{9,25},{17,1},{25,9},{2,18},{10... | collective-permute-start | bytes 196616 | tf_op jit(solution)/shard_map/ppermute | solution.py:650
  16.8 1.5 %collective-permute-start.7 = (f32[4,8,1152]{2,1,0:T(8,128)S(1)}, f32[4,8,1152]{2,1,0:T(8,128)S(1)}, u32[]{:S(2)}, u32[]{:S(2)}) collective-permute-start(f32[4,8,1152]{2,1,0:T(8,128)S(1)} %get-tuple-element.34), channel_id=1, source_target_pairs={{0,8},{16,24},{8,0},{24,16},{1,9},{17,25},{9,1},{25,17},{2,10},{18... | collective-permute-start | bytes 442376 | tf_op jit(solution)/shard_map/ppermute | solution.py:633
  18.3 1.5 %collective-permute-start.8 = (f32[4,8,1152]{2,1,0:T(8,128)S(1)}, f32[4,8,1152]{2,1,0:T(8,128)S(1)}, u32[]{:S(2)}, u32[]{:S(2)}) collective-permute-start(f32[4,8,1152]{2,1,0:T(8,128)S(1)} %get-tuple-element.35), channel_id=1, source_target_pairs={{8,16},{24,0},{16,8},{0,24},{9,17},{25,1},{17,9},{1,25},{10,18},{2... | collective-permute-start | bytes 442376 | tf_op jit(solution)/shard_map/ppermute | solution.py:633
  19.8 0.8 %collective-permute-done.6.refs_3_ = f32[8,2048]{1,0:T(8,128)S(1)} collective-permute-done((f32[8,2048]{1,0:T(8,128)S(1)}, f32[8,2048]{1,0:T(8,128)S(1)}, u32[]{:S(2)}, u32[]{:S(2)}) %collective-permute-start.6) | collective-permute-done | bytes 65568 | tf_op jit(solution)/shard_map/ppermute | solution.py:650
  20.6 0.3 collective-permute-done.5.refs_2_.even_ref
  20.8 1.2 %synthesis.1 = f32[32,4,128]{2,1,0:T(4,128)} custom-call(f32[8,2048]{1,0:T(8,128)S(1)} %get-tuple-element.31.refs_0_, f32[8,2176]{1,0:T(8,128)S(1)} %collective-permute-done.4.refs_1_.odd_ref, f32[8,2176]{1,0:T(8,128)S(1)} %collective-permute-done.5.refs_2_.even_ref, f32[8,2048]{1,0:T(8,128)S(1)} %collective-permute-done.6.refs_3_, f32[1,2048]{1,0:T(1,128)S(1)} %bitcast.1, ...), custom_call_target="tpu_custom_call" | custom-call | flops 99999997952 | bytes 400000000 | tf_op jit(solution)/shard_map/synthesis/pallas_call | solution.py:663
  22.0 2.7 %all-to-all-start = ((f32[32,4,128]{2,1,0:T(4,128)}), f32[32,4,128]{2,1,0:T(4,128)S(1)}, u32[]{:S(2)}, u32[]{:S(2)}) async-start(f32[32,4,128]{2,1,0:T(4,128)} %synthesis.1), calls=%async_computation | async-start | bytes 131072 | tf_op jit(solution)/shard_map/all_to_all | solution.py:673
  24.7 1.6 %collective-permute-done.8.odd_rows = f32[4,8,1152]{2,1,0:T(8,128)S(1)} collective-permute-done((f32[4,8,1152]{2,1,0:T(8,128)S(1)}, f32[4,8,1152]{2,1,0:T(8,128)S(1)}, u32[]{:S(2)}, u32[]{:S(2)}) %collective-permute-start.8) | collective-permute-done | bytes 147488 | tf_op jit(solution)/shard_map/ppermute | solution.py:633
  26.3 1.9 %windows.1 = (f32[80,1152]{1,0:T(8,128)S(1)}, f32[80,1152]{1,0:T(8,128)S(1)}, f32[80,1152]{1,0:T(8,128)S(1)}, f32[80,1152]{1,0:T(8,128)S(1)}, f32[80,1152]{1,0:T(8,128)S(1)}, /*index=5*/bf16[128,1152]{1,0:T(8,128)(2,1)S(1)}) custom-call(s32[32]{0:T(128)} %waves_hbm.3, f32[64,1080]{1,0:T(8,128)} %height_hbm.5, f32[64,1080]{1,0:T(8,128)} %east_hbm.5, ...), custom_call_target="tpu_custom_call" | custom-call | flops 99999997952 | bytes 400000000 | tf_op jit(solution)/shard_map/windows/pallas_call | solution.py:675
  28.2 3.8 %all-to-all-done.synth_ref = f32[32,4,128]{2,1,0:T(4,128)S(1)} async-done(((f32[32,4,128]{2,1,0:T(4,128)}), f32[32,4,128]{2,1,0:T(4,128)S(1)}, u32[]{:S(2)}, u32[]{:S(2)}) %all-to-all-start) | async-done | bytes 65568 | tf_op jit(solution)/shard_map/all_to_all | solution.py:673
  32.1 2.6 %substeps.1 = (f32[64,1080]{1,0:T(8,128)}, f32[64,1080]{1,0:T(8,128)}, f32[64,1080]{1,0:T(8,128)}, f32[64,1080]{1,0:T(8,128)}) custom-call(f32[32,4,128]{2,1,0:T(4,128)S(1)} %all-to-all-done.synth_ref, bf16[128,1152]{1,0:T(8,128)(2,1)S(1)} %get-tuple-element.36.harm_ref, f32[80,1152]{1,0:T(8,128)S(1)} %get-tuple-element.37.surface_win, ...), custom_call_target="tpu_custom_call" | custom-call | tf_op jit(solution)/shard_map/substeps/pallas_call | solution.py:692
  (5 shorter events, 0.0 us)
Async XLA Ops:
  2.2 1.4 %collective-permute-start = (f32[64,128]{1,0:T(8,128)S(1)}, f32[64,128]{1,0:T(8,128)S(1)}, u32[]{:S(2)}, u32[]{:S(2)}) collective-permute-start(f32[64,128]{1,0:T(8,128)S(1)} %get-tuple-element.25), channel_id=1, source_target_pairs={{0,1},{1,0},{2,3},{3,2},{4,5},{5,4},{6,7},{7,6},{8,9},{9,8},{10,11... | collective-permute-start | bytes 98312 | tf_op jit(solution)/shard_map/ppermute | solution.py:596
  3.6 9.0 %collective-permute-start.1 = (f32[40,128]{1,0:T(8,128)S(1)}, f32[40,128]{1,0:T(8,128)S(1)}, u32[]{:S(2)}, u32[]{:S(2)}) collective-permute-start(f32[40,128]{1,0:T(8,128)S(1)} %get-tuple-element.27), channel_id=1, source_target_pairs={{0,3},{1,2},{2,1},{3,0},{4,7},{5,6},{6,5},{7,4},{8,11},{9,10},{10,... | collective-permute-start | bytes 61448 | tf_op jit(solution)/shard_map/ppermute | solution.py:615
  6.3 6.4 %collective-permute-start.3 = (f32[40,128]{1,0:T(8,128)S(1)}, f32[40,128]{1,0:T(8,128)S(1)}, u32[]{:S(2)}, u32[]{:S(2)}) collective-permute-start(f32[40,128]{1,0:T(8,128)S(1)} %get-tuple-element.29), channel_id=1, source_target_pairs={{0,7},{1,6},{2,5},{3,4},{4,3},{5,2},{6,1},{7,0},{8,15},{9,14},{10,... | collective-permute-start | bytes 61448 | tf_op jit(solution)/shard_map/ppermute | solution.py:615
  8.7 3.9 %collective-permute-start.2 = (f32[8,128]{1,0:T(8,128)S(1)}, f32[8,128]{1,0:T(8,128)S(1)}, u32[]{:S(2)}, u32[]{:S(2)}) collective-permute-start(f32[8,128]{1,0:T(8,128)S(1)} %get-tuple-element.28), channel_id=1, source_target_pairs={{0,5},{1,4},{2,7},{3,6},{4,1},{5,0},{6,3},{7,2},{8,13},{9,12},{10,... | collective-permute-start | bytes 12296 | tf_op jit(solution)/shard_map/ppermute | solution.py:615
  8.8 12.0 %copy-start = (f32[2048]{0:T(1024)S(1)}, f32[2048]{0:T(1024)}, u32[]{:S(2)}) copy-start(f32[2048]{0:T(1024)} %param.11) | copy-start | bytes 24580
  13.2 7.3 %collective-permute-start.4 = (f32[8,2176]{1,0:T(8,128)S(1)}, f32[8,2176]{1,0:T(8,128)S(1)}, u32[]{:S(2)}, u32[]{:S(2)}) collective-permute-start(f32[8,2176]{1,0:T(8,128)S(1)} %get-tuple-element.32), channel_id=1, source_target_pairs={{0,24},{8,16},{16,8},{24,0},{1,25},{9,17},{17,9},{25,1},{2,26},{10... | collective-permute-start | bytes 208904 | tf_op jit(solution)/shard_map/ppermute | solution.py:650
  15.8 5.1 %collective-permute-start.5 = (f32[8,2176]{1,0:T(8,128)S(1)}, f32[8,2176]{1,0:T(8,128)S(1)}, u32[]{:S(2)}, u32[]{:S(2)}) collective-permute-start(f32[8,2176]{1,0:T(8,128)S(1)} %get-tuple-element.33), channel_id=1, source_target_pairs={{0,8},{8,0},{16,24},{24,16},{1,9},{9,1},{17,25},{25,17},{2,10},{10... | collective-permute-start | bytes 208904 | tf_op jit(solution)/shard_map/ppermute | solution.py:650
  16.3 4.3 %collective-permute-start.6 = (f32[8,2048]{1,0:T(8,128)S(1)}, f32[8,2048]{1,0:T(8,128)S(1)}, u32[]{:S(2)}, u32[]{:S(2)}) collective-permute-start(f32[8,2048]{1,0:T(8,128)S(1)} %get-tuple-element.31.refs_0_), channel_id=1, source_target_pairs={{0,16},{8,24},{16,0},{24,8},{1,17},{9,25},{17,1},{25,9},{2,18},{10... | collective-permute-start | bytes 196616 | tf_op jit(solution)/shard_map/ppermute | solution.py:650
  16.8 7.9 %collective-permute-start.7 = (f32[4,8,1152]{2,1,0:T(8,128)S(1)}, f32[4,8,1152]{2,1,0:T(8,128)S(1)}, u32[]{:S(2)}, u32[]{:S(2)}) collective-permute-start(f32[4,8,1152]{2,1,0:T(8,128)S(1)} %get-tuple-element.34), channel_id=1, source_target_pairs={{0,8},{16,24},{8,0},{24,16},{1,9},{17,25},{9,1},{25,17},{2,10},{18... | collective-permute-start | bytes 442376 | tf_op jit(solution)/shard_map/ppermute | solution.py:633
  18.3 8.0 %collective-permute-start.8 = (f32[4,8,1152]{2,1,0:T(8,128)S(1)}, f32[4,8,1152]{2,1,0:T(8,128)S(1)}, u32[]{:S(2)}, u32[]{:S(2)}) collective-permute-start(f32[4,8,1152]{2,1,0:T(8,128)S(1)} %get-tuple-element.35), channel_id=1, source_target_pairs={{8,16},{24,0},{16,8},{0,24},{9,17},{25,1},{17,9},{1,25},{10,18},{2... | collective-permute-start | bytes 442376 | tf_op jit(solution)/shard_map/ppermute | solution.py:633
  22.0 10.1 %all-to-all-start = ((f32[32,4,128]{2,1,0:T(4,128)}), f32[32,4,128]{2,1,0:T(4,128)S(1)}, u32[]{:S(2)}, u32[]{:S(2)}) async-start(f32[32,4,128]{2,1,0:T(4,128)} %synthesis.1), calls=%async_computation | async-start | bytes 131072 | tf_op jit(solution)/shard_map/all_to_all | solution.py:673

commit v10 on v9

--- a/solution.py
+++ b/solution.py
@@ -55,12 +55,10 @@
     for core, shift in row_groups(sectors):
         first = owner(me, sectors, core, shift) * slots
         group = [waves_ref[first + slot] for slot in range(slots)]
-        order += group + group if paired else group
-    if not paired:
-        order = order + order
+        order += group
     row = lax.broadcasted_iota(jnp.int32, (8, 1), 0)
     blocks = []
-    for first in range(0, waves, 8):
+    for first in range(0, waves // 2, 8):
         block = jnp.zeros((8, 1), jnp.int32)
         for at, value in enumerate(order[first : first + 8]):
             block = jnp.where(row == at, value, block)
@@ -70,17 +68,12 @@
     turns = jnp.floor(start.astype(f32) * (1.0 / period)).astype(jnp.int32)
     start = (start - turns * period).astype(f32)
     wave = wave.astype(f32)
-    row = lax.broadcasted_iota(jnp.int32, (waves, 1), 0)
-    if paired:
-        row = lax.rem(row, 2 * slots)
-    sine = (row >= (slots if paired else waves // 2)).astype(f32)
-    offset = 4.0 * start - period * sine
     for tile in range(0, width, 128):
         lane = lax.broadcasted_iota(jnp.int32, (1, 128), 1) + tile
         lane = jnp.where(lane < cols + MARGIN, lane, lane - width).astype(f32)
         product = wave * lane
         product = product - period * jnp.floor(product * (1.0 / period))
-        quarter = 4.0 * product + offset
+        quarter = 4.0 * (product + start)
         turn = jnp.floor(quarter * (1.0 / period) + 0.5)
         angle = (quarter - period * turn) * (0.5 * math.pi / period)
         square = angle * angle
@@ -94,8 +87,17 @@
         )
         phase = turn - 4.0 * jnp.floor(turn * 0.25)
         odd = (phase == 1.0) | (phase == 3.0)
-        value = jnp.where(odd, sine_of, cosine)
-        value = jnp.where((phase == 1.0) | (phase == 2.0), -value, value)
+        cosines = jnp.where(odd, sine_of, cosine)
+        cosines = jnp.where((phase == 1.0) | (phase == 2.0), -cosines, cosines)
+        sines = jnp.where(odd, cosine, sine_of)
+        sines = jnp.where(phase >= 2.0, -sines, sines)
+        if paired:
+            parts = []
+            for first in range(0, waves // 2, slots):
+                parts += [cosines[first : first + slots], sines[first : first + slots]]
+        else:
+            parts = [cosines, sines]
+        value = jnp.concatenate(parts, axis=0)
         hi, lo = split2(value)
         harm_ref[:waves, tile : tile + 128] = hi
         harm_ref[waves:, tile : tile + 128] = lo

time: 34.9 us -> 34.7 us (level)
  no operation moved by 1% of the time
where the time goes in v10:
time: 34.7 us; the launch traced here: 34.5 us
  starting transfers between devices  15 us (43%)
  waiting for transfers between devices  9.46 us (27%)
  Pallas kernels  9.36 us (27%)
  between operations  0.68 us (2%)
    ppermute x3, starting transfers between devices, shards(): arrived.append(lax.ppermute(block, 'lon', across))  5.23 us
    all_to_all x1, waiting for transfers between devices, shards(): everyone = lax.all_to_all(synth, ('lat', 'lon'), 0, 0, tiled=True)  3.96 us
    ppermute x3, starting transfers between devices, shards(): lax.ppermute(block, 'lat', [(i, i ^ step) for i in range(bands)])  3.55 us
    ppermute x2, starting transfers between devices, shards(): lax.ppermute(block, 'lat', pairs)  2.98 us
    all_to_all x1, starting transfers between devices, shards(): everyone = lax.all_to_all(synth, ('lat', 'lon'), 0, 0, tiled=True)  2.68 us
    pallas_call x1, Pallas kernels, shards(): pl.pallas_call(functools.partial(substep_kernel, sectors, bands), out_sha...  2.56 us
    ppermute x3, waiting for transfers between devices, shards(): arrived.append(lax.ppermute(block, 'lon', across))  1.95 us
    pallas_call x1, Pallas kernels, shards(): pl.pallas_call(stage_kernel, out_shape=[struct((4, MARGIN, width))] * 2 +...  1.86 us
  transfers between devices with their start and end apart: 10, of which 6 were waited for; matrix products, arithmetic and copies ran while one was open for 0% of the time, Pallas kernels for 14%

profile of v10, /device:TPU:0, one launch (start us, length us, event | category | flops | bytes accessed | tf_op | source)
XLA Modules:
  0.0 34.5 jit_solution(15432261015281636244)
XLA Ops:
  0.6 1.4 %transform.1 = (f32[4,8,128]{2,1,0:T(8,128)S(1)}, f32[64,128]{1,0:T(8,128)S(1)}, f32[32,128]{1,0:T(8,128)S(1)}) custom-call(s32[32]{0:T(128)} %waves_hbm.3, f32[64,1080]{1,0:T(8,128)} %height_hbm.5, f32[64,1080]{1,0:T(8,128)} %east_hbm.5, f32[64,1080]{1,0:T(8,128)} %north_hbm.5, s32[64,1080]{1,0:T(8,128)} %land_hbm.5), custom_call_target="tpu_custom_call" | custom-call | tf_op jit(solution)/shard_map/transform/pallas_call | solution.py:575
  2.1 0.5 %collective-permute-start = (f32[64,128]{1,0:T(8,128)S(1)}, f32[64,128]{1,0:T(8,128)S(1)}, u32[]{:S(2)}, u32[]{:S(2)}) collective-permute-start(f32[64,128]{1,0:T(8,128)S(1)} %get-tuple-element.25), channel_id=1, source_target_pairs={{0,1},{1,0},{2,3},{3,2},{4,5},{5,4},{6,7},{7,6},{8,9},{9,8},{10,11... | collective-permute-start | bytes 98312 | tf_op jit(solution)/shard_map/ppermute | solution.py:598
  2.6 0.9 %collective-permute-done.recv_ref.refs_4_.core_ref = f32[64,128]{1,0:T(8,128)S(1)} collective-permute-done((f32[64,128]{1,0:T(8,128)S(1)}, f32[64,128]{1,0:T(8,128)S(1)}, u32[]{:S(2)}, u32[]{:S(2)}) %collective-permute-start) | collective-permute-done | bytes 32800 | tf_op jit(solution)/shard_map/ppermute | solution.py:598
  3.5 2.7 %collective-permute-start.1 = (f32[40,128]{1,0:T(8,128)S(1)}, f32[40,128]{1,0:T(8,128)S(1)}, u32[]{:S(2)}, u32[]{:S(2)}) collective-permute-start(f32[40,128]{1,0:T(8,128)S(1)} %get-tuple-element.27), channel_id=1, source_target_pairs={{0,3},{1,2},{2,1},{3,0},{4,7},{5,6},{6,5},{7,4},{8,11},{9,10},{10,... | collective-permute-start | bytes 61448 | tf_op jit(solution)/shard_map/ppermute | solution.py:617
  6.1 2.4 %collective-permute-start.3 = (f32[40,128]{1,0:T(8,128)S(1)}, f32[40,128]{1,0:T(8,128)S(1)}, u32[]{:S(2)}, u32[]{:S(2)}) collective-permute-start(f32[40,128]{1,0:T(8,128)S(1)} %get-tuple-element.29), channel_id=1, source_target_pairs={{0,7},{1,6},{2,5},{3,4},{4,3},{5,2},{6,1},{7,0},{8,15},{9,14},{10,... | collective-permute-start | bytes 61448 | tf_op jit(solution)/shard_map/ppermute | solution.py:617
  8.6 0.1 collective-permute-start.2
  8.7 1.9 %stage.1 = (f32[4,8,1152]{2,1,0:T(8,128)S(1)}, f32[4,8,1152]{2,1,0:T(8,128)S(1)}, f32[4,64,2048]{2,1,0:T(8,128)S(1)}) custom-call(f32[8,128]{1,0:T(8,128)S(1)} %get-tuple-element.26.after_ref.refs_0_, f32[64,1080]{1,0:T(8,128)} %height_hbm.5, f32[64,1080]{1,0:T(8,128)} %east_hbm.5, f32[64,1080]{1,0:T(8,128)} %north_hbm.5, s32[64,1080]{1,0:T(8,128)} %land_hbm.5, ...), custom_call_target="tpu_custom_call" | custom-call | tf_op jit(solution)/shard_map/stage/pallas_call | solution.py:620
  10.6 1.9 %collective-permute-done.2.refs_2_ = f32[8,128]{1,0:T(8,128)S(1)} collective-permute-done((f32[8,128]{1,0:T(8,128)S(1)}, f32[8,128]{1,0:T(8,128)S(1)}, u32[]{:S(2)}, u32[]{:S(2)}) %collective-permute-start.2) | collective-permute-done | bytes 4128 | tf_op jit(solution)/shard_map/ppermute | solution.py:617
  12.5 0.6 %analysis.1 = (f32[8,2048]{1,0:T(8,128)S(1)}, f32[8,2176]{1,0:T(8,128)S(1)}, f32[8,2176]{1,0:T(8,128)S(1)}) custom-call(f32[8,128]{1,0:T(8,128)S(1)} %get-tuple-element.26.after_ref.refs_0_, f32[40,128]{1,0:T(8,128)S(1)} %collective-permute-done.1.refs_1_.west_ref, f32[8,128]{1,0:T(8,128)S(1)} %collective-permute-done.2.refs_2_, ...), custom_call_target="tpu_custom_call" | custom-call | tf_op jit(solution)/shard_map/analysis/pallas_call | solution.py:642
  13.1 2.5 %collective-permute-start.4 = (f32[8,2176]{1,0:T(8,128)S(1)}, f32[8,2176]{1,0:T(8,128)S(1)}, u32[]{:S(2)}, u32[]{:S(2)}) collective-permute-start(f32[8,2176]{1,0:T(8,128)S(1)} %get-tuple-element.32), channel_id=1, source_target_pairs={{0,24},{8,16},{16,8},{24,0},{1,25},{9,17},{17,9},{25,1},{2,26},{10... | collective-permute-start | bytes 208904 | tf_op jit(solution)/shard_map/ppermute | solution.py:652
  15.6 0.5 %collective-permute-start.5 = (f32[8,2176]{1,0:T(8,128)S(1)}, f32[8,2176]{1,0:T(8,128)S(1)}, u32[]{:S(2)}, u32[]{:S(2)}) collective-permute-start(f32[8,2176]{1,0:T(8,128)S(1)} %get-tuple-element.33), channel_id=1, source_target_pairs={{0,8},{8,0},{16,24},{24,16},{1,9},{9,1},{17,25},{25,17},{2,10},{10... | collective-permute-start | bytes 208904 | tf_op jit(solution)/shard_map/ppermute | solution.py:652
  16.1 0.5 %collective-permute-start.6 = (f32[8,2048]{1,0:T(8,128)S(1)}, f32[8,2048]{1,0:T(8,128)S(1)}, u32[]{:S(2)}, u32[]{:S(2)}) collective-permute-start(f32[8,2048]{1,0:T(8,128)S(1)} %get-tuple-element.31.refs_0_), channel_id=1, source_target_pairs={{0,16},{8,24},{16,0},{24,8},{1,17},{9,25},{17,1},{25,9},{2,18},{10... | collective-permute-start | bytes 196616 | tf_op jit(solution)/shard_map/ppermute | solution.py:652
  16.6 1.5 %collective-permute-start.7 = (f32[4,8,1152]{2,1,0:T(8,128)S(1)}, f32[4,8,1152]{2,1,0:T(8,128)S(1)}, u32[]{:S(2)}, u32[]{:S(2)}) collective-permute-start(f32[4,8,1152]{2,1,0:T(8,128)S(1)} %get-tuple-element.34), channel_id=1, source_target_pairs={{0,8},{16,24},{8,0},{24,16},{1,9},{17,25},{9,1},{25,17},{2,10},{18... | collective-permute-start | bytes 442376 | tf_op jit(solution)/shard_map/ppermute | solution.py:635
  18.1 1.5 %collective-permute-start.8 = (f32[4,8,1152]{2,1,0:T(8,128)S(1)}, f32[4,8,1152]{2,1,0:T(8,128)S(1)}, u32[]{:S(2)}, u32[]{:S(2)}) collective-permute-start(f32[4,8,1152]{2,1,0:T(8,128)S(1)} %get-tuple-element.35), channel_id=1, source_target_pairs={{8,16},{24,0},{16,8},{0,24},{9,17},{25,1},{17,9},{1,25},{10,18},{2... | collective-permute-start | bytes 442376 | tf_op jit(solution)/shard_map/ppermute | solution.py:635
  19.6 0.8 %collective-permute-done.6.refs_3_ = f32[8,2048]{1,0:T(8,128)S(1)} collective-permute-done((f32[8,2048]{1,0:T(8,128)S(1)}, f32[8,2048]{1,0:T(8,128)S(1)}, u32[]{:S(2)}, u32[]{:S(2)}) %collective-permute-start.6) | collective-permute-done | bytes 65568 | tf_op jit(solution)/shard_map/ppermute | solution.py:652
  20.4 0.0 collective-permute-done.4.refs_1_.odd_ref
  20.4 0.3 collective-permute-done.5.refs_2_.even_ref
  20.7 1.2 %synthesis.1 = f32[32,4,128]{2,1,0:T(4,128)} custom-call(f32[8,2048]{1,0:T(8,128)S(1)} %get-tuple-element.31.refs_0_, f32[8,2176]{1,0:T(8,128)S(1)} %collective-permute-done.4.refs_1_.odd_ref, f32[8,2176]{1,0:T(8,128)S(1)} %collective-permute-done.5.refs_2_.even_ref, f32[8,2048]{1,0:T(8,128)S(1)} %collective-permute-done.6.refs_3_, f32[1,2048]{1,0:T(1,128)S(1)} %bitcast.1, ...), custom_call_target="tpu_custom_call" | custom-call | flops 99999997952 | bytes 400000000 | tf_op jit(solution)/shard_map/synthesis/pallas_call | solution.py:665
  21.8 2.7 %all-to-all-start = ((f32[32,4,128]{2,1,0:T(4,128)}), f32[32,4,128]{2,1,0:T(4,128)S(1)}, u32[]{:S(2)}, u32[]{:S(2)}) async-start(f32[32,4,128]{2,1,0:T(4,128)} %synthesis.1), calls=%async_computation | async-start | bytes 131072 | tf_op jit(solution)/shard_map/all_to_all | solution.py:675
  24.5 0.0 collective-permute-done.7.even_rows
  24.5 1.6 %collective-permute-done.8.odd_rows = f32[4,8,1152]{2,1,0:T(8,128)S(1)} collective-permute-done((f32[4,8,1152]{2,1,0:T(8,128)S(1)}, f32[4,8,1152]{2,1,0:T(8,128)S(1)}, u32[]{:S(2)}, u32[]{:S(2)}) %collective-permute-start.8) | collective-permute-done | bytes 147488 | tf_op jit(solution)/shard_map/ppermute | solution.py:635
  26.2 1.8 %windows.1 = (f32[80,1152]{1,0:T(8,128)S(1)}, f32[80,1152]{1,0:T(8,128)S(1)}, f32[80,1152]{1,0:T(8,128)S(1)}, f32[80,1152]{1,0:T(8,128)S(1)}, f32[80,1152]{1,0:T(8,128)S(1)}, /*index=5*/bf16[128,1152]{1,0:T(8,128)(2,1)S(1)}) custom-call(s32[32]{0:T(128)} %waves_hbm.3, f32[64,1080]{1,0:T(8,128)} %height_hbm.5, f32[64,1080]{1,0:T(8,128)} %east_hbm.5, ...), custom_call_target="tpu_custom_call" | custom-call | flops 99999997952 | bytes 400000000 | tf_op jit(solution)/shard_map/windows/pallas_call | solution.py:677
  28.0 4.0 %all-to-all-done.synth_ref = f32[32,4,128]{2,1,0:T(4,128)S(1)} async-done(((f32[32,4,128]{2,1,0:T(4,128)}), f32[32,4,128]{2,1,0:T(4,128)S(1)}, u32[]{:S(2)}, u32[]{:S(2)}) %all-to-all-start) | async-done | bytes 65568 | tf_op jit(solution)/shard_map/all_to_all | solution.py:675
  31.9 2.6 %substeps.1 = (f32[64,1080]{1,0:T(8,128)}, f32[64,1080]{1,0:T(8,128)}, f32[64,1080]{1,0:T(8,128)}, f32[64,1080]{1,0:T(8,128)}) custom-call(f32[32,4,128]{2,1,0:T(4,128)S(1)} %all-to-all-done.synth_ref, bf16[128,1152]{1,0:T(8,128)(2,1)S(1)} %get-tuple-element.36.harm_ref, f32[80,1152]{1,0:T(8,128)S(1)} %get-tuple-element.37.surface_win, ...), custom_call_target="tpu_custom_call" | custom-call | tf_op jit(solution)/shard_map/substeps/pallas_call | solution.py:694
  (5 shorter events, 0.0 us)
Async XLA Ops:
  2.1 1.4 %collective-permute-start = (f32[64,128]{1,0:T(8,128)S(1)}, f32[64,128]{1,0:T(8,128)S(1)}, u32[]{:S(2)}, u32[]{:S(2)}) collective-permute-start(f32[64,128]{1,0:T(8,128)S(1)} %get-tuple-element.25), channel_id=1, source_target_pairs={{0,1},{1,0},{2,3},{3,2},{4,5},{5,4},{6,7},{7,6},{8,9},{9,8},{10,11... | collective-permute-start | bytes 98312 | tf_op jit(solution)/shard_map/ppermute | solution.py:598
  3.5 9.0 %collective-permute-start.1 = (f32[40,128]{1,0:T(8,128)S(1)}, f32[40,128]{1,0:T(8,128)S(1)}, u32[]{:S(2)}, u32[]{:S(2)}) collective-permute-start(f32[40,128]{1,0:T(8,128)S(1)} %get-tuple-element.27), channel_id=1, source_target_pairs={{0,3},{1,2},{2,1},{3,0},{4,7},{5,6},{6,5},{7,4},{8,11},{9,10},{10,... | collective-permute-start | bytes 61448 | tf_op jit(solution)/shard_map/ppermute | solution.py:617
  6.1 6.4 %collective-permute-start.3 = (f32[40,128]{1,0:T(8,128)S(1)}, f32[40,128]{1,0:T(8,128)S(1)}, u32[]{:S(2)}, u32[]{:S(2)}) collective-permute-start(f32[40,128]{1,0:T(8,128)S(1)} %get-tuple-element.29), channel_id=1, source_target_pairs={{0,7},{1,6},{2,5},{3,4},{4,3},{5,2},{6,1},{7,0},{8,15},{9,14},{10,... | collective-permute-start | bytes 61448 | tf_op jit(solution)/shard_map/ppermute | solution.py:617
  8.6 3.9 %collective-permute-start.2 = (f32[8,128]{1,0:T(8,128)S(1)}, f32[8,128]{1,0:T(8,128)S(1)}, u32[]{:S(2)}, u32[]{:S(2)}) collective-permute-start(f32[8,128]{1,0:T(8,128)S(1)} %get-tuple-element.28), channel_id=1, source_target_pairs={{0,5},{1,4},{2,7},{3,6},{4,1},{5,0},{6,3},{7,2},{8,13},{9,12},{10,... | collective-permute-start | bytes 12296 | tf_op jit(solution)/shard_map/ppermute | solution.py:617
  8.7 12.0 %copy-start = (f32[2048]{0:T(1024)S(1)}, f32[2048]{0:T(1024)}, u32[]{:S(2)}) copy-start(f32[2048]{0:T(1024)} %param.11) | copy-start | bytes 24580
  13.1 7.3 %collective-permute-start.4 = (f32[8,2176]{1,0:T(8,128)S(1)}, f32[8,2176]{1,0:T(8,128)S(1)}, u32[]{:S(2)}, u32[]{:S(2)}) collective-permute-start(f32[8,2176]{1,0:T(8,128)S(1)} %get-tuple-element.32), channel_id=1, source_target_pairs={{0,24},{8,16},{16,8},{24,0},{1,25},{9,17},{17,9},{25,1},{2,26},{10... | collective-permute-start | bytes 208904 | tf_op jit(solution)/shard_map/ppermute | solution.py:652
  15.6 5.1 %collective-permute-start.5 = (f32[8,2176]{1,0:T(8,128)S(1)}, f32[8,2176]{1,0:T(8,128)S(1)}, u32[]{:S(2)}, u32[]{:S(2)}) collective-permute-start(f32[8,2176]{1,0:T(8,128)S(1)} %get-tuple-element.33), channel_id=1, source_target_pairs={{0,8},{8,0},{16,24},{24,16},{1,9},{9,1},{17,25},{25,17},{2,10},{10... | collective-permute-start | bytes 208904 | tf_op jit(solution)/shard_map/ppermute | solution.py:652
  16.1 4.3 %collective-permute-start.6 = (f32[8,2048]{1,0:T(8,128)S(1)}, f32[8,2048]{1,0:T(8,128)S(1)}, u32[]{:S(2)}, u32[]{:S(2)}) collective-permute-start(f32[8,2048]{1,0:T(8,128)S(1)} %get-tuple-element.31.refs_0_), channel_id=1, source_target_pairs={{0,16},{8,24},{16,0},{24,8},{1,17},{9,25},{17,1},{25,9},{2,18},{10... | collective-permute-start | bytes 196616 | tf_op jit(solution)/shard_map/ppermute | solution.py:652
  16.6 7.9 %collective-permute-start.7 = (f32[4,8,1152]{2,1,0:T(8,128)S(1)}, f32[4,8,1152]{2,1,0:T(8,128)S(1)}, u32[]{:S(2)}, u32[]{:S(2)}) collective-permute-start(f32[4,8,1152]{2,1,0:T(8,128)S(1)} %get-tuple-element.34), channel_id=1, source_target_pairs={{0,8},{16,24},{8,0},{24,16},{1,9},{17,25},{9,1},{25,17},{2,10},{18... | collective-permute-start | bytes 442376 | tf_op jit(solution)/shard_map/ppermute | solution.py:635
  18.1 8.0 %collective-permute-start.8 = (f32[4,8,1152]{2,1,0:T(8,128)S(1)}, f32[4,8,1152]{2,1,0:T(8,128)S(1)}, u32[]{:S(2)}, u32[]{:S(2)}) collective-permute-start(f32[4,8,1152]{2,1,0:T(8,128)S(1)} %get-tuple-element.35), channel_id=1, source_target_pairs={{8,16},{24,0},{16,8},{0,24},{9,17},{25,1},{17,9},{1,25},{10,18},{2... | collective-permute-start | bytes 442376 | tf_op jit(solution)/shard_map/ppermute | solution.py:635
  21.8 10.1 %all-to-all-start = ((f32[32,4,128]{2,1,0:T(4,128)}), f32[32,4,128]{2,1,0:T(4,128)S(1)}, u32[]{:S(2)}, u32[]{:S(2)}) async-start(f32[32,4,128]{2,1,0:T(4,128)} %synthesis.1), calls=%async_computation | async-start | bytes 131072 | tf_op jit(solution)/shard_map/all_to_all | solution.py:675
